TPU v7x, 32 devices: a whole 2x2x4 slice. The times are simulated.
32 devices in a mesh: dp: 4 (over y, x), ctx: 4 (over z), tensor: 2 (over core).
Axes of the slice: x: 2, y: 2, z: 4, core: 2. Of those that a mesh axis runs over, the one named last changes fastest.
Arguments:
- activations: bfloat16 [2, 8, 1024, 896], P(None, 'dp', 'ctx'), may hold values from -6 to 6
- segments: int32 [2, 8, 1024], P(None, 'dp', 'ctx'), may hold values from 0 to 20, as said below
- cotangent: bfloat16 [2, 8, 1024, 896], P(None, 'dp', 'ctx'), may hold values from -6 to 6
- query_weight: bfloat16 [896, 896], P(('dp', 'ctx'), 'tensor'), may hold values from -0.1875 to 0.1875
- key_weight: bfloat16 [896, 128], P(('dp', 'ctx'), 'tensor'), may hold values from -0.1875 to 0.1875
- value_weight: bfloat16 [896, 128], P(('dp', 'ctx'), 'tensor'), may hold values from -0.1875 to 0.1875
- out_weight: bfloat16 [896, 896], P('tensor', ('dp', 'ctx')), may hold values from -0.75 to 0.75
- query_bias: float32 [896], P('tensor'), may hold values from -3 to 3
- key_bias_vector: float32 [128], P('tensor'), may hold values from -3 to 3
- value_bias: float32 [128], P('tensor'), may hold values from -3 to 3
- attention_gain: float32 [896], replicated, may hold values from 0.1 to 1.9
- gate_weight: bfloat16 [896, 4864], P(('dp', 'ctx'), 'tensor'), may hold values from -0.1875 to 0.1875
- up_weight: bfloat16 [896, 4864], P(('dp', 'ctx'), 'tensor'), may hold values from -0.1875 to 0.1875
- down_weight: bfloat16 [4864, 896], P('tensor', ('dp', 'ctx')), may hold values from -0.078125 to 0.078125
- mlp_gain: float32 [896], replicated, may hold values from 0.1 to 1.9
Outputs:
- output: bfloat16 [2, 8, 1024, 896], P(None, 'dp', 'ctx')
- input_grad: float32 [2, 8, 1024, 896], P(None, 'dp', 'ctx')
- grad_query_weight: float32 [896, 896], P(('dp', 'ctx'), 'tensor')
- grad_key_weight: float32 [896, 128], P(('dp', 'ctx'), 'tensor')
- grad_value_weight: float32 [896, 128], P(('dp', 'ctx'), 'tensor')
- grad_out_weight: float32 [896, 896], P('tensor', ('dp', 'ctx'))
- grad_query_bias: float32 [896], P('tensor')
- grad_key_bias: float32 [128], P('tensor')
- grad_value_bias: float32 [128], P('tensor')
- grad_attention_gain: float32 [896], replicated
- grad_gate_weight: float32 [896, 4864], P(('dp', 'ctx'), 'tensor')
- grad_up_weight: float32 [896, 4864], P(('dp', 'ctx'), 'tensor')
- grad_down_weight: float32 [4864, 896], P('tensor', ('dp', 'ctx'))
- grad_mlp_gain: float32 [896], replicated
Inputs may be any that keep to these rules, and one draw needn't show every extreme that they name: `segments`: within each sequence the numbers start at 0 and never fall. Every document except a sequence's last has 51 to 512 tokens. In each micro-batch, among the sequences of each index of dp, one holds a single document.
All inputs are finite; a program needn't handle non-finite values.
Results may differ from a plain program's by a relative error of at most 0.038.
Values may be sent and summed in bfloat16 or wider, within the bound.
No kernel may reach another device: no remote copies, remote signals or barrier semaphores. Data moves between devices by JAX's collectives and lax.ppermute only.
A program may use at most 192 MiB of HBM per device.

v0:
```python
import jax
import jax.numpy as jnp
from jax import lax
from jax.sharding import PartitionSpec as P

HEAD = 64


eps = 1e-06
theta = 1000000.0
masked = -1e30


def positions_of(segment):
    index = jnp.arange(segment.shape[-1], dtype=jnp.int32)
    change = jnp.concatenate(
        [jnp.ones(segment.shape[:-1] + (1,), jnp.bool_), segment[..., 1:] != segment[..., :-1]],
        axis=-1,
    )
    starts = lax.cummax(jnp.where(change, index, 0), axis=segment.ndim - 1)
    return index - starts


def rotary_tables(position, head_slot):
    half = head_slot // 2
    freq = theta ** (-(2.0 / head_slot) * jnp.arange(half, dtype=jnp.float32))
    angle = position.astype(jnp.float32)[..., None] * freq
    return (jnp.cos(angle), jnp.sin(angle))


def rotate(values, cosine, sine):
    half = values.shape[-1] // 2
    lower_half = values[..., :half]
    upper_half = values[..., half:]
    return jnp.concatenate(
        [lower_half * cosine - upper_half * sine, upper_half * cosine + lower_half * sine], axis=-1
    )


def unrotate(values, cosine, sine):
    half = values.shape[-1] // 2
    lower_half = values[..., :half]
    upper_half = values[..., half:]
    return jnp.concatenate(
        [lower_half * cosine + upper_half * sine, upper_half * cosine - lower_half * sine], axis=-1
    )


def product(left, right):
    return jnp.dot(left, right, preferred_element_type=jnp.float32)


def branch_total(partial_out):
    return lax.psum(partial_out.astype(jnp.bfloat16), "tensor").astype(jnp.float32)


def input_total(partial_grad):
    return lax.psum(partial_grad.astype(jnp.bfloat16), "tensor").astype(jnp.float32)


def fetch_forward(
    query_weight, key_weight, value_weight, out_weight, gate_weight, up_weight, down_weight
):
    attn_parts = (
        lax.all_gather(query_weight, ("dp", "ctx"), axis=0, tiled=True),
        lax.all_gather(key_weight, ("dp", "ctx"), axis=0, tiled=True),
        lax.all_gather(value_weight, ("dp", "ctx"), axis=0, tiled=True),
        lax.all_gather(out_weight, ("dp", "ctx"), axis=1, tiled=True),
    )
    mlp_parts = (
        lax.all_gather(gate_weight, ("dp", "ctx"), axis=0, tiled=True),
        lax.all_gather(up_weight, ("dp", "ctx"), axis=0, tiled=True),
        lax.all_gather(down_weight, ("dp", "ctx"), axis=1, tiled=True),
    )
    return tuple(attn_parts) + tuple(mlp_parts)


def fetch_backward(
    query_weight, key_weight, value_weight, out_weight, gate_weight, up_weight, down_weight
):
    attn_parts = (
        lax.all_gather(query_weight, ("dp", "ctx"), axis=0, tiled=True),
        lax.all_gather(key_weight, ("dp", "ctx"), axis=0, tiled=True),
        lax.all_gather(value_weight, ("dp", "ctx"), axis=0, tiled=True),
        lax.all_gather(out_weight, ("dp", "ctx"), axis=1, tiled=True),
    )
    mlp_parts = (
        lax.all_gather(gate_weight, ("dp", "ctx"), axis=0, tiled=True),
        lax.all_gather(up_weight, ("dp", "ctx"), axis=0, tiled=True),
        lax.all_gather(down_weight, ("dp", "ctx"), axis=1, tiled=True),
    )
    return tuple(attn_parts) + tuple(mlp_parts)


def local(
    activations,
    segments,
    cotangent,
    query_weight,
    key_weight,
    value_weight,
    out_weight,
    query_bias,
    key_bias_vector,
    value_bias,
    attention_gain,
    gate_weight,
    up_weight,
    down_weight,
    mlp_gain,
):
    micro_count, seq_count, stretch, width = activations.shape
    head_slot = HEAD
    group = query_weight.shape[1] // head_slot
    rows = group * stretch
    tokens_now = seq_count * stretch
    scale = head_slot ** (-0.5)
    offset = lax.axis_index("ctx") * stretch
    whole_ids = lax.all_gather(segments, "ctx", axis=2, tiled=True)
    whole_pos = positions_of(whole_ids)
    local_pos = lax.dynamic_slice_in_dim(whole_pos, offset, stretch, 2)
    cosine_all, sine_all = rotary_tables(local_pos, head_slot)
    query_rows = jnp.tile(offset + jnp.arange(stretch, dtype=jnp.int32), group)
    shards = (
        query_weight,
        key_weight,
        value_weight,
        out_weight,
        gate_weight,
        up_weight,
        down_weight,
    )
    totals = (
        jnp.zeros((width, group * head_slot), jnp.float32),
        jnp.zeros((width, head_slot), jnp.float32),
        jnp.zeros((width, head_slot), jnp.float32),
        jnp.zeros((group * head_slot, width), jnp.float32),
        jnp.zeros((width, gate_weight.shape[1]), jnp.float32),
        jnp.zeros((width, up_weight.shape[1]), jnp.float32),
        jnp.zeros((down_weight.shape[0], width), jnp.float32),
        jnp.zeros((group * head_slot,), jnp.float32),
        jnp.zeros((head_slot,), jnp.float32),
        jnp.zeros((head_slot,), jnp.float32),
        jnp.zeros((width,), jnp.float32),
        jnp.zeros((width,), jnp.float32),
    )
    outputs = []
    grad_inputs = []
    for micro in range(micro_count):
        current = fetch_forward(*shards)
        run_totals = totals
        wq_full, wk_full, wv_full, wo_full, wg_full, wu_full, wd_full = current
        cosine = cosine_all[micro][:, :, None, :]
        sine = sine_all[micro][:, :, None, :]
        ids_now = whole_ids[micro]
        query_ids = jnp.tile(segments[micro], (1, group))
        source = activations[micro].reshape(tokens_now, width).astype(jnp.float32)
        inverse1 = lax.rsqrt(jnp.mean(source * source, axis=-1, keepdims=True) + eps)
        unit1 = source * inverse1
        normed1 = (unit1 * attention_gain).astype(jnp.bfloat16)
        query = product(normed1, wq_full) + query_bias
        key = product(normed1, wk_full) + key_bias_vector
        value = (product(normed1, wv_full) + value_bias).astype(jnp.bfloat16)
        query_rot = rotate(
            query.reshape(seq_count, stretch, group, head_slot), cosine, sine
        ).astype(jnp.bfloat16)
        key_rot = rotate(key.reshape(seq_count, stretch, 1, head_slot), cosine, sine).astype(
            jnp.bfloat16
        )
        pair = jnp.concatenate(
            [
                key_rot.reshape(seq_count, stretch, head_slot),
                value.reshape(seq_count, stretch, head_slot),
            ],
            axis=-1,
        )
        query_tensor = query_rot.transpose(0, 2, 1, 3).reshape(seq_count, rows, head_slot)

        def scores_of(segment_piece):
            count = segment_piece.shape[1]
            scores = (
                jnp.einsum(
                    "hlf,htf->hlt",
                    query_tensor,
                    segment_piece[..., :head_slot],
                    preferred_element_type=jnp.float32,
                )
                * scale
            )
            key_rows = jnp.arange(count, dtype=jnp.int32)
            allowed = (query_ids[:, :, None] == ids_now[:, None, :]) & (
                key_rows[None, None, :] <= query_rows[None, :, None]
            )
            return (scores, allowed)

        forward_segment_piece = lax.all_gather(pair, "ctx", axis=1, tiled=True)
        best = jnp.full((seq_count, rows), masked, jnp.float32)
        forward_scores, forward_allowed = scores_of(forward_segment_piece)
        forward_scores = jnp.where(forward_allowed, forward_scores, masked)
        top = jnp.maximum(best, jnp.max(forward_scores, axis=2))
        weights = jnp.where(forward_allowed, jnp.exp(forward_scores - top[..., None]), 0.0)
        running = jnp.sum(weights, axis=2)
        summed = jnp.einsum(
            "tgu,tuz->tgz",
            weights.astype(jnp.bfloat16),
            forward_segment_piece[..., head_slot:],
            preferred_element_type=jnp.float32,
        )
        best, running, summed = (top, running, summed)
        attention = summed / running[..., None]
        logsum = best + jnp.log(running)
        attended = (
            attention.astype(jnp.bfloat16)
            .reshape(seq_count, group, stretch, head_slot)
            .transpose(0, 2, 1, 3)
            .reshape(tokens_now, group * head_slot)
        )
        mixed = source + branch_total(product(attended, wo_full))
        inverse2 = lax.rsqrt(jnp.mean(mixed * mixed, axis=-1, keepdims=True) + eps)
        unit2 = mixed * inverse2
        normed2 = (unit2 * mlp_gain).astype(jnp.bfloat16)
        gate = product(normed2, wg_full)
        up_proj = product(normed2, wu_full)
        sigma = jax.nn.sigmoid(gate)
        silu = gate * sigma
        hidden = (silu * up_proj).astype(jnp.bfloat16)
        result = mixed + branch_total(product(hidden, wd_full))
        output_now = result.astype(jnp.bfloat16).reshape(seq_count, stretch, width)
        wq_back, wk_back, wv_back, wo_back, wg_back, wu_back, wd_back = fetch_backward(*shards)
        grad_result = cotangent[micro].reshape(tokens_now, width).astype(jnp.float32)
        grad_branch = grad_result.astype(jnp.bfloat16)
        grad_down = product(hidden.T, grad_branch)
        grad_hidden = product(grad_branch, wd_back.T)
        grad_gate = (grad_hidden * up_proj * sigma * (1.0 + gate * (1.0 - sigma))).astype(
            jnp.bfloat16
        )
        up_gradient = (grad_hidden * silu).astype(jnp.bfloat16)
        grad_gate_w = product(normed2.T, grad_gate)
        grad_up_w = product(normed2.T, up_gradient)
        grad_normed2 = input_total(product(grad_gate, wg_back.T) + product(up_gradient, wu_back.T))
        grad_gain2 = jnp.sum(grad_normed2 * unit2, axis=0)
        scaled2 = grad_normed2 * mlp_gain
        grad_mixed = grad_result + inverse2 * (
            scaled2 - unit2 * jnp.mean(scaled2 * unit2, axis=-1, keepdims=True)
        )
        grad_attn = grad_mixed.astype(jnp.bfloat16)
        grad_out_w = product(attended.T, grad_attn)
        grad_attended = product(grad_attn, wo_back.T).astype(jnp.bfloat16)
        grad_heads = (
            grad_attended.reshape(seq_count, stretch, group, head_slot)
            .transpose(0, 2, 1, 3)
            .reshape(seq_count, rows, head_slot)
        )
        delta = jnp.sum(grad_heads.astype(jnp.float32) * attention, axis=-1)
        backward_segment_piece = lax.all_gather(pair, "ctx", axis=1, tiled=True)
        backward_scores, backward_allowed = scores_of(backward_segment_piece)
        prob = jnp.where(backward_allowed, jnp.exp(backward_scores - logsum[..., None]), 0.0)
        grad_prob = jnp.einsum(
            "hlf,htf->hlt",
            grad_heads,
            backward_segment_piece[..., head_slot:],
            preferred_element_type=jnp.float32,
        )
        score_gradient = (prob * (grad_prob - delta[..., None])).astype(jnp.bfloat16)
        grad_query_acc = (
            jnp.einsum(
                "tgu,tuz->tgz",
                score_gradient,
                backward_segment_piece[..., :head_slot],
                preferred_element_type=jnp.float32,
            )
            * scale
        )
        grad_key_block = (
            jnp.einsum(
                "tnp,tnr->tpr", score_gradient, query_tensor, preferred_element_type=jnp.float32
            )
            * scale
        )
        grad_value_block = jnp.einsum(
            "tnp,tnr->tpr",
            prob.astype(jnp.bfloat16),
            grad_heads,
            preferred_element_type=jnp.float32,
        )
        block = jnp.concatenate([grad_key_block, grad_value_block], axis=-1)
        grad_pair = block
        grad_query_heads, grad_pair = (grad_query_acc, grad_pair)
        own_pair = lax.psum_scatter(
            grad_pair.astype(jnp.bfloat16), "ctx", scatter_dimension=1, tiled=True
        ).astype(jnp.float32)
        key_gradient = (
            unrotate(own_pair[..., :head_slot][:, :, None, :], cosine, sine)
            .reshape(tokens_now, head_slot)
            .astype(jnp.bfloat16)
        )
        grad_value = own_pair[..., head_slot:].reshape(tokens_now, head_slot).astype(jnp.bfloat16)
        grad_query_tok = grad_query_heads.reshape(seq_count, group, stretch, head_slot).transpose(
            0, 2, 1, 3
        )
        grad_query = (
            unrotate(grad_query_tok, cosine, sine)
            .reshape(tokens_now, group * head_slot)
            .astype(jnp.bfloat16)
        )
        grad_query_w = product(normed1.T, grad_query)
        grad_key_w = product(normed1.T, key_gradient)
        grad_value_w = product(normed1.T, grad_value)
        grad_query_b = jnp.sum(grad_query.astype(jnp.float32), axis=0)
        grad_key_b = jnp.sum(key_gradient.astype(jnp.float32), axis=0)
        grad_value_b = jnp.sum(grad_value.astype(jnp.float32), axis=0)
        grad_normed1 = input_total(
            product(grad_query, wq_back.T)
            + product(key_gradient, wk_back.T)
            + product(grad_value, wv_back.T)
        )
        grad_gain1 = jnp.sum(grad_normed1 * unit1, axis=0)
        scaled1 = grad_normed1 * attention_gain
        grad_source = grad_mixed + inverse1 * (
            scaled1 - unit1 * jnp.mean(scaled1 * unit1, axis=-1, keepdims=True)
        )
        terms = (
            grad_query_w,
            grad_key_w,
            grad_value_w,
            grad_out_w,
            grad_gate_w,
            grad_up_w,
            grad_down,
            grad_query_b,
            grad_key_b,
            grad_value_b,
            grad_gain1,
            grad_gain2,
        )
        run_totals = tuple((left + right for left, right in zip(run_totals, terms)))
        totals, output_now, grad_now = (
            run_totals,
            output_now,
            grad_source.reshape(seq_count, stretch, width),
        )
        outputs.append(output_now)
        grad_inputs.append(grad_now)
    owned = (
        lax.psum_scatter(totals[0], ("dp", "ctx"), scatter_dimension=0, tiled=True),
        lax.psum_scatter(totals[1], ("dp", "ctx"), scatter_dimension=0, tiled=True),
        lax.psum_scatter(totals[2], ("dp", "ctx"), scatter_dimension=0, tiled=True),
        lax.psum_scatter(totals[3], ("dp", "ctx"), scatter_dimension=1, tiled=True),
        lax.psum_scatter(totals[4], ("dp", "ctx"), scatter_dimension=0, tiled=True),
        lax.psum_scatter(totals[5], ("dp", "ctx"), scatter_dimension=0, tiled=True),
        lax.psum_scatter(totals[6], ("dp", "ctx"), scatter_dimension=1, tiled=True),
    )
    smalls = lax.psum((totals[7], totals[8], totals[9], totals[10], totals[11]), ("dp", "ctx"))
    return (
        jnp.stack(outputs, axis=0),
        jnp.stack(grad_inputs, axis=0),
        owned[0],
        owned[1],
        owned[2],
        owned[3],
        smalls[0],
        smalls[1],
        smalls[2],
        smalls[3],
        owned[4],
        owned[5],
        owned[6],
        smalls[4],
    )


def solution(mesh):
    return jax.shard_map(
        local,
        mesh=mesh,
        in_specs=(
            P(None, "dp", "ctx", None),
            P(None, "dp", "ctx"),
            P(None, "dp", "ctx", None),
            P(("dp", "ctx"), "tensor"),
            P(("dp", "ctx"), "tensor"),
            P(("dp", "ctx"), "tensor"),
            P("tensor", ("dp", "ctx")),
            P("tensor"),
            P("tensor"),
            P("tensor"),
            P(),
            P(("dp", "ctx"), "tensor"),
            P(("dp", "ctx"), "tensor"),
            P("tensor", ("dp", "ctx")),
            P(),
        ),
        out_specs=(
            P(None, "dp", "ctx", None),
            P(None, "dp", "ctx", None),
            P(("dp", "ctx"), "tensor"),
            P(("dp", "ctx"), "tensor"),
            P(("dp", "ctx"), "tensor"),
            P("tensor", ("dp", "ctx")),
            P("tensor"),
            P("tensor"),
            P("tensor"),
            P(),
            P(("dp", "ctx"), "tensor"),
            P(("dp", "ctx"), "tensor"),
            P("tensor", ("dp", "ctx")),
            P(),
        ),
        check_vma=False,
    )
```

profile of v0, /device:TPU:0, one launch (start us, length us, event | category | flops | bytes accessed | tf_op | source)
XLA Modules:
  0.0 1613.3 jit_solution(11315929968140908975)
XLA Ops:
  8.1 13.9 all_gather.20
  25.9 48.0 %all_gather.21 = bf16[896,448]{1,0:T(8,128)(2,1)S(1)} all-gather(bf16[56,448]{1,0:T(8,128)(2,1)} %param.18), channel_id=1, replica_groups=mesh['dp'=4,'ctx'=4,'tensor'=2] {'dp','ctx'}, dimensions={0}, use_global_device_ids=true | all-gather | bytes 852992 | tf_op jit(solution)/shard_map/all_gather | solution.py:65
  73.9 37.3 %all_gather.22 = bf16[896,64]{1,0:T(8,128)(2,1)S(1)} all-gather(bf16[56,64]{1,0:T(8,128)(2,1)S(1)} %copy-done.87), channel_id=1, replica_groups=mesh['dp'=4,'ctx'=4,'tensor'=2] {'dp','ctx'}, dimensions={0}, use_global_device_ids=true | all-gather | bytes 121856 | tf_op jit(solution)/shard_map/all_gather | solution.py:66
  116.5 39.4 %all_gather.23 = bf16[896,64]{1,0:T(8,128)(2,1)S(1)} all-gather(bf16[56,64]{1,0:T(8,128)(2,1)S(1)} %copy-done.88), channel_id=1, replica_groups=mesh['dp'=4,'ctx'=4,'tensor'=2] {'dp','ctx'}, dimensions={0}, use_global_device_ids=true | all-gather | bytes 121856 | tf_op jit(solution)/shard_map/all_gather | solution.py:67
  158.6 2.7 iota_compare_fusion
  171.2 14.7 all_gather.29
  185.9 2.7 reshape.443
  194.0 15.6 all_gather.24
  211.7 12.7 fusion.2
  224.4 14.9 fusion.16
  239.4 6.6 fusion.142
  249.0 43.9 %all_gather.25 = bf16[448,896]{0,1:T(8,128)(2,1)S(1)} all-gather(bf16[448,56]{0,1:T(8,128)(2,1)S(1)} %copy-done.74), channel_id=1, replica_groups=mesh['dp'=4,'ctx'=4,'tensor'=2] {'dp','ctx'}, dimensions={1}, use_global_device_ids=true | all-gather | bytes 852992 | tf_op jit(solution)/shard_map/all_gather | solution.py:68
  292.8 10.4 fusion.143
  307.2 2.9 convolution_convert_fusion.2
  313.6 2.8 fusion.137
  316.5 15.0 all-reduce.18.cloned.1.call-done
  335.8 55.4 %all-gather.4.cloned.1.call-done = bf16[896,2432]{1,0:T(8,128)(2,1)} async-done(((bf16[56,2432]{1,0:T(8,128)(2,1)}), bf16[896,2432]{1,0:T(8,128)(2,1)}) %all-gather.4.cloned.1.call-update) | async-done | bytes 4358160 | tf_op jit(solution)/shard_map/all_gather | solution.py:71
  391.1 7.5 fusion.146
  398.7 71.1 %all-gather.6.cloned.1.call-done = bf16[896,2432]{1,0:T(8,128)(2,1)} async-done(((bf16[56,2432]{1,0:T(8,128)(2,1)}), bf16[896,2432]{1,0:T(8,128)(2,1)}) %all-gather.6.cloned.1.call-update) | async-done | bytes 4358160 | tf_op jit(solution)/shard_map/all_gather | solution.py:72
  469.8 7.7 fusion.147
  477.5 4.9 fusion.144
  482.4 4.5 fusion.145
  486.9 61.7 %all-gather.8.cloned.1.call-done = bf16[2432,896]{0,1:T(8,128)(2,1)} async-done(((bf16[2432,56]{0,1:T(8,128)(2,1)}), bf16[2432,896]{0,1:T(8,128)(2,1)}) %all-gather.8.cloned.1.call-update) | async-done | bytes 4358160 | tf_op jit(solution)/shard_map/all_gather | solution.py:73
  548.5 10.8 multiply_convert_fusion.2
  559.4 6.9 fusion.151
  566.3 7.2 multiply_convert_fusion.4
  573.6 2.8 fusion.148
  576.5 3.8 add_convert_fusion.1
  580.3 3.7 add_convert_fusion.3
  584.2 6.9 convolution_convert_fusion
  591.1 6.1 convolution_convert_fusion.1
  597.3 6.5 all-reduce.16.cloned.1.call-done
  603.8 4.1 fusion.46
  607.9 2.8 fusion.45
  619.7 8.6 fusion.69
  628.4 9.8 multiply_convert_fusion
  638.3 2.3 fusion.65
  640.6 2.3 convolution_multiply_fusion
  643.8 3.2 convolution_convert_fusion.5
  651.0 2.3 reshape.458
  654.8 10.5 multiply_convert_fusion.1
  665.4 3.0 copy-done.2
  670.6 2.5 reshape.462
  676.8 8.1 fusion.66
  686.1 5.4 convolution_multiply_fusion.1
  691.5 2.4 reshape.459
  699.9 8.9 reduce-scatter.25.cloned.1.call-done
  723.3 2.5 convolution_add_fusion.7
  730.1 2.5 fusion.84
  734.9 5.6 fusion.156
  740.5 6.2 convolution_add_fusion.2
  746.8 4.7 fusion.157
  751.5 6.2 convolution_add_fusion.1
  758.1 4.7 fusion.158
  762.9 6.4 convolution_add_fusion
  770.3 2.8 fusion.47
  773.2 73.4 %all-reduce.6 = (f32[448]{0:T(512)}, f32[64]{0:T(128)}, f32[64]{0:T(128)}, f32[896]{0:T(1024)}, f32[896]{0:T(1024)}) all-reduce(f32[448]{0:T(512)S(1)} %add.315, f32[64]{0:T(128)S(1)} %add.316, f32[64]{0:T(128)S(1)} %add.317, f32[896]{0:T(1024)S(1)} %add.318, f32[896]{0:T(1024)S(1)} %add.322), channel_id=1, replica_groups=mesh['dp'=4,'ctx'=4,'tensor'=2] {'dp','ctx'}, use_global_device_ids=true, to_apply=%region_32.33 | all-reduce | flops 2368 | bytes 18944 | tf_op jit(solution)/shard_map/psum | solution.py:353
  846.6 4.2 fusion.42
  854.3 18.7 %reduce-scatter.35.cloned.1.call-done = f32[56,64]{1,0:T(8,128)} async-done(((f32[896,64]{1,0:T(8,128)}), f32[56,64]{1,0:T(8,128)}) %reduce-scatter.35.cloned.1.call-update) | async-done | bytes 14352
  873.0 81.7 %reduce-scatter.29.cloned.1.call-done = f32[56,448]{1,0:T(8,128)} async-done(((f32[896,448]{1,0:T(8,128)}), f32[56,448]{1,0:T(8,128)}) %reduce-scatter.29.cloned.1.call-update) | async-done | bytes 100368 | tf_op jit(solution)/shard_map/reduce_scatter | solution.py:345
  954.7 82.7 %reduce-scatter.31.cloned.1.call-done = f32[448,56]{0,1:T(8,128)} async-done(((f32[448,896]{0,1:T(8,128)}), f32[448,56]{0,1:T(8,128)}) %reduce-scatter.31.cloned.1.call-update) | async-done | bytes 100368 | tf_op jit(solution)/shard_map/reduce_scatter | solution.py:348
  1037.4 187.3 %reduce-scatter.37.cloned.1.call-done = f32[56,2432]{1,0:T(8,128)} async-done(((f32[896,2432]{1,0:T(8,128)}), f32[56,2432]{1,0:T(8,128)}) %reduce-scatter.37.cloned.1.call-update) | async-done | bytes 544784
  1224.6 190.5 %reduce-scatter.39.cloned.1.call-done = f32[56,2432]{1,0:T(8,128)} async-done(((f32[896,2432]{1,0:T(8,128)}), f32[56,2432]{1,0:T(8,128)}) %reduce-scatter.39.cloned.1.call-update) | async-done | bytes 544784
  1415.1 190.6 %reduce-scatter.41.cloned.1.call-done = f32[2432,56]{0,1:T(8,128)} async-done(((f32[2432,896]{0,1:T(8,128)}), f32[2432,56]{0,1:T(8,128)}) %reduce-scatter.41.cloned.1.call-update) | async-done | bytes 544784
  (380 shorter events, 97.9 us)
Async XLA Ops:
  8.0 103.2 %copy-start = (bf16[2,2,256,896]{3,2,1,0:T(8,128)(2,1)S(1)}, bf16[2,2,256,896]{3,2,1,0:T(8,128)(2,1)}, u32[]{:S(2)}) copy-start(bf16[2,2,256,896]{3,2,1,0:T(8,128)(2,1)} %param.15) | copy-start | bytes 5505028
  8.0 65.9 %copy-start.87 = (bf16[56,64]{1,0:T(8,128)(2,1)S(1)}, bf16[56,64]{1,0:T(8,128)(2,1)}, u32[]{:S(2)}) copy-start(bf16[56,64]{1,0:T(8,128)(2,1)} %param.19) | copy-start | bytes 21508
  8.0 103.2 %copy-start.71 = (f32[896]{0:T(1024)S(1)}, f32[896]{0:T(1024)}, u32[]{:S(2)}) copy-start(f32[896]{0:T(1024)} %param.25) | copy-start | bytes 10756
  8.0 323.5 %all-reduce.18.cloned.1.call-start = ((), (), s32[]{:S(2)}) async-start(), calls=%async_computation.23 | async-start | bytes 3670016 | tf_op jit(solution)/shard_map/psum | solution.py:54
  25.3 86.4 %copy-start.91 = (f32[64]{0:T(128)S(1)}, f32[64]{0:T(128)}, u32[]{:S(2)}) copy-start(f32[64]{0:T(128)} %param.23) | copy-start | bytes 772
  25.9 86.9 %copy-start.76 = (f32[1,2,2,128]{3,1,2,0:T(2,128)}, f32[1,2,2,128]{3,1,2,0:T(2,128)S(1)}, u32[]{:S(2)}) copy-start(f32[1,2,2,128]{3,1,2,0:T(2,128)S(1)} %copy.215) | copy-start | bytes 6148
  25.9 86.9 %copy-start.78 = (f32[1,2,2,128]{3,1,2,0:T(2,128)}, f32[1,2,2,128]{3,1,2,0:T(2,128)S(1)}, u32[]{:S(2)}) copy-start(f32[1,2,2,128]{3,1,2,0:T(2,128)S(1)} %copy.212) | copy-start | bytes 6148
  73.9 40.9 %copy-start.17 = (bf16[896,448]{1,0:T(8,128)(2,1)}, bf16[896,448]{1,0:T(8,128)(2,1)S(1)}, u32[]{:S(2)}) copy-start(bf16[896,448]{1,0:T(8,128)(2,1)S(1)} %all_gather.21) | copy-start | bytes 2408452
  113.2 42.7 %copy-start.92 = (f32[64]{0:T(128)S(1)}, f32[64]{0:T(128)}, u32[]{:S(2)}) copy-start(f32[64]{0:T(128)} %param.24) | copy-start | bytes 772
  166.7 23.4 %copy-start.53 = (f32[2,256,32]{1,2,0:T(8,128)}, f32[2,256,32]{1,2,0:T(8,128)S(1)}, u32[]{:S(2)}) copy-start(f32[2,256,32]{1,2,0:T(8,128)S(1)} %get-tuple-element.108) | copy-start | bytes 196612
  166.7 23.4 %copy-start.55 = (f32[2,256,32]{1,2,0:T(8,128)}, f32[2,256,32]{1,2,0:T(8,128)S(1)}, u32[]{:S(2)}) copy-start(f32[2,256,32]{1,2,0:T(8,128)S(1)} %get-tuple-element.130) | copy-start | bytes 196612
  169.1 40.5 %copy-start.31 = (bf16[2,1792,64]{1,2,0:T(8,128)(2,1)}, bf16[2,1792,64]{1,2,0:T(8,128)(2,1)S(1)}, u32[]{:S(2)}) copy-start(bf16[2,1792,64]{1,2,0:T(8,128)(2,1)S(1)} %reshape.452) | copy-start | bytes 1376260
  188.6 5.4 copy-start.68
  211.7 27.7 %copy-start.1 = (f32[2,1792,1024]{1,2,0:T(8,128)}, f32[2,1792,1024]{1,2,0:T(8,128)S(1)}, u32[]{:S(2)}) copy-start(f32[2,1792,1024]{1,2,0:T(8,128)S(1)} %fusion.88) | copy-start | bytes 44040196
  224.4 15.0 copy-start.19
  247.6 45.3 %copy-start.20 = (pred[1792,1024]{0,1:T(8,128)(4,1)S(1)}, pred[1792,1024]{0,1:T(8,128)(4,1)}, u32[]{:S(2)}) copy-start(pred[1792,1024]{0,1:T(8,128)(4,1)} %iota_compare_fusion) | copy-start | bytes 5505028
  292.8 17.2 %copy-start.15 = (bf16[448,896]{0,1:T(8,128)(2,1)}, bf16[448,896]{0,1:T(8,128)(2,1)S(1)}, u32[]{:S(2)}) copy-start(bf16[448,896]{0,1:T(8,128)(2,1)S(1)} %all_gather.25) | copy-start | bytes 2408452
  311.8 79.3 %all-gather.4.cloned.1.call-start = ((), (), s32[]{:S(2)}) async-start(), calls=%async_computation.9 | async-start | bytes 4630528 | tf_op jit(solution)/shard_map/all_gather | solution.py:71
  312.4 157.4 %all-gather.6.cloned.1.call-start = ((), (), s32[]{:S(2)}) async-start(), calls=%async_computation.10 | async-start | bytes 4630528 | tf_op jit(solution)/shard_map/all_gather | solution.py:72
  313.0 235.5 %all-gather.8.cloned.1.call-start = ((), (), s32[]{:S(2)}) async-start(), calls=%async_computation.11 | async-start | bytes 4630528 | tf_op jit(solution)/shard_map/all_gather | solution.py:73
  313.6 290.2 %all-reduce.16.cloned.1.call-start = ((), (), s32[]{:S(2)}) async-start(), calls=%async_computation.22 | async-start | bytes 3670016 | tf_op jit(solution)/shard_map/psum | solution.py:58
  316.5 17.3 %copy-start.75 = (f32[896]{0:T(1024)S(1)}, f32[896]{0:T(1024)}, u32[]{:S(2)}) copy-start(f32[896]{0:T(1024)} %param.29) | copy-start | bytes 10756
  469.8 7.7 copy-start.52
  469.8 7.7 copy-start.95
  469.8 12.6 slice-start.2
  477.5 4.9 slice-start.3
  559.3 6.9 copy-start.40
  559.4 17.1 %copy-start.38 = (bf16[512,2432]{1,0:T(8,128)(2,1)}, bf16[512,2432]{1,0:T(8,128)(2,1)S(1)}, u32[]{:S(2)}) copy-start(bf16[512,2432]{1,0:T(8,128)(2,1)S(1)} %get-tuple-element.58) | copy-start | bytes 7471108
  559.4 6.9 copy-start.34
  559.4 7.0 copy-start.94
  559.4 14.3 slice-start
  559.4 17.1 %slice-start.4 = ((s8[4358144]{0:T(1024)(128)(4,1)}), s8[4194304]{0:T(1024)(128)(4,1)S(1)}, s32[]{:S(2)}) async-start(s8[4358144]{0:T(1024)(128)(4,1)} %bitcast.457), calls=%async_computation.28 | async-start | bytes 8388608
  566.3 7.3 slice-start.1
  566.3 10.2 slice-start.5
  573.6 6.7 copy-start.98
  584.1 113.4 %reduce-scatter.27.cloned.1.call-start = ((), (), s32[]{:S(2)}) async-start(), calls=%async_computation.13 | async-start | bytes 655360 | tf_op jit(solution)/shard_map/reduce_scatter | solution.py:289
  584.2 70.6 %copy-start.85 = (f32[2,1792]{1,0:T(2,128)}, f32[2,1792]{1,0:T(2,128)S(1)}, u32[]{:S(2)}) copy-start(f32[2,1792]{1,0:T(2,128)S(1)} %log_add_fusion.1) | copy-start | bytes 43012
  584.2 6.9 copy-start.97
  619.6 8.6 copy-start.50
  619.7 8.6 copy-start.51
  619.7 8.7 copy-start.21
  628.4 9.8 copy-start.32
  643.8 65.1 %reduce-scatter.25.cloned.1.call-start = ((), (), s32[]{:S(2)}) async-start(), calls=%async_computation.12 | async-start | bytes 655360 | tf_op jit(solution)/shard_map/reduce_scatter | solution.py:289
  647.0 7.8 copy-start.33
  654.8 13.5 copy-start.48
  685.8 8.1 copy-start.54
  685.8 8.1 copy-start.56
  685.9 84.5 %all-reduce.14.cloned.1.call-start = ((), (), s32[]{:S(2)}) async-start(), calls=%async_computation.21 | async-start | bytes 7340032 | tf_op jit(solution)/shard_map/psum | solution.py:54
  695.3 15.5 copy-start.26
  696.6 14.6 copy-start.43
  696.6 14.6 copy-start.45
  697.5 14.4 copy-start.24
  717.5 136.8 %reduce-scatter.33.cloned.1.call-start = ((), (), s32[]{:S(2)}) async-start(), calls=%async_computation.16 | async-start | bytes 487424
  721.3 151.7 %reduce-scatter.35.cloned.1.call-start = ((), (), s32[]{:S(2)}) async-start(), calls=%async_computation.17 | async-start | bytes 487424
  725.8 228.9 %reduce-scatter.29.cloned.1.call-start = ((), (), s32[]{:S(2)}) async-start(), calls=%async_computation.14 | async-start | bytes 1949696 | tf_op jit(solution)/shard_map/reduce_scatter | solution.py:345
  730.0 307.4 %reduce-scatter.31.cloned.1.call-start = ((), (), s32[]{:S(2)}) async-start(), calls=%async_computation.15 | async-start | bytes 1949696 | tf_op jit(solution)/shard_map/reduce_scatter | solution.py:348
  734.6 490.0 %reduce-scatter.37.cloned.1.call-start = ((), (), s32[]{:S(2)}) async-start(), calls=%async_computation.18 | async-start | bytes 9261056
  734.8 5.6 copy-start.11
  734.9 5.6 copy-start.41
  746.7 668.4 %reduce-scatter.39.cloned.1.call-start = ((), (), s32[]{:S(2)}) async-start(), calls=%async_computation.19 | async-start | bytes 9261056
  746.8 4.7 copy-start.12
  757.8 847.9 %reduce-scatter.41.cloned.1.call-start = ((), (), s32[]{:S(2)}) async-start(), calls=%async_computation.20 | async-start | bytes 9261056
  758.1 4.8 copy-start.14
  758.1 4.8 copy-start.27
  (57 other events, 130.8 us)
Sparse Core Ops, SparseCore 0:
  312.0 19.5 all-reduce.17
  584.2 19.5 all-reduce.15
  643.9 22.7 reduce-scatter.26
  686.0 22.8 reduce-scatter.24
  717.6 22.6 all-reduce.13
Sparse Core Ops, SparseCore 1:
  315.4 75.7 all-gather.3
  394.1 75.7 all-gather.5
  472.8 75.7 all-gather.7
  721.4 75.3 reduce-scatter.32
  799.6 73.3 reduce-scatter.34
  876.0 78.6 reduce-scatter.28
  957.4 79.9 reduce-scatter.30
  1040.2 184.3 reduce-scatter.36
  1227.5 187.5 reduce-scatter.38
  1418.1 187.5 reduce-scatter.40
where the time goes:
time: 1620 us; the launch traced here: 1610 us
  waiting for transfers between devices  972 us (60%)
  blocking collectives  286 us (18%)
  matrix products  224 us (14%)
  other arithmetic  59.8 us (4%)
  local copies, waits for them, and re-layouts  53 us (3%)
  between operations  17.4 us (1%)
    unnamed x20, waiting for transfers between devices  589 us
    dot_general x42, matrix products, product(): return jnp.dot(left, right, preferred_element_type=jnp.float32)  143 us
    reduce_scatter x1, waiting for transfers between devices, local(): lax.psum_scatter(totals[3], ('dp', 'ctx'), scatter_dimension=1, tiled=True)  82.7 us
    reduce_scatter x1, waiting for transfers between devices, local(): lax.psum_scatter(totals[0], ('dp', 'ctx'), scatter_dimension=0, tiled=True)  81.7 us
    psum x1, blocking collectives, local(): lax.psum((totals[7], totals[8], totals[9], totals[10], totals[11]), ('dp'...  73.4 us
    all_gather x1, waiting for transfers between devices, fetch_forward(): lax.all_gather(up_weight, ('dp', 'ctx'), axis=0, tiled=True)  71.1 us
    all_gather x1, waiting for transfers between devices, fetch_forward(): lax.all_gather(down_weight, ('dp', 'ctx'), axis=1, tiled=True)  61.7 us
    all_gather x1, waiting for transfers between devices, fetch_forward(): lax.all_gather(gate_weight, ('dp', 'ctx'), axis=0, tiled=True)  55.4 us
  transfers between devices with their start and end apart: 15, of which 12 were waited for; matrix products, arithmetic and copies ran while one was open for 10% of the time, Pallas kernels for 0%

commit v1 on v0

v1 whole, which is shorter than its diff:
```python
import functools

import jax
import jax.numpy as jnp
from jax import lax
from jax.experimental import pallas as pl
from jax.experimental.pallas import tpu as pltpu
from jax.sharding import PartitionSpec as P

HEAD = 64

eps = 1e-06
theta = 1000000.0
masked = -1e30
f32 = jnp.float32
bf16 = jnp.bfloat16
VMEM_LIMIT = 56 * 1024 * 1024


def contract(left, right, dims):
    return lax.dot_general(left, right, ((dims[:1], dims[1:]), ((), ())), preferred_element_type=f32)


def swap(value, axis, size, bit):
    return lax.ppermute(value, axis, [(i, i ^ bit) for i in range(size)])


def tensor_sum(partial, size):
    sent = partial.astype(bf16)
    if size == 2:
        return sent.astype(f32) + swap(sent, "tensor", 2, 1).astype(f32)
    return lax.psum(sent, "tensor").astype(f32)


def place_kernel(where_ref, *refs):
    count = len(refs) - 2
    pieces, out_ref, sems = refs[:count], refs[count], refs[count + 1]
    copies = []
    for i in range(count):
        copies.append(pltpu.make_async_copy(pieces[i], out_ref.at[where_ref[i]], sems.at[i]))
    for copy in copies:
        copy.start()
    for copy in copies:
        copy.wait()


def place(pieces, where):
    count = len(pieces)
    return pl.pallas_call(
        place_kernel,
        out_shape=jax.ShapeDtypeStruct((count,) + pieces[0].shape, pieces[0].dtype),
        in_specs=[pl.BlockSpec(memory_space=pltpu.SMEM)] + [pl.BlockSpec(memory_space=pl.ANY)] * count,
        out_specs=pl.BlockSpec(memory_space=pltpu.VMEM),
        scratch_shapes=[pltpu.SemaphoreType.DMA((count,))],
        compiler_params=pltpu.CompilerParams(vmem_limit_bytes=VMEM_LIMIT),
    )(where, *pieces)


def gather_rows(shard, fast):
    if not fast:
        return lax.all_gather(shard, ("dp", "ctx"), axis=0, tiled=True)
    rows, width = shard.shape
    dp, ctx = lax.axis_index("dp"), lax.axis_index("ctx")
    other = swap(shard, "ctx", 4, 1)
    even = ctx % 2 == 0
    near = jnp.concatenate([jnp.where(even, shard, other), jnp.where(even, other, shard)], axis=0)
    far = swap(near, "ctx", 4, 2)
    near_1 = swap(near, "dp", 4, 1)
    near_2 = swap(near, "dp", 4, 2)
    near_3 = swap(near_1, "dp", 4, 2)
    far_2 = swap(far, "dp", 4, 2)
    far_1 = swap(far, "dp", 4, 1)
    far_3 = swap(far_2, "dp", 4, 1)
    half = ctx // 2
    spots = [(dp ^ k) * 2 + (half ^ h) for h in (0, 1) for k in (0, 1, 2, 3)]
    whole = place(
        [near, near_1, near_2, near_3, far, far_1, far_2, far_3], jnp.stack(spots).astype(jnp.int32)
    )
    return whole.reshape(16 * rows, width)


def pick(value, index, axis):
    return lax.dynamic_index_in_dim(value, index, axis, keepdims=False)


def add16(left, right):
    return (left.astype(f32) + right.astype(f32)).astype(bf16)


def scatter_rows(total, fast):
    total = total.astype(bf16)
    if not fast:
        return lax.psum_scatter(total, ("dp", "ctx"), scatter_dimension=0, tiled=True).astype(f32)
    rows, width = total.shape[0] // 16, total.shape[1]
    dp, ctx = lax.axis_index("dp"), lax.axis_index("ctx")
    y, x, half, odd = dp // 2, dp % 2, ctx // 2, ctx % 2
    cut = total.reshape(2, 2, 2, 2 * rows, width)
    first, second = cut[:, :, 0], cut[:, :, 1]
    first = add16(pick(first, y, 0), swap(pick(first, 1 - y, 0), "dp", 4, 2))
    second = add16(pick(second, x, 1), swap(pick(second, 1 - x, 1), "dp", 4, 1))
    first = add16(pick(first, x, 0), swap(pick(first, 1 - x, 0), "dp", 4, 1))
    second = add16(pick(second, y, 0), swap(pick(second, 1 - y, 0), "dp", 4, 2))
    low = half == 0
    both = add16(
        jnp.where(low, first, second), swap(jnp.where(low, second, first), "ctx", 4, 2)
    ).reshape(2, rows, width)
    return pick(both, odd, 0).astype(f32) + swap(pick(both, 1 - odd, 0), "ctx", 4, 1).astype(f32)


def sum_small(value, fast):
    if not fast:
        return lax.psum(value, ("dp", "ctx"))
    for axis, bit in (("ctx", 1), ("ctx", 2), ("dp", 1), ("dp", 2)):
        value = value + swap(value, axis, 4, bit)
    return value


def earlier(value, ctx_size):
    blocks = [value]
    for back in range(1, ctx_size):
        blocks.append(lax.ppermute(value, "ctx", [(i, i + back) for i in range(ctx_size - back)]))
    return jnp.concatenate(blocks, axis=-1)


def give_back(value, ctx_size):
    stretch = value.shape[-1] // ctx_size
    total = value[..., :stretch].astype(f32)
    for back in range(1, ctx_size):
        block = value[..., back * stretch : (back + 1) * stretch]
        total = total + lax.ppermute(
            block, "ctx", [(i + back, i) for i in range(ctx_size - back)]
        ).astype(f32)
    return total


def set_up(keys, queries, bias):
    info = keys[0].T
    allowed = (info[:, 0:1] == queries[0, 0:1]) & (info[:, 1:2] <= queries[0, 1:2])
    bias[...] = jnp.where(allowed, 0.0, masked)


def turned(value):
    return value.astype(f32).T.astype(bf16)


def forward_kernel(q_ref, kv_ref, keys, queries, out_ref, log_ref, bias, key):
    @pl.when(pl.program_id(1) == 0)
    def _():
        set_up(keys, queries, bias)
        key[...] = turned(kv_ref[:HEAD, :])

    scores = jnp.dot(key[...], q_ref[...], preferred_element_type=f32) + bias[...]
    top = jnp.max(scores, axis=0, keepdims=True)
    weights = jnp.exp(scores - top)
    total = jnp.sum(weights, axis=0, keepdims=True)
    summed = jnp.dot(kv_ref[HEAD:, :], weights.astype(bf16), preferred_element_type=f32)
    out_ref[...] = (summed / total).astype(bf16)
    log_ref[0, 0] = top + jnp.log(total)


def backward_kernel(
    q_ref, do_ref, out_ref, log_ref, kv_ref, keys, queries, dq_ref, dkv_ref, bias, key, val, acc
):
    head = pl.program_id(1)

    @pl.when(head == 0)
    def _():
        set_up(keys, queries, bias)
        key[...] = turned(kv_ref[:HEAD, :])
        val[...] = turned(kv_ref[HEAD:, :])
        acc[...] = jnp.zeros_like(acc)

    query, grad = q_ref[...], do_ref[...]
    scores = jnp.dot(key[...], query, preferred_element_type=f32) + bias[...]
    prob = jnp.exp(scores - log_ref[0, 0])
    delta = jnp.sum(grad.astype(f32) * out_ref[...].astype(f32), axis=0, keepdims=True)
    grad_prob = jnp.dot(val[...], grad, preferred_element_type=f32)
    grad_score = (prob * (grad_prob - delta)).astype(bf16)
    dq_ref[...] = jnp.dot(kv_ref[:HEAD, :], grad_score, preferred_element_type=f32)
    acc[:HEAD, :] += contract(query, grad_score, (1, 1))
    acc[HEAD:, :] += contract(grad, prob.astype(bf16), (1, 1))

    @pl.when(head == pl.num_programs(1) - 1)
    def _():
        dkv_ref[...] = acc[...].astype(bf16)


def attention_specs(stretch, length):
    head_block = pl.BlockSpec((HEAD, stretch), lambda s, h: (h, s))
    log_block = pl.BlockSpec((1, 1, 1, stretch), lambda s, h: (s, h, 0, 0))
    kv_block = pl.BlockSpec((2 * HEAD, length), lambda s, h: (0, s))
    key_block = pl.BlockSpec((1, 8, length), lambda s, h: (s, 0, 0))
    query_block = pl.BlockSpec((1, 8, stretch), lambda s, h: (s, 0, 0))
    return head_block, log_block, kv_block, [key_block, query_block]


def attention_forward(query, pair, ids, stretch, length):
    seqs, group = query.shape[1] // stretch, query.shape[0] // HEAD
    head_block, log_block, kv_block, id_blocks = attention_specs(stretch, length)
    return pl.pallas_call(
        forward_kernel,
        grid=(seqs, group),
        in_specs=[head_block, kv_block] + id_blocks,
        out_specs=[head_block, log_block],
        out_shape=[
            jax.ShapeDtypeStruct(query.shape, bf16),
            jax.ShapeDtypeStruct((seqs, group, 1, stretch), f32),
        ],
        scratch_shapes=[pltpu.VMEM((length, stretch), f32), pltpu.VMEM((length, HEAD), bf16)],
        compiler_params=pltpu.CompilerParams(vmem_limit_bytes=VMEM_LIMIT),
    )(query, pair, *ids)


def attention_backward(query, grad, attended, logsum, pair, ids, stretch, length):
    seqs, group = query.shape[1] // stretch, query.shape[0] // HEAD
    head_block, log_block, kv_block, id_blocks = attention_specs(stretch, length)
    return pl.pallas_call(
        backward_kernel,
        grid=(seqs, group),
        in_specs=[head_block, head_block, head_block, log_block, kv_block] + id_blocks,
        out_specs=[head_block, kv_block],
        out_shape=[
            jax.ShapeDtypeStruct(query.shape, f32),
            jax.ShapeDtypeStruct(pair.shape, bf16),
        ],
        scratch_shapes=[
            pltpu.VMEM((length, stretch), f32),
            pltpu.VMEM((length, HEAD), bf16),
            pltpu.VMEM((length, HEAD), bf16),
            pltpu.VMEM((2 * HEAD, length), f32),
        ],
        compiler_params=pltpu.CompilerParams(vmem_limit_bytes=VMEM_LIMIT),
    )(query, grad, attended, logsum, pair, *ids)


def turn(values, cosine, sine, sign):
    feats, tokens = values.shape
    parts = values.reshape(feats // HEAD, 2, HEAD // 2, tokens)
    a, b = parts[:, 0], parts[:, 1]
    s = sine * sign
    return jnp.stack([a * cosine - b * s, b * cosine + a * s], axis=1).reshape(feats, tokens)


def norm_grad(grad, gain, unit, inverse):
    scaled = grad * gain
    return inverse * (scaled - unit * jnp.mean(scaled * unit, axis=-1, keepdims=True))


def local(
    sizes,
    activations,
    segments,
    cotangent,
    query_weight,
    key_weight,
    value_weight,
    out_weight,
    query_bias,
    key_bias_vector,
    value_bias,
    attention_gain,
    gate_weight,
    up_weight,
    down_weight,
    mlp_gain,
):
    dp_size, ctx_size, tensor_size = sizes
    fast = dp_size == 4 and ctx_size == 4
    near_keys = ctx_size <= 4
    micros, per_micro, stretch, width = activations.shape
    seqs = micros * per_micro
    tokens = seqs * stretch
    length = ctx_size * stretch
    qw = query_weight.shape[1]
    units = gate_weight.shape[1]
    scale = HEAD ** (-0.5)
    ctx = lax.axis_index("ctx")

    qkv_shard = jnp.concatenate([query_weight, key_weight, value_weight], axis=1)
    w_qkv = gather_rows(qkv_shard, fast)
    w_out = gather_rows(out_weight.T, fast)
    w_gate = gather_rows(gate_weight, fast)
    w_up = gather_rows(up_weight, fast)
    w_down = gather_rows(down_weight.T, fast)

    own_ids = segments.reshape(seqs, stretch)
    steps = jnp.arange(stretch, dtype=jnp.int32)
    query_pos = ctx * stretch + steps
    if near_keys:
        key_pos = jnp.concatenate([(ctx - r) * stretch + steps for r in range(ctx_size)])
        key_ids = jnp.where(key_pos >= 0, earlier(own_ids, ctx_size), -1)
    else:
        key_pos = jnp.arange(length, dtype=jnp.int32)
        key_ids = lax.all_gather(own_ids, "ctx", axis=1, tiled=True)
    before = (key_ids[:, :, None] == own_ids[:, None, :]) & (
        key_pos[None, :, None] < query_pos[None, None, :]
    )
    position = jnp.sum(before.astype(f32), axis=1).reshape(1, tokens)
    freq = theta ** (-(2.0 / HEAD) * jnp.arange(HEAD // 2, dtype=f32))
    angle = freq[:, None] * position
    cosine, sine = jnp.cos(angle), jnp.sin(angle)
    ids = tuple(
        jnp.concatenate(
            [number[:, None], jnp.broadcast_to(place_of, number.shape)[:, None]] + [number[:, None]] * 6, axis=1
        ).astype(f32)
        for number, place_of in ((key_ids, key_pos), (own_ids, query_pos))
    )

    source = activations.reshape(tokens, width).astype(f32)
    inverse1 = lax.rsqrt(jnp.mean(source * source, axis=-1, keepdims=True) + eps)
    unit1 = source * inverse1
    normed1 = (unit1 * attention_gain).astype(bf16)
    bias = jnp.concatenate([query_bias, key_bias_vector, value_bias])
    qkv = contract(w_qkv, normed1, (0, 1)) + bias[:, None]
    query = (turn(qkv[:qw], cosine, sine, 1.0).astype(bf16) * scale).astype(bf16)
    key = turn(qkv[qw : qw + HEAD], cosine, sine, 1.0).astype(bf16)
    pair = jnp.concatenate([key, qkv[qw + HEAD :].astype(bf16)], axis=0)

    def group_of(value, m):
        wide = value.shape[1] // micros
        return value[:, m * wide : (m + 1) * wide]

    def ids_of(m):
        return tuple(v[m * per_micro : (m + 1) * per_micro] for v in ids)

    pairs, attended, logsums = [], [], []
    for m in range(micros):
        mine = group_of(pair, m).reshape(2 * HEAD, per_micro, stretch)
        if near_keys:
            wide = earlier(mine, ctx_size)
        else:
            wide = lax.all_gather(mine, "ctx", axis=2, tiled=True)
        pairs.append(wide.reshape(2 * HEAD, per_micro * length))
    for m in range(micros):
        out, logsum = attention_forward(group_of(query, m), pairs[m], ids_of(m), stretch, length)
        attended.append(out)
        logsums.append(logsum)
    partial = jnp.concatenate([contract(out, w_out, (0, 1)) for out in attended], axis=0)
    mixed = source + tensor_sum(partial, tensor_size)

    inverse2 = lax.rsqrt(jnp.mean(mixed * mixed, axis=-1, keepdims=True) + eps)
    unit2 = mixed * inverse2
    normed2 = (unit2 * mlp_gain).astype(bf16)
    gate = contract(normed2, w_gate, (1, 0))
    up_proj = contract(normed2, w_up, (1, 0))
    sigma = jax.nn.sigmoid(gate)
    silu = gate * sigma
    hidden = (silu * up_proj).astype(bf16)
    result = mixed + tensor_sum(contract(hidden, w_down, (1, 1)), tensor_size)
    output = result.astype(bf16).reshape(activations.shape)

    grad_branch = cotangent.reshape(tokens, width)
    grad_result = grad_branch.astype(f32)
    grad_down = scatter_rows(contract(grad_branch, hidden, (0, 0)), fast)
    grad_hidden = contract(grad_branch, w_down, (1, 0))
    grad_gate = (grad_hidden * up_proj * sigma * (1.0 + gate * (1.0 - sigma))).astype(bf16)
    grad_up = (grad_hidden * silu).astype(bf16)
    grad_gate_w = scatter_rows(contract(normed2, grad_gate, (0, 0)), fast)
    grad_up_w = scatter_rows(contract(normed2, grad_up, (0, 0)), fast)
    grad_normed2 = tensor_sum(
        contract(grad_gate, w_gate, (1, 1)) + contract(grad_up, w_up, (1, 1)), tensor_size
    )
    grad_gain2 = jnp.sum(grad_normed2 * unit2, axis=0)
    grad_mixed = grad_result + norm_grad(grad_normed2, mlp_gain, unit2, inverse2)

    grad_attn = grad_mixed.astype(bf16)
    grad_out_w = jnp.zeros((width, qw), f32)
    grad_queries, grad_pairs = [], []
    for m in range(micros):
        rows = tokens // micros
        grad_attn_now = grad_attn[m * rows : (m + 1) * rows]
        grad_out_w = grad_out_w + contract(grad_attn_now, attended[m], (0, 1))
        grad_attended = contract(w_out, grad_attn_now, (0, 1)).astype(bf16)
        grad_query, grad_wide = attention_backward(
            group_of(query, m), grad_attended, attended[m], logsums[m], pairs[m], ids_of(m), stretch, length
        )
        grad_wide = grad_wide.reshape(2 * HEAD, per_micro, length)
        if near_keys:
            own = give_back(grad_wide, ctx_size)
        else:
            own = lax.psum_scatter(grad_wide, "ctx", scatter_dimension=2, tiled=True).astype(f32)
        grad_queries.append(grad_query)
        grad_pairs.append(own.reshape(2 * HEAD, per_micro * stretch))
    grad_query = jnp.concatenate(grad_queries, axis=1) * scale
    grad_pair = jnp.concatenate(grad_pairs, axis=1)
    grad_qkv = jnp.concatenate(
        [
            turn(grad_query, cosine, sine, -1.0),
            turn(grad_pair[:HEAD], cosine, sine, -1.0),
            grad_pair[HEAD:],
        ],
        axis=0,
    ).astype(bf16)
    grad_bias = jnp.sum(grad_qkv.astype(f32), axis=1)
    grad_out_w = scatter_rows(grad_out_w, fast)
    grad_qkv_w = scatter_rows(contract(normed1, grad_qkv, (0, 1)), fast)
    grad_normed1 = tensor_sum(contract(grad_qkv, w_qkv, (0, 1)), tensor_size)
    grad_gain1 = jnp.sum(grad_normed1 * unit1, axis=0)
    grad_source = grad_mixed + norm_grad(grad_normed1, attention_gain, unit1, inverse1)

    smalls = sum_small(jnp.concatenate([grad_bias, grad_gain1, grad_gain2]), fast)
    ends = [qw, qw + HEAD, qw + 2 * HEAD, qw + 2 * HEAD + width]
    small = jnp.split(smalls, ends)
    return (
        output,
        grad_source.reshape(activations.shape),
        grad_qkv_w[:, :qw],
        grad_qkv_w[:, qw : qw + HEAD],
        grad_qkv_w[:, qw + HEAD :],
        grad_out_w.T,
        small[0],
        small[1],
        small[2],
        small[3],
        grad_gate_w,
        grad_up_w,
        grad_down.T,
        small[4],
    )


def solution(mesh):
    sizes = (mesh.shape["dp"], mesh.shape["ctx"], mesh.shape["tensor"])
    return jax.shard_map(
        functools.partial(local, sizes),
        mesh=mesh,
        in_specs=(
            P(None, "dp", "ctx", None),
            P(None, "dp", "ctx"),
            P(None, "dp", "ctx", None),
            P(("dp", "ctx"), "tensor"),
            P(("dp", "ctx"), "tensor"),
            P(("dp", "ctx"), "tensor"),
            P("tensor", ("dp", "ctx")),
            P("tensor"),
            P("tensor"),
            P("tensor"),
            P(),
            P(("dp", "ctx"), "tensor"),
            P(("dp", "ctx"), "tensor"),
            P("tensor", ("dp", "ctx")),
            P(),
        ),
        out_specs=(
            P(None, "dp", "ctx", None),
            P(None, "dp", "ctx", None),
            P(("dp", "ctx"), "tensor"),
            P(("dp", "ctx"), "tensor"),
            P(("dp", "ctx"), "tensor"),
            P("tensor", ("dp", "ctx")),
            P("tensor"),
            P("tensor"),
            P("tensor"),
            P(),
            P(("dp", "ctx"), "tensor"),
            P(("dp", "ctx"), "tensor"),
            P("tensor", ("dp", "ctx")),
            P(),
        ),
        check_vma=False,
    )
```

time: 1620 us -> 647 us (0.40)
  waiting for transfers between devices: 972 us -> 198 us
  blocking collectives: 286 us -> 0 us
  starting transfers between devices: 1.28 us -> 139 us
  matrix products: 224 us -> 110 us
  Pallas kernels: 0 us -> 79.2 us
    unnamed x20 -> x0, waiting for transfers between devices: 589 us -> none
    all_gather x7 -> x0, blocking collectives: 213 us -> none  [the longest x1 48 us: fetch_forward(): lax.all_gather(query_weight, ('dp', 'ctx'), axis=0, tiled=True)]
    ppermute x0 -> x93, waiting for transfers between devices: none -> 198 us  [the longest x78 180 us: swap(): return lax.ppermute(value, axis, [(i, i ^ bit) for i in range(size)])]
    all_gather x3 -> x0, waiting for transfers between devices: 188 us -> none  [the longest x1 71.1 us: fetch_forward(): lax.all_gather(up_weight, ('dp', 'ctx'), axis=0, tiled=True)]
    reduce_scatter x4 -> x0, waiting for transfers between devices: 173 us -> none  [the longest x1 82.7 us: local(): lax.psum_scatter(totals[3], ('dp', 'ctx'), scatter_dimension=1, tiled=True)]
    ppermute x0 -> x93, starting transfers between devices: none -> 139 us  [the longest x78 82.1 us: swap(): return lax.ppermute(value, axis, [(i, i ^ bit) for i in range(size)])]
    dot_general x54 -> x18, matrix products: 224 us -> 110 us  [contract(): lax.dot_general(left, right, ((dims[:1], dims[1:]), ((), ())), preferred_...]
    pallas_call x0 -> x9, Pallas kernels: none -> 79.2 us  [the longest x2 30.8 us: attention_backward(): pl.pallas_call(backward_kernel, grid=(seqs, group), in_specs=[head_block,...]
  transfers between devices with their start and end apart: 15 -> 93, of which waited for: 12 -> 36; matrix products, arithmetic and copies ran while one was open for 10% -> 24% of each run, Pallas kernels for 0% -> 12%
where the time goes in v1:
time: 647 us; the launch traced here: 636 us
  waiting for transfers between devices  198 us (31%)
  starting transfers between devices  139 us (21%)
  matrix products  110 us (17%)
  Pallas kernels  79.2 us (12%)
  other arithmetic  57 us (9%)
  local copies, waits for them, and re-layouts  50 us (8%)
    ppermute x78, waiting for transfers between devices, swap(): return lax.ppermute(value, axis, [(i, i ^ bit) for i in range(size)])  180 us
    dot_general x18, matrix products, contract(): lax.dot_general(left, right, ((dims[:1], dims[1:]), ((), ())), preferred_...  110 us
    ppermute x78, starting transfers between devices, swap(): return lax.ppermute(value, axis, [(i, i ^ bit) for i in range(size)])  82.1 us
    ppermute x9, starting transfers between devices, earlier(): lax.ppermute(value, 'ctx', [(i, i + back) for i in range(ctx_size - back)])  48.6 us
    pallas_call x2, Pallas kernels, attention_backward(): pl.pallas_call(backward_kernel, grid=(seqs, group), in_specs=[head_block,...  30.8 us
    pallas_call x2, Pallas kernels, attention_forward(): pl.pallas_call(forward_kernel, grid=(seqs, group), in_specs=[head_block,...  27.5 us
    pallas_call x5, Pallas kernels, place(): pl.pallas_call(place_kernel, out_shape=jax.ShapeDtypeStruct((count,) + pi...  20.9 us
    ppermute x6, waiting for transfers between devices, give_back(): lax.ppermute(block, 'ctx', [(i + back, i) for i in range(ctx_size - back)])  17.9 us
  transfers between devices with their start and end apart: 93, of which 36 were waited for; matrix products, arithmetic and copies ran while one was open for 24% of the time, Pallas kernels for 12%

profile of v1, /device:TPU:0, one launch (start us, length us, event | category | flops | bytes accessed | tf_op | source)
XLA Modules:
  0.0 636.2 jit_solution(17083830570071993366)
XLA Ops:
  1.5 6.9 %collective-permute-start.10 = (s32[4,256]{1,0:T(4,128)S(1)}, s32[4,256]{1,0:T(4,128)S(1)}, u32[]{:S(2)}, u32[]{:S(2)}) collective-permute-start(s32[4,256]{1,0:T(4,128)S(1)} %concatenate.91), channel_id=1, source_target_pairs={{0,6},{1,7},{8,14},{9,15},{16,22},{17,23},{24,30},{25,31}} | collective-permute-start | bytes 12296 | tf_op jit(solution)/shard_map/ppermute | solution.py:121
  9.7 2.5 collective-permute-start.9
  28.4 3.0 collective-permute-start.18
  31.3 11.7 %collective-permute-done.4.refs_4_ = bf16[112,576]{1,0:T(8,128)(2,1)S(1)} collective-permute-done((bf16[112,576]{1,0:T(8,128)(2,1)S(1)}, bf16[112,576]{1,0:T(8,128)(2,1)S(1)}, u32[]{:S(2)}, u32[]{:S(2)}) %collective-permute-start.4) | collective-permute-done | bytes 129056 | tf_op jit(solution)/shard_map/ppermute | solution.py:25
  48.0 2.1 broadcast_select_fusion.4
  54.8 2.1 collective-permute-done.2.refs_2_
  64.6 3.1 shard_map.254
  67.7 2.8 convolution_add_fusion
  73.3 2.5 collective-permute-start.11
  77.7 4.9 collective-permute-start.12
  83.9 7.0 %collective-permute-start.22 = (bf16[128,2,256]{2,1,0:T(2,128)(2,1)}, bf16[128,2,256]{2,1,0:T(2,128)(2,1)S(1)}, u32[]{:S(2)}, u32[]{:S(2)}) collective-permute-start(bf16[128,2,256]{2,1,0:T(2,128)(2,1)} %reshape.734), channel_id=1, source_target_pairs={{0,2},{2,4},{4,6},{1,3},{3,5},{5,7},{8,10},{10,12},{12,14},{9,11},... | collective-permute-start | bytes 393224 | tf_op jit(solution)/shard_map/ppermute | solution.py:121
  94.1 9.3 %collective-permute-start.23 = (bf16[128,2,256]{2,1,0:T(2,128)(2,1)}, bf16[128,2,256]{2,1,0:T(2,128)(2,1)S(1)}, u32[]{:S(2)}, u32[]{:S(2)}) collective-permute-start(bf16[128,2,256]{2,1,0:T(2,128)(2,1)} %reshape.734), channel_id=1, source_target_pairs={{0,4},{2,6},{1,5},{3,7},{8,12},{10,14},{9,13},{11,15},{16,20},{18,... | collective-permute-start | bytes 393224 | tf_op jit(solution)/shard_map/ppermute | solution.py:121
  103.4 13.1 %collective-permute-start.24 = (bf16[128,2,256]{2,1,0:T(2,128)(2,1)}, bf16[128,2,256]{2,1,0:T(2,128)(2,1)S(1)}, u32[]{:S(2)}, u32[]{:S(2)}) collective-permute-start(bf16[128,2,256]{2,1,0:T(2,128)(2,1)} %reshape.734), channel_id=1, source_target_pairs={{0,6},{1,7},{8,14},{9,15},{16,22},{17,23},{24,30},{25,31}} | collective-permute-start | bytes 393224 | tf_op jit(solution)/shard_map/ppermute | solution.py:121
  118.3 2.9 shard_map.256
  123.2 2.8 collective-permute-start.46
  128.7 12.2 %collective-permute-done.38.refs_4_ = bf16[112,2432]{1,0:T(8,128)(2,1)S(1)} collective-permute-done((bf16[112,2432]{1,0:T(8,128)(2,1)S(1)}, bf16[112,2432]{1,0:T(8,128)(2,1)S(1)}, u32[]{:S(2)}, u32[]{:S(2)}) %collective-permute-start.38) | collective-permute-done | bytes 544800 | tf_op jit(solution)/shard_map/ppermute | solution.py:25
  143.8 20.5 %collective-permute-done.46.refs_4_ = bf16[112,2432]{1,0:T(8,128)(2,1)} collective-permute-done((bf16[112,2432]{1,0:T(8,128)(2,1)}, bf16[112,2432]{1,0:T(8,128)(2,1)}, u32[]{:S(2)}, u32[]{:S(2)}) %collective-permute-start.46) | collective-permute-done | bytes 544800 | tf_op jit(solution)/shard_map/ppermute | solution.py:25
  167.5 13.9 %shard_map.255 = (bf16[448,512]{1,0:T(8,128)(2,1)}, f32[2,7,1,256]{3,2,1,0:T(1,128)}) custom-call(bf16[448,512]{1,0:T(8,128)(2,1)} %get-tuple-element.60.q_ref, bf16[128,2048]{1,0:T(8,128)(2,1)} %bitcast.328, f32[2,8,1024]{2,1,0:T(8,128)} %get-tuple-element.84.keys, f32[2,8,256]{2,1,0:T(8,128)} %get-tuple-element.88.queries), custom_call_target="tpu_custom_call" | custom-call | tf_op jit(solution)/shard_map/pallas_call | solution.py:200
  186.4 13.7 %shard_map.257 = (bf16[448,512]{1,0:T(8,128)(2,1)}, f32[2,7,1,256]{3,2,1,0:T(1,128)}) custom-call(bf16[448,512]{1,0:T(8,128)(2,1)} %get-tuple-element.61.q_ref, bf16[128,2048]{1,0:T(8,128)(2,1)} %bitcast.330, f32[2,8,1024]{2,1,0:T(8,128)} %get-tuple-element.85.keys, f32[2,8,256]{2,1,0:T(8,128)} %get-tuple-element.89.queries), custom_call_target="tpu_custom_call" | custom-call | tf_op jit(solution)/shard_map/pallas_call | solution.py:200
  208.5 7.0 %collective-permute-done.37.refs_3_ = bf16[112,2432]{1,0:T(8,128)(2,1)S(1)} collective-permute-done((bf16[112,2432]{1,0:T(8,128)(2,1)S(1)}, bf16[112,2432]{1,0:T(8,128)(2,1)S(1)}, u32[]{:S(2)}, u32[]{:S(2)}) %collective-permute-start.37) | collective-permute-done | bytes 544800 | tf_op jit(solution)/shard_map/ppermute | solution.py:25
  216.7 10.6 %collective-permute-done.48.refs_6_ = bf16[112,2432]{1,0:T(8,128)(2,1)} collective-permute-done((bf16[112,2432]{1,0:T(8,128)(2,1)}, bf16[112,2432]{1,0:T(8,128)(2,1)}, u32[]{:S(2)}, u32[]{:S(2)}) %collective-permute-start.48) | collective-permute-done | bytes 544800 | tf_op jit(solution)/shard_map/ppermute | solution.py:25
  231.4 5.0 shard_map.258
  236.4 4.9 shard_map.259
  242.9 6.1 collective-permute-done.45.refs_3_
  250.5 5.0 shard_map.260
  255.5 10.3 %fusion.82 = f32[2432,1024]{0,1:T(8,128)} fusion(bf16[1024,896]{1,0:T(8,128)(2,1)S(1)} %bitcast.325, bf16[896,2432]{1,0:T(8,128)(2,1)} %bitcast.337), kind=kOutput, calls=%fused_computation.233 | convolution fusion | flops 4462739456 | bytes 16154624 | tf_op jit(solution)/shard_map/dot_general | solution.py:21
  265.9 2.4 multiply_reduce_fusion.2
  268.7 11.1 %fusion.80 = f32[1024,2432]{1,0:T(8,128)} fusion(bf16[1024,896]{1,0:T(8,128)(2,1)S(1)} %multiply_convert_fusion.1, bf16[896,2432]{1,0:T(8,128)(2,1)} %bitcast.333), kind=kOutput, calls=%fused_computation.231 | convolution fusion | flops 4462739456 | bytes 16154624 | tf_op jit(solution)/shard_map/dot_general | solution.py:21
  279.8 18.9 %fusion.2 = (bf16[1024,2432]{1,0:T(8,128)(2,1)}, bf16[1024,2432]{1,0:T(8,128)(2,1)}, bf16[1024,2432]{1,0:T(8,128)(2,1)}) fusion(f32[2432,1024]{0,1:T(8,128)} %fusion.82, f32[1024,2432]{1,0:T(8,128)} %fusion.80, bf16[1024,896]{1,0:T(8,128)(2,1)S(1)} %multiply_convert_fusion.1, bf16[896,2432]{1,0:T(8,128)(2,1)} %bitcast.339), kind=kOutput, calls=%fused_computation.4 | convolution fusion | flops 4500094976 | bytes 41058304 | tf_op jit(solution)/shard_map/dot_general | solution.py:21
  298.6 7.6 %convolution_convert_fusion.1 = bf16[896,2432]{1,0:T(8,128)(2,1)S(1)} fusion(bf16[1024,896]{1,0:T(8,128)(2,1)S(1)} %multiply_convert_fusion.1, bf16[1024,2432]{1,0:T(8,128)(2,1)} %get-tuple-element.37), kind=kOutput, calls=%fused_computation.10 | convolution fusion | flops 4464918528 | bytes 11173888 | tf_op jit(solution)/shard_map/dot_general | solution.py:21
  306.2 9.6 %fusion.81 = f32[1024,896]{1,0:T(8,128)} fusion(bf16[1024,2432]{1,0:T(8,128)(2,1)S(1)} %copy-done.96, bf16[896,2432]{1,0:T(8,128)(2,1)} %bitcast.340), kind=kOutput, calls=%fused_computation.232 | convolution fusion | flops 4462739456 | bytes 13008896 | tf_op jit(solution)/shard_map/dot_general | solution.py:21
  315.8 7.4 %convolution_convert_fusion = bf16[2432,896]{0,1:T(8,128)(2,1)S(1)} fusion(bf16[1024,2432]{1,0:T(8,128)(2,1)} %get-tuple-element.38, bf16[1024,896]{1,0:T(8,128)(2,1)S(1)} %bitcast.326), kind=kOutput, calls=%fused_computation.9 | convolution fusion | flops 4464918528 | bytes 11173888 | tf_op jit(solution)/shard_map/dot_general | solution.py:21
  332.6 7.4 %convolution_convert_fusion.2 = bf16[896,2432]{1,0:T(8,128)(2,1)S(1)} fusion(bf16[1024,896]{1,0:T(8,128)(2,1)S(1)} %multiply_convert_fusion.1, bf16[1024,2432]{1,0:T(8,128)(2,1)} %get-tuple-element.36), kind=kOutput, calls=%fused_computation.11 | convolution fusion | flops 4464918528 | bytes 11173888 | tf_op jit(solution)/shard_map/dot_general | solution.py:21
  342.2 8.9 %add_convert_fusion = bf16[1024,896]{1,0:T(8,128)(2,1)S(1)} fusion(f32[1024,896]{1,0:T(8,128)} %fusion.81, bf16[1024,2432]{1,0:T(8,128)(2,1)} %get-tuple-element.36, bf16[896,2432]{1,0:T(8,128)(2,1)S(1)} %bitcast.336), kind=kOutput, calls=%fused_computation.35 | convolution fusion | flops 4464574464 | bytes 14843904 | tf_op jit(solution)/shard_map/dot_general | solution.py:21
  351.1 10.4 %convolution_convert_fusion.4 = bf16[1024,896]{1,0:T(8,128)(2,1)} fusion(bf16[1024,2432]{1,0:T(8,128)(2,1)} %get-tuple-element.38, bf16[896,2432]{1,0:T(8,128)(2,1)} %bitcast.338), kind=kOutput, calls=%fused_computation.57 | convolution fusion | flops 4463656960 | bytes 11173888 | tf_op jit(solution)/shard_map/dot_general | solution.py:21
  366.3 9.3 %collective-permute-done.83 = bf16[2,112,2432]{2,1,0:T(8,128)(2,1)} collective-permute-done((bf16[2,112,2432]{2,1,0:T(8,128)(2,1)}, bf16[2,112,2432]{2,1,0:T(8,128)(2,1)}, u32[]{:S(2)}, u32[]{:S(2)}) %collective-permute-start.83) | collective-permute-done | bytes 1089568 | tf_op jit(solution)/shard_map/ppermute | solution.py:25
  380.8 15.3 %collective-permute-done.77 = bf16[2,112,2432]{2,1,0:T(8,128)(2,1)S(1)} collective-permute-done((bf16[2,112,2432]{2,1,0:T(8,128)(2,1)S(1)}, bf16[2,112,2432]{2,1,0:T(8,128)(2,1)S(1)}, u32[]{:S(2)}, u32[]{:S(2)}) %collective-permute-start.77) | collective-permute-done | bytes 1089568 | tf_op jit(solution)/shard_map/ppermute | solution.py:25
  397.6 3.6 collective-permute-done.75
  402.9 10.0 %collective-permute-done.90 = bf16[112,2432]{1,0:T(8,128)(2,1)S(1)} collective-permute-done((bf16[112,2432]{1,0:T(8,128)(2,1)S(1)}, bf16[112,2432]{1,0:T(8,128)(2,1)S(1)}, u32[]{:S(2)}, u32[]{:S(2)}) %collective-permute-start.90) | collective-permute-done | bytes 544800 | tf_op jit(solution)/shard_map/ppermute | solution.py:25
  416.0 8.6 %collective-permute-done.84 = bf16[112,2432]{1,0:T(8,128)(2,1)S(1)} collective-permute-done((bf16[112,2432]{1,0:T(8,128)(2,1)S(1)}, bf16[112,2432]{1,0:T(8,128)(2,1)S(1)}, u32[]{:S(2)}, u32[]{:S(2)}) %collective-permute-start.84) | collective-permute-done | bytes 544800 | tf_op jit(solution)/shard_map/ppermute | solution.py:25
  427.0 4.9 collective-permute-done.78
  431.9 2.0 collective-permute-done.76
  442.2 15.3 %shard_map.262 = (f32[448,512]{1,0:T(8,128)}, bf16[128,2048]{1,0:T(8,128)(2,1)}) custom-call(bf16[448,512]{1,0:T(8,128)(2,1)} %get-tuple-element.61.q_ref, bf16[448,512]{1,0:T(8,128)(2,1)} %convolution_convert_fusion.8.do_ref, bf16[448,512]{1,0:T(8,128)(2,1)} %get-tuple-element.23.out_ref, f32[2,7,1,256]{3,2,1,0:T(1,128)} %get-tuple-element.26.log_ref, ...), custom_call_target="tpu_custom_call" | custom-call | tf_op jit(solution)/shard_map/pallas_call | solution.py:217
  457.5 2.2 reshape.744
  465.6 15.5 %shard_map.261 = (f32[448,512]{1,0:T(8,128)}, bf16[128,2048]{1,0:T(8,128)(2,1)}) custom-call(bf16[448,512]{1,0:T(8,128)(2,1)} %get-tuple-element.60.q_ref, bf16[448,512]{1,0:T(8,128)(2,1)} %convolution_convert_fusion.9.do_ref, bf16[448,512]{1,0:T(8,128)(2,1)} %get-tuple-element.22.out_ref, f32[2,7,1,256]{3,2,1,0:T(1,128)} %get-tuple-element.24.log_ref, ...), custom_call_target="tpu_custom_call" | custom-call | tf_op jit(solution)/shard_map/pallas_call | solution.py:217
  481.1 2.2 reshape.742
  485.3 2.9 add_convert_fusion.2
  488.2 5.2 reshape.751
  493.4 2.2 fusion.71
  512.7 3.0 collective-permute-done.52
  515.6 9.6 %collective-permute-start.85 = (bf16[112,2432]{1,0:T(8,128)(2,1)S(1)}, bf16[112,2432]{1,0:T(8,128)(2,1)S(1)}, u32[]{:S(2)}, u32[]{:S(2)}) collective-permute-start(bf16[112,2432]{1,0:T(8,128)(2,1)S(1)} %copy-done.63), channel_id=1, source_target_pairs={{0,4},{2,6},{4,0},{6,2},{1,5},{3,7},{5,1},{7,3},{8,12},{10,14},{12... | collective-permute-start | bytes 1634312 | tf_op jit(solution)/shard_map/ppermute | solution.py:25
  525.2 14.9 %collective-permute-done.53 = bf16[128,2,256]{2,1,0:T(2,128)(2,1)S(1)} collective-permute-done((bf16[128,2,256]{2,1,0:T(2,128)(2,1)S(1)}, bf16[128,2,256]{2,1,0:T(2,128)(2,1)S(1)}, u32[]{:S(2)}, u32[]{:S(2)}) %collective-permute-start.53) | collective-permute-done | bytes 131104 | tf_op jit(solution)/shard_map/ppermute | solution.py:130
  544.0 2.2 collective-permute-done.67
  555.7 4.5 collective-permute-done.85
  560.7 9.4 %collective-permute-done.79 = bf16[112,2432]{1,0:T(8,128)(2,1)S(1)} collective-permute-done((bf16[112,2432]{1,0:T(8,128)(2,1)S(1)}, bf16[112,2432]{1,0:T(8,128)(2,1)S(1)}, u32[]{:S(2)}, u32[]{:S(2)}) %collective-permute-start.79) | collective-permute-done | bytes 544800 | tf_op jit(solution)/shard_map/ppermute | solution.py:25
  572.8 11.4 %collective-permute-done.70 = bf16[56,448]{1,0:T(8,128)(2,1)S(1)} collective-permute-done((bf16[56,448]{1,0:T(8,128)(2,1)S(1)}, bf16[56,448]{1,0:T(8,128)(2,1)S(1)}, u32[]{:S(2)}, u32[]{:S(2)}) %collective-permute-start.70) | collective-permute-done | bytes 50208 | tf_op jit(solution)/shard_map/ppermute | solution.py:25
  586.6 6.1 collective-permute-done.80
  593.5 2.8 fusion.14
  596.7 3.9 convolution_convert_fusion.5
  600.6 2.3 copy.56
  605.2 3.3 collective-permute-done.72
  609.8 2.5 collective-permute-done.73
  615.9 7.4 %fusion.12 = (f32[1024,896]{1,0:T(8,128)}, bf16[1024,896]{1,0:T(8,128)(2,1)}) fusion(bf16[2,2,256,896]{3,2,1,0:T(8,128)(2,1)S(1)} %copy-done.2, bf16[1024,896]{1,0:T(8,128)(2,1)} %copy-done.7, bf16[1024,896]{1,0:T(8,128)(2,1)} %copy-done.6, f32[1024]{0:T(1024)S(1)} %broadcast_multiply_fusion.1, f32[896]{0:T(1024)S(1)} %copy-done.91, f32[1024]{0:T(1024)S(1)} %bitcast.389, ...), kind=kLoop, calls=%fused_computation.24 | loop fusion | flops 22937600 | bytes 23878656 | tf_op jit(solution)/shard_map/add | solution.py:399
  625.5 4.3 collective-permute-done.63
  (503 shorter events, 177.1 us)
Async XLA Ops:
  1.5 20.5 %collective-permute-start.10 = (s32[4,256]{1,0:T(4,128)S(1)}, s32[4,256]{1,0:T(4,128)S(1)}, u32[]{:S(2)}, u32[]{:S(2)}) collective-permute-start(s32[4,256]{1,0:T(4,128)S(1)} %concatenate.91), channel_id=1, source_target_pairs={{0,6},{1,7},{8,14},{9,15},{16,22},{17,23},{24,30},{25,31}} | collective-permute-start | bytes 12296 | tf_op jit(solution)/shard_map/ppermute | solution.py:121
  8.4 13.7 %collective-permute-start.8 = (s32[4,256]{1,0:T(4,128)S(1)}, s32[4,256]{1,0:T(4,128)S(1)}, u32[]{:S(2)}, u32[]{:S(2)}) collective-permute-start(s32[4,256]{1,0:T(4,128)S(1)} %concatenate.91), channel_id=1, source_target_pairs={{0,2},{2,4},{4,6},{1,3},{3,5},{5,7},{8,10},{10,12},{12,14},{9,11},... | collective-permute-start | bytes 12296 | tf_op jit(solution)/shard_map/ppermute | solution.py:121
  9.7 14.3 %collective-permute-start.9 = (s32[4,256]{1,0:T(4,128)S(1)}, s32[4,256]{1,0:T(4,128)S(1)}, u32[]{:S(2)}, u32[]{:S(2)}) collective-permute-start(s32[4,256]{1,0:T(4,128)S(1)} %concatenate.91), channel_id=1, source_target_pairs={{0,4},{2,6},{1,5},{3,7},{8,12},{10,14},{9,13},{11,15},{16,20},{18,... | collective-permute-start | bytes 12296 | tf_op jit(solution)/shard_map/ppermute | solution.py:121
  13.2 14.2 %collective-permute-start = (bf16[56,576]{1,0:T(8,128)(2,1)S(1)}, bf16[56,576]{1,0:T(8,128)(2,1)S(1)}, u32[]{:S(2)}, u32[]{:S(2)}) collective-permute-start(bf16[56,576]{1,0:T(8,128)(2,1)S(1)} %pad_maximum_fusion.13), channel_id=1, source_target_pairs={{0,2},{2,0},{4,6},{6,4},{1,3},{3,1},{5,7},{7,5},{8,10},{10,8},{12,... | collective-permute-start | bytes 193544 | tf_op jit(solution)/shard_map/ppermute | solution.py:25
  13.3 15.1 %collective-permute-start.14 = (bf16[56,448]{1,0:T(8,128)(2,1)}, bf16[56,448]{1,0:T(8,128)(2,1)S(1)}, u32[]{:S(2)}, u32[]{:S(2)}) collective-permute-start(bf16[56,448]{1,0:T(8,128)(2,1)} %bitcast.387), channel_id=1, source_target_pairs={{0,2},{2,0},{4,6},{6,4},{1,3},{3,1},{5,7},{7,5},{8,10},{10,8},{12,... | collective-permute-start | bytes 150536 | tf_op jit(solution)/shard_map/ppermute | solution.py:25
  22.0 31.7 %collective-permute-start.26 = (bf16[56,2432]{1,0:T(8,128)(2,1)S(1)}, bf16[56,2432]{1,0:T(8,128)(2,1)S(1)}, u32[]{:S(2)}, u32[]{:S(2)}) collective-permute-start(bf16[56,2432]{1,0:T(8,128)(2,1)S(1)} %copy-done.68), channel_id=1, source_target_pairs={{0,2},{2,0},{4,6},{6,4},{1,3},{3,1},{5,7},{7,5},{8,10},{10,8},{12,... | collective-permute-start | bytes 817160 | tf_op jit(solution)/shard_map/ppermute | solution.py:25
  22.1 22.4 %collective-permute-start.34 = (bf16[56,2432]{1,0:T(8,128)(2,1)}, bf16[56,2432]{1,0:T(8,128)(2,1)}, u32[]{:S(2)}, u32[]{:S(2)}) collective-permute-start(bf16[56,2432]{1,0:T(8,128)(2,1)} %param.27), channel_id=1, source_target_pairs={{0,2},{2,0},{4,6},{6,4},{1,3},{3,1},{5,7},{7,5},{8,10},{10,8},{12,... | collective-permute-start | bytes 817160 | tf_op jit(solution)/shard_map/ppermute | solution.py:25
  24.1 22.4 %collective-permute-start.42 = (bf16[56,2432]{1,0:T(8,128)(2,1)S(1)}, bf16[56,2432]{1,0:T(8,128)(2,1)}, u32[]{:S(2)}, u32[]{:S(2)}) collective-permute-start(bf16[56,2432]{1,0:T(8,128)(2,1)S(1)} %bitcast.381), channel_id=1, source_target_pairs={{0,2},{2,0},{4,6},{6,4},{1,3},{3,1},{5,7},{7,5},{8,10},{10,8},{12,... | collective-permute-start | bytes 817160 | tf_op jit(solution)/shard_map/ppermute | solution.py:25
  28.2 14.8 %collective-permute-start.4 = (bf16[112,576]{1,0:T(8,128)(2,1)S(1)}, bf16[112,576]{1,0:T(8,128)(2,1)S(1)}, u32[]{:S(2)}, u32[]{:S(2)}) collective-permute-start(bf16[112,576]{1,0:T(8,128)(2,1)S(1)} %pad_maximum_fusion.8.refs_0_), channel_id=1, source_target_pairs={{0,4},{2,6},{4,0},{6,2},{1,5},{3,7},{5,1},{7,3},{8,12},{10,14},{12... | collective-permute-start | bytes 387080 | tf_op jit(solution)/shard_map/ppermute | solution.py:25
  28.4 21.8 %collective-permute-start.18 = (bf16[112,448]{1,0:T(8,128)(2,1)S(1)}, bf16[112,448]{1,0:T(8,128)(2,1)}, u32[]{:S(2)}, u32[]{:S(2)}) collective-permute-start(bf16[112,448]{1,0:T(8,128)(2,1)S(1)} %pad_maximum_fusion.12.refs_0_), channel_id=1, source_target_pairs={{0,4},{2,6},{4,0},{6,2},{1,5},{3,7},{5,1},{7,3},{8,12},{10,14},{12... | collective-permute-start | bytes 301064 | tf_op jit(solution)/shard_map/ppermute | solution.py:25
  56.9 19.7 %collective-permute-start.16 = (bf16[112,448]{1,0:T(8,128)(2,1)S(1)}, bf16[112,448]{1,0:T(8,128)(2,1)}, u32[]{:S(2)}, u32[]{:S(2)}) collective-permute-start(bf16[112,448]{1,0:T(8,128)(2,1)S(1)} %pad_maximum_fusion.12.refs_0_), channel_id=1, source_target_pairs={{0,16},{8,24},{16,0},{24,8},{1,17},{9,25},{17,1},{25,9},{2,18},{10... | collective-permute-start | bytes 301064 | tf_op jit(solution)/shard_map/ppermute | solution.py:25
  59.5 17.2 %collective-permute-start.19 = (bf16[112,448]{1,0:T(8,128)(2,1)}, bf16[112,448]{1,0:T(8,128)(2,1)}, u32[]{:S(2)}, u32[]{:S(2)}) collective-permute-start(bf16[112,448]{1,0:T(8,128)(2,1)} %collective-permute-done.18.refs_4_), channel_id=1, source_target_pairs={{0,8},{8,0},{16,24},{24,16},{1,9},{9,1},{17,25},{25,17},{2,10},{10... | collective-permute-start | bytes 301064 | tf_op jit(solution)/shard_map/ppermute | solution.py:25
  61.0 16.8 %collective-permute-start.17 = (bf16[112,448]{1,0:T(8,128)(2,1)}, bf16[112,448]{1,0:T(8,128)(2,1)}, u32[]{:S(2)}, u32[]{:S(2)}) collective-permute-start(bf16[112,448]{1,0:T(8,128)(2,1)} %collective-permute-done.15.refs_1_), channel_id=1, source_target_pairs={{0,16},{8,24},{16,0},{24,8},{1,17},{9,25},{17,1},{25,9},{2,18},{10... | collective-permute-start | bytes 301064 | tf_op jit(solution)/shard_map/ppermute | solution.py:25
  62.4 20.2 %collective-permute-start.21 = (bf16[112,448]{1,0:T(8,128)(2,1)}, bf16[112,448]{1,0:T(8,128)(2,1)}, u32[]{:S(2)}, u32[]{:S(2)}) collective-permute-start(bf16[112,448]{1,0:T(8,128)(2,1)} %collective-permute-done.20.refs_6_), channel_id=1, source_target_pairs={{0,8},{8,0},{16,24},{24,16},{1,9},{9,1},{17,25},{25,17},{2,10},{10... | collective-permute-start | bytes 301064 | tf_op jit(solution)/shard_map/ppermute | solution.py:25
  76.6 45.8 %collective-permute-start.30 = (bf16[112,2432]{1,0:T(8,128)(2,1)S(1)}, bf16[112,2432]{1,0:T(8,128)(2,1)S(1)}, u32[]{:S(2)}, u32[]{:S(2)}) collective-permute-start(bf16[112,2432]{1,0:T(8,128)(2,1)S(1)} %pad_maximum_fusion.3.refs_0_), channel_id=1, source_target_pairs={{0,4},{2,6},{4,0},{6,2},{1,5},{3,7},{5,1},{7,3},{8,12},{10,14},{12... | collective-permute-start | bytes 1634312 | tf_op jit(solution)/shard_map/ppermute | solution.py:25
  76.6 46.5 %collective-permute-start.27 = (bf16[112,2432]{1,0:T(8,128)(2,1)S(1)}, bf16[112,2432]{1,0:T(8,128)(2,1)S(1)}, u32[]{:S(2)}, u32[]{:S(2)}) collective-permute-start(bf16[112,2432]{1,0:T(8,128)(2,1)S(1)} %pad_maximum_fusion.3.refs_0_), channel_id=1, source_target_pairs={{0,8},{8,0},{16,24},{24,16},{1,9},{9,1},{17,25},{25,17},{2,10},{10... | collective-permute-start | bytes 1634312 | tf_op jit(solution)/shard_map/ppermute | solution.py:25
  77.7 14.3 %collective-permute-start.12 = (bf16[128,2,256]{2,1,0:T(2,128)(2,1)}, bf16[128,2,256]{2,1,0:T(2,128)(2,1)}, u32[]{:S(2)}, u32[]{:S(2)}) collective-permute-start(bf16[128,2,256]{2,1,0:T(2,128)(2,1)} %reshape.731), channel_id=1, source_target_pairs={{0,4},{2,6},{1,5},{3,7},{8,12},{10,14},{9,13},{11,15},{16,20},{18,... | collective-permute-start | bytes 393224 | tf_op jit(solution)/shard_map/ppermute | solution.py:121
  83.9 19.4 %collective-permute-start.22 = (bf16[128,2,256]{2,1,0:T(2,128)(2,1)}, bf16[128,2,256]{2,1,0:T(2,128)(2,1)S(1)}, u32[]{:S(2)}, u32[]{:S(2)}) collective-permute-start(bf16[128,2,256]{2,1,0:T(2,128)(2,1)} %reshape.734), channel_id=1, source_target_pairs={{0,2},{2,4},{4,6},{1,3},{3,5},{5,7},{8,10},{10,12},{12,14},{9,11},... | collective-permute-start | bytes 393224 | tf_op jit(solution)/shard_map/ppermute | solution.py:121
  92.1 34.4 %collective-permute-start.28 = (bf16[112,2432]{1,0:T(8,128)(2,1)S(1)}, bf16[112,2432]{1,0:T(8,128)(2,1)S(1)}, u32[]{:S(2)}, u32[]{:S(2)}) collective-permute-start(bf16[112,2432]{1,0:T(8,128)(2,1)S(1)} %pad_maximum_fusion.3.refs_0_), channel_id=1, source_target_pairs={{0,16},{8,24},{16,0},{24,8},{1,17},{9,25},{17,1},{25,9},{2,18},{10... | collective-permute-start | bytes 1634312 | tf_op jit(solution)/shard_map/ppermute | solution.py:25
  94.1 27.2 %collective-permute-start.23 = (bf16[128,2,256]{2,1,0:T(2,128)(2,1)}, bf16[128,2,256]{2,1,0:T(2,128)(2,1)S(1)}, u32[]{:S(2)}, u32[]{:S(2)}) collective-permute-start(bf16[128,2,256]{2,1,0:T(2,128)(2,1)} %reshape.734), channel_id=1, source_target_pairs={{0,4},{2,6},{1,5},{3,7},{8,12},{10,14},{9,13},{11,15},{16,20},{18,... | collective-permute-start | bytes 393224 | tf_op jit(solution)/shard_map/ppermute | solution.py:121
  103.4 18.0 %collective-permute-start.24 = (bf16[128,2,256]{2,1,0:T(2,128)(2,1)}, bf16[128,2,256]{2,1,0:T(2,128)(2,1)S(1)}, u32[]{:S(2)}, u32[]{:S(2)}) collective-permute-start(bf16[128,2,256]{2,1,0:T(2,128)(2,1)} %reshape.734), channel_id=1, source_target_pairs={{0,6},{1,7},{8,14},{9,15},{16,22},{17,23},{24,30},{25,31}} | collective-permute-start | bytes 393224 | tf_op jit(solution)/shard_map/ppermute | solution.py:121
  121.3 19.6 %collective-permute-start.38 = (bf16[112,2432]{1,0:T(8,128)(2,1)S(1)}, bf16[112,2432]{1,0:T(8,128)(2,1)S(1)}, u32[]{:S(2)}, u32[]{:S(2)}) collective-permute-start(bf16[112,2432]{1,0:T(8,128)(2,1)S(1)} %pad_maximum_fusion.4.refs_0_), channel_id=1, source_target_pairs={{0,4},{2,6},{4,0},{6,2},{1,5},{3,7},{5,1},{7,3},{8,12},{10,14},{12... | collective-permute-start | bytes 1634312 | tf_op jit(solution)/shard_map/ppermute | solution.py:25
  121.4 20.3 %collective-permute-start.35 = (bf16[112,2432]{1,0:T(8,128)(2,1)S(1)}, bf16[112,2432]{1,0:T(8,128)(2,1)S(1)}, u32[]{:S(2)}, u32[]{:S(2)}) collective-permute-start(bf16[112,2432]{1,0:T(8,128)(2,1)S(1)} %pad_maximum_fusion.4.refs_0_), channel_id=1, source_target_pairs={{0,8},{8,0},{16,24},{24,16},{1,9},{9,1},{17,25},{25,17},{2,10},{10... | collective-permute-start | bytes 1634312 | tf_op jit(solution)/shard_map/ppermute | solution.py:25
  122.4 20.2 %collective-permute-start.36 = (bf16[112,2432]{1,0:T(8,128)(2,1)S(1)}, bf16[112,2432]{1,0:T(8,128)(2,1)S(1)}, u32[]{:S(2)}, u32[]{:S(2)}) collective-permute-start(bf16[112,2432]{1,0:T(8,128)(2,1)S(1)} %pad_maximum_fusion.4.refs_0_), channel_id=1, source_target_pairs={{0,16},{8,24},{16,0},{24,8},{1,17},{9,25},{17,1},{25,9},{2,18},{10... | collective-permute-start | bytes 1634312 | tf_op jit(solution)/shard_map/ppermute | solution.py:25
  123.2 41.1 %collective-permute-start.46 = (bf16[112,2432]{1,0:T(8,128)(2,1)}, bf16[112,2432]{1,0:T(8,128)(2,1)}, u32[]{:S(2)}, u32[]{:S(2)}) collective-permute-start(bf16[112,2432]{1,0:T(8,128)(2,1)} %pad_maximum_fusion.5.refs_0_), channel_id=1, source_target_pairs={{0,4},{2,6},{4,0},{6,2},{1,5},{3,7},{5,1},{7,3},{8,12},{10,14},{12... | collective-permute-start | bytes 1634312 | tf_op jit(solution)/shard_map/ppermute | solution.py:25
  126.5 56.7 %collective-permute-start.43 = (bf16[112,2432]{1,0:T(8,128)(2,1)}, bf16[112,2432]{1,0:T(8,128)(2,1)S(1)}, u32[]{:S(2)}, u32[]{:S(2)}) collective-permute-start(bf16[112,2432]{1,0:T(8,128)(2,1)} %pad_maximum_fusion.5.refs_0_), channel_id=1, source_target_pairs={{0,8},{8,0},{16,24},{24,16},{1,9},{9,1},{17,25},{25,17},{2,10},{10... | collective-permute-start | bytes 1634312 | tf_op jit(solution)/shard_map/ppermute | solution.py:25
  140.9 59.2 %collective-permute-start.32 = (bf16[112,2432]{1,0:T(8,128)(2,1)S(1)}, bf16[112,2432]{1,0:T(8,128)(2,1)S(1)}, u32[]{:S(2)}, u32[]{:S(2)}) collective-permute-start(bf16[112,2432]{1,0:T(8,128)(2,1)S(1)} %collective-permute-done.30.refs_4_), channel_id=1, source_target_pairs={{0,16},{8,24},{16,0},{24,8},{1,17},{9,25},{17,1},{25,9},{2,18},{10... | collective-permute-start | bytes 1634312 | tf_op jit(solution)/shard_map/ppermute | solution.py:25
  141.7 59.7 %collective-permute-start.31 = (bf16[112,2432]{1,0:T(8,128)(2,1)S(1)}, bf16[112,2432]{1,0:T(8,128)(2,1)}, u32[]{:S(2)}, u32[]{:S(2)}) collective-permute-start(bf16[112,2432]{1,0:T(8,128)(2,1)S(1)} %collective-permute-done.30.refs_4_), channel_id=1, source_target_pairs={{0,8},{8,0},{16,24},{24,16},{1,9},{9,1},{17,25},{25,17},{2,10},{10... | collective-permute-start | bytes 1634312 | tf_op jit(solution)/shard_map/ppermute | solution.py:25
  142.5 59.7 %collective-permute-start.29 = (bf16[112,2432]{1,0:T(8,128)(2,1)S(1)}, bf16[112,2432]{1,0:T(8,128)(2,1)S(1)}, u32[]{:S(2)}, u32[]{:S(2)}) collective-permute-start(bf16[112,2432]{1,0:T(8,128)(2,1)S(1)} %collective-permute-done.27.refs_1_), channel_id=1, source_target_pairs={{0,16},{8,24},{16,0},{24,8},{1,17},{9,25},{17,1},{25,9},{2,18},{10... | collective-permute-start | bytes 1634312 | tf_op jit(solution)/shard_map/ppermute | solution.py:25
  164.3 39.2 %collective-permute-start.40 = (bf16[112,2432]{1,0:T(8,128)(2,1)S(1)}, bf16[112,2432]{1,0:T(8,128)(2,1)}, u32[]{:S(2)}, u32[]{:S(2)}) collective-permute-start(bf16[112,2432]{1,0:T(8,128)(2,1)S(1)} %collective-permute-done.38.refs_4_), channel_id=1, source_target_pairs={{0,16},{8,24},{16,0},{24,8},{1,17},{9,25},{17,1},{25,9},{2,18},{10... | collective-permute-start | bytes 1634312 | tf_op jit(solution)/shard_map/ppermute | solution.py:25
  183.2 25.2 %collective-permute-start.39 = (bf16[112,2432]{1,0:T(8,128)(2,1)S(1)}, bf16[112,2432]{1,0:T(8,128)(2,1)S(1)}, u32[]{:S(2)}, u32[]{:S(2)}) collective-permute-start(bf16[112,2432]{1,0:T(8,128)(2,1)S(1)} %collective-permute-done.38.refs_4_), channel_id=1, source_target_pairs={{0,8},{8,0},{16,24},{24,16},{1,9},{9,1},{17,25},{25,17},{2,10},{10... | collective-permute-start | bytes 1634312 | tf_op jit(solution)/shard_map/ppermute | solution.py:25
  200.1 15.4 %collective-permute-start.37 = (bf16[112,2432]{1,0:T(8,128)(2,1)S(1)}, bf16[112,2432]{1,0:T(8,128)(2,1)S(1)}, u32[]{:S(2)}, u32[]{:S(2)}) collective-permute-start(bf16[112,2432]{1,0:T(8,128)(2,1)S(1)} %collective-permute-done.35.refs_1_), channel_id=1, source_target_pairs={{0,16},{8,24},{16,0},{24,8},{1,17},{9,25},{17,1},{25,9},{2,18},{10... | collective-permute-start | bytes 1634312 | tf_op jit(solution)/shard_map/ppermute | solution.py:25
  201.4 25.9 %collective-permute-start.48 = (bf16[112,2432]{1,0:T(8,128)(2,1)}, bf16[112,2432]{1,0:T(8,128)(2,1)}, u32[]{:S(2)}, u32[]{:S(2)}) collective-permute-start(bf16[112,2432]{1,0:T(8,128)(2,1)} %collective-permute-done.46.refs_4_), channel_id=1, source_target_pairs={{0,16},{8,24},{16,0},{24,8},{1,17},{9,25},{17,1},{25,9},{2,18},{10... | collective-permute-start | bytes 1634312 | tf_op jit(solution)/shard_map/ppermute | solution.py:25
  202.2 26.3 %collective-permute-start.33 = (bf16[112,2432]{1,0:T(8,128)(2,1)S(1)}, bf16[112,2432]{1,0:T(8,128)(2,1)S(1)}, u32[]{:S(2)}, u32[]{:S(2)}) collective-permute-start(bf16[112,2432]{1,0:T(8,128)(2,1)S(1)} %collective-permute-done.32.refs_6_), channel_id=1, source_target_pairs={{0,8},{8,0},{16,24},{24,16},{1,9},{9,1},{17,25},{25,17},{2,10},{10... | collective-permute-start | bytes 1634312 | tf_op jit(solution)/shard_map/ppermute | solution.py:25
  203.5 26.4 %collective-permute-start.41 = (bf16[112,2432]{1,0:T(8,128)(2,1)}, bf16[112,2432]{1,0:T(8,128)(2,1)S(1)}, u32[]{:S(2)}, u32[]{:S(2)}) collective-permute-start(bf16[112,2432]{1,0:T(8,128)(2,1)} %collective-permute-done.40.refs_6_), channel_id=1, source_target_pairs={{0,8},{8,0},{16,24},{24,16},{1,9},{9,1},{17,25},{25,17},{2,10},{10... | collective-permute-start | bytes 1634312 | tf_op jit(solution)/shard_map/ppermute | solution.py:25
  208.4 57.5 %collective-permute-start.25 = (bf16[1024,896]{1,0:T(8,128)(2,1)}, bf16[1024,896]{1,0:T(8,128)(2,1)}, u32[]{:S(2)}, u32[]{:S(2)}) collective-permute-start(bf16[1024,896]{1,0:T(8,128)(2,1)} %pad_maximum_fusion), channel_id=1, source_target_pairs={{0,1},{1,0},{2,3},{3,2},{4,5},{5,4},{6,7},{7,6},{8,9},{9,8},{10,11... | collective-permute-start | bytes 5505032 | tf_op jit(solution)/shard_map/ppermute | solution.py:25
  215.5 25.8 %collective-permute-start.44 = (bf16[112,2432]{1,0:T(8,128)(2,1)}, bf16[112,2432]{1,0:T(8,128)(2,1)}, u32[]{:S(2)}, u32[]{:S(2)}) collective-permute-start(bf16[112,2432]{1,0:T(8,128)(2,1)} %pad_maximum_fusion.5.refs_0_), channel_id=1, source_target_pairs={{0,16},{8,24},{16,0},{24,8},{1,17},{9,25},{17,1},{25,9},{2,18},{10... | collective-permute-start | bytes 1634312 | tf_op jit(solution)/shard_map/ppermute | solution.py:25
  227.3 15.6 %collective-permute-start.47 = (bf16[112,2432]{1,0:T(8,128)(2,1)}, bf16[112,2432]{1,0:T(8,128)(2,1)}, u32[]{:S(2)}, u32[]{:S(2)}) collective-permute-start(bf16[112,2432]{1,0:T(8,128)(2,1)} %collective-permute-done.46.refs_4_), channel_id=1, source_target_pairs={{0,8},{8,0},{16,24},{24,16},{1,9},{9,1},{17,25},{25,17},{2,10},{10... | collective-permute-start | bytes 1634312 | tf_op jit(solution)/shard_map/ppermute | solution.py:25
  228.6 20.5 %collective-permute-start.45 = (bf16[112,2432]{1,0:T(8,128)(2,1)S(1)}, bf16[112,2432]{1,0:T(8,128)(2,1)}, u32[]{:S(2)}, u32[]{:S(2)}) collective-permute-start(bf16[112,2432]{1,0:T(8,128)(2,1)S(1)} %collective-permute-done.43.refs_1_), channel_id=1, source_target_pairs={{0,16},{8,24},{16,0},{24,8},{1,17},{9,25},{17,1},{25,9},{2,18},{10... | collective-permute-start | bytes 1634312 | tf_op jit(solution)/shard_map/ppermute | solution.py:25
  230.7 19.8 %collective-permute-start.49 = (bf16[112,2432]{1,0:T(8,128)(2,1)}, bf16[112,2432]{1,0:T(8,128)(2,1)}, u32[]{:S(2)}, u32[]{:S(2)}) collective-permute-start(bf16[112,2432]{1,0:T(8,128)(2,1)} %collective-permute-done.48.refs_6_), channel_id=1, source_target_pairs={{0,8},{8,0},{16,24},{24,16},{1,9},{9,1},{17,25},{25,17},{2,10},{10... | collective-permute-start | bytes 1634312 | tf_op jit(solution)/shard_map/ppermute | solution.py:25
  325.0 36.5 %collective-permute-start.89 = (bf16[2,112,2432]{2,1,0:T(8,128)(2,1)}, bf16[2,112,2432]{2,1,0:T(8,128)(2,1)}, u32[]{:S(2)}, u32[]{:S(2)}) collective-permute-start(bf16[2,112,2432]{2,1,0:T(8,128)(2,1)} %dynamic-slice_bitcast_fusion), channel_id=1, source_target_pairs={{0,8},{8,0},{16,24},{24,16},{1,9},{9,1},{17,25},{25,17},{2,10},{10... | collective-permute-start | bytes 3268616 | tf_op jit(solution)/shard_map/ppermute | solution.py:25
  327.3 37.1 %collective-permute-start.87 = (bf16[2,112,2432]{2,1,0:T(8,128)(2,1)}, bf16[2,112,2432]{2,1,0:T(8,128)(2,1)}, u32[]{:S(2)}, u32[]{:S(2)}) collective-permute-start(bf16[2,112,2432]{2,1,0:T(8,128)(2,1)} %dynamic-slice_bitcast_fusion.1), channel_id=1, source_target_pairs={{0,16},{8,24},{16,0},{24,8},{1,17},{9,25},{17,1},{25,9},{2,18},{10... | collective-permute-start | bytes 3268616 | tf_op jit(solution)/shard_map/ppermute | solution.py:25
  330.0 45.7 %collective-permute-start.83 = (bf16[2,112,2432]{2,1,0:T(8,128)(2,1)}, bf16[2,112,2432]{2,1,0:T(8,128)(2,1)}, u32[]{:S(2)}, u32[]{:S(2)}) collective-permute-start(bf16[2,112,2432]{2,1,0:T(8,128)(2,1)} %dynamic-slice_bitcast_fusion.2), channel_id=1, source_target_pairs={{0,8},{8,0},{16,24},{24,16},{1,9},{9,1},{17,25},{25,17},{2,10},{10... | collective-permute-start | bytes 3268616 | tf_op jit(solution)/shard_map/ppermute | solution.py:25
  331.7 46.2 %collective-permute-start.81 = (bf16[2,112,2432]{2,1,0:T(8,128)(2,1)}, bf16[2,112,2432]{2,1,0:T(8,128)(2,1)}, u32[]{:S(2)}, u32[]{:S(2)}) collective-permute-start(bf16[2,112,2432]{2,1,0:T(8,128)(2,1)} %dynamic-slice_bitcast_fusion.3), channel_id=1, source_target_pairs={{0,16},{8,24},{16,0},{24,8},{1,17},{9,25},{17,1},{25,9},{2,18},{10... | collective-permute-start | bytes 3268616 | tf_op jit(solution)/shard_map/ppermute | solution.py:25
  340.4 55.7 %collective-permute-start.77 = (bf16[2,112,2432]{2,1,0:T(8,128)(2,1)S(1)}, bf16[2,112,2432]{2,1,0:T(8,128)(2,1)S(1)}, u32[]{:S(2)}, u32[]{:S(2)}) collective-permute-start(bf16[2,112,2432]{2,1,0:T(8,128)(2,1)S(1)} %dynamic-slice_bitcast_fusion.4), channel_id=1, source_target_pairs={{0,8},{8,0},{16,24},{24,16},{1,9},{9,1},{17,25},{25,17},{2,10},{10... | collective-permute-start | bytes 3268616 | tf_op jit(solution)/shard_map/ppermute | solution.py:25
  361.6 39.6 %collective-permute-start.75 = (bf16[2,112,2432]{2,1,0:T(8,128)(2,1)S(1)}, bf16[2,112,2432]{2,1,0:T(8,128)(2,1)S(1)}, u32[]{:S(2)}, u32[]{:S(2)}) collective-permute-start(bf16[2,112,2432]{2,1,0:T(8,128)(2,1)S(1)} %dynamic-slice_bitcast_fusion.5), channel_id=1, source_target_pairs={{0,16},{8,24},{16,0},{24,8},{1,17},{9,25},{17,1},{25,9},{2,18},{10... | collective-permute-start | bytes 3268616 | tf_op jit(solution)/shard_map/ppermute | solution.py:25
  364.4 70.7 %collective-permute-start.51 = (bf16[1024,896]{1,0:T(8,128)(2,1)S(1)}, bf16[1024,896]{1,0:T(8,128)(2,1)S(1)}, u32[]{:S(2)}, u32[]{:S(2)}) collective-permute-start(bf16[1024,896]{1,0:T(8,128)(2,1)S(1)} %add_convert_fusion), channel_id=1, source_target_pairs={{0,1},{1,0},{2,3},{3,2},{4,5},{5,4},{6,7},{7,6},{8,9},{9,8},{10,11... | collective-permute-start | bytes 5505032 | tf_op jit(solution)/shard_map/ppermute | solution.py:25
  375.7 240.2 %collective-permute-start.50 = (bf16[1024,896]{1,0:T(8,128)(2,1)}, bf16[1024,896]{1,0:T(8,128)(2,1)}, u32[]{:S(2)}, u32[]{:S(2)}) collective-permute-start(bf16[1024,896]{1,0:T(8,128)(2,1)} %convolution_convert_fusion.4), channel_id=1, source_target_pairs={{0,1},{1,0},{2,3},{3,2},{4,5},{5,4},{6,7},{7,6},{8,9},{9,8},{10,11... | collective-permute-start | bytes 5505032 | tf_op jit(solution)/shard_map/ppermute | solution.py:25
  378.0 34.9 %collective-permute-start.90 = (bf16[112,2432]{1,0:T(8,128)(2,1)S(1)}, bf16[112,2432]{1,0:T(8,128)(2,1)S(1)}, u32[]{:S(2)}, u32[]{:S(2)}) collective-permute-start(bf16[112,2432]{1,0:T(8,128)(2,1)S(1)} %dynamic-slice_bitcast_fusion.6), channel_id=1, source_target_pairs={{0,16},{8,24},{16,0},{24,8},{1,17},{9,25},{17,1},{25,9},{2,18},{10... | collective-permute-start | bytes 1634312 | tf_op jit(solution)/shard_map/ppermute | solution.py:25
  396.1 17.5 %collective-permute-start.88 = (bf16[112,2432]{1,0:T(8,128)(2,1)S(1)}, bf16[112,2432]{1,0:T(8,128)(2,1)S(1)}, u32[]{:S(2)}, u32[]{:S(2)}) collective-permute-start(bf16[112,2432]{1,0:T(8,128)(2,1)S(1)} %dynamic-slice_bitcast_fusion.7), channel_id=1, source_target_pairs={{0,8},{8,0},{16,24},{24,16},{1,9},{9,1},{17,25},{25,17},{2,10},{10... | collective-permute-start | bytes 1634312 | tf_op jit(solution)/shard_map/ppermute | solution.py:25
  401.2 23.3 %collective-permute-start.84 = (bf16[112,2432]{1,0:T(8,128)(2,1)S(1)}, bf16[112,2432]{1,0:T(8,128)(2,1)S(1)}, u32[]{:S(2)}, u32[]{:S(2)}) collective-permute-start(bf16[112,2432]{1,0:T(8,128)(2,1)S(1)} %dynamic-slice_bitcast_fusion.8), channel_id=1, source_target_pairs={{0,16},{8,24},{16,0},{24,8},{1,17},{9,25},{17,1},{25,9},{2,18},{10... | collective-permute-start | bytes 1634312 | tf_op jit(solution)/shard_map/ppermute | solution.py:25
  413.7 18.3 %collective-permute-start.78 = (bf16[112,2432]{1,0:T(8,128)(2,1)S(1)}, bf16[112,2432]{1,0:T(8,128)(2,1)S(1)}, u32[]{:S(2)}, u32[]{:S(2)}) collective-permute-start(bf16[112,2432]{1,0:T(8,128)(2,1)S(1)} %dynamic-slice_bitcast_fusion.10), channel_id=1, source_target_pairs={{0,16},{8,24},{16,0},{24,8},{1,17},{9,25},{17,1},{25,9},{2,18},{10... | collective-permute-start | bytes 1634312 | tf_op jit(solution)/shard_map/ppermute | solution.py:25
  425.8 126.8 %collective-permute-start.91 = (bf16[112,2432]{1,0:T(8,128)(2,1)}, bf16[112,2432]{1,0:T(8,128)(2,1)}, u32[]{:S(2)}, u32[]{:S(2)}) collective-permute-start(bf16[112,2432]{1,0:T(8,128)(2,1)} %broadcast_select_fusion), channel_id=1, source_target_pairs={{0,4},{2,6},{4,0},{6,2},{1,5},{3,7},{5,1},{7,3},{8,12},{10,14},{12... | collective-permute-start | bytes 1634312 | tf_op jit(solution)/shard_map/ppermute | solution.py:25
  461.7 45.0 %collective-permute-start.55 = (bf16[128,2,256]{2,1,0:T(2,128)(2,1)}, bf16[128,2,256]{2,1,0:T(2,128)(2,1)}, u32[]{:S(2)}, u32[]{:S(2)}) collective-permute-start(bf16[128,2,256]{2,1,0:T(2,128)(2,1)} %get-tuple-element.68), channel_id=1, source_target_pairs={{2,0},{4,2},{6,4},{3,1},{5,3},{7,5},{10,8},{12,10},{14,12},{11,9},... | collective-permute-start | bytes 393224 | tf_op jit(solution)/shard_map/ppermute | solution.py:130
  463.0 45.4 %collective-permute-start.56 = (bf16[128,2,256]{2,1,0:T(2,128)(2,1)}, bf16[128,2,256]{2,1,0:T(2,128)(2,1)}, u32[]{:S(2)}, u32[]{:S(2)}) collective-permute-start(bf16[128,2,256]{2,1,0:T(2,128)(2,1)} %get-tuple-element.70), channel_id=1, source_target_pairs={{4,0},{6,2},{5,1},{7,3},{12,8},{14,10},{13,9},{15,11},{20,16},{22,... | collective-permute-start | bytes 393224 | tf_op jit(solution)/shard_map/ppermute | solution.py:130
  464.3 45.4 %collective-permute-start.57 = (bf16[128,2,256]{2,1,0:T(2,128)(2,1)}, bf16[128,2,256]{2,1,0:T(2,128)(2,1)}, u32[]{:S(2)}, u32[]{:S(2)}) collective-permute-start(bf16[128,2,256]{2,1,0:T(2,128)(2,1)} %get-tuple-element.69), channel_id=1, source_target_pairs={{6,0},{7,1},{14,8},{15,9},{22,16},{23,17},{30,24},{31,25}} | collective-permute-start | bytes 393224 | tf_op jit(solution)/shard_map/ppermute | solution.py:130
  508.4 31.7 %collective-permute-start.53 = (bf16[128,2,256]{2,1,0:T(2,128)(2,1)S(1)}, bf16[128,2,256]{2,1,0:T(2,128)(2,1)S(1)}, u32[]{:S(2)}, u32[]{:S(2)}) collective-permute-start(bf16[128,2,256]{2,1,0:T(2,128)(2,1)S(1)} %copy-done.81), channel_id=1, source_target_pairs={{4,0},{6,2},{5,1},{7,3},{12,8},{14,10},{13,9},{15,11},{20,16},{22,... | collective-permute-start | bytes 393224 | tf_op jit(solution)/shard_map/ppermute | solution.py:130
  509.7 31.2 %collective-permute-start.54 = (bf16[128,2,256]{2,1,0:T(2,128)(2,1)S(1)}, bf16[128,2,256]{2,1,0:T(2,128)(2,1)S(1)}, u32[]{:S(2)}, u32[]{:S(2)}) collective-permute-start(bf16[128,2,256]{2,1,0:T(2,128)(2,1)S(1)} %copy-done.80), channel_id=1, source_target_pairs={{6,0},{7,1},{14,8},{15,9},{22,16},{23,17},{30,24},{31,25}} | collective-permute-start | bytes 393224 | tf_op jit(solution)/shard_map/ppermute | solution.py:130
  515.6 44.6 %collective-permute-start.85 = (bf16[112,2432]{1,0:T(8,128)(2,1)S(1)}, bf16[112,2432]{1,0:T(8,128)(2,1)S(1)}, u32[]{:S(2)}, u32[]{:S(2)}) collective-permute-start(bf16[112,2432]{1,0:T(8,128)(2,1)S(1)} %copy-done.63), channel_id=1, source_target_pairs={{0,4},{2,6},{4,0},{6,2},{1,5},{3,7},{5,1},{7,3},{8,12},{10,14},{12... | collective-permute-start | bytes 1634312 | tf_op jit(solution)/shard_map/ppermute | solution.py:25
  551.1 19.0 %collective-permute-start.79 = (bf16[112,2432]{1,0:T(8,128)(2,1)S(1)}, bf16[112,2432]{1,0:T(8,128)(2,1)S(1)}, u32[]{:S(2)}, u32[]{:S(2)}) collective-permute-start(bf16[112,2432]{1,0:T(8,128)(2,1)S(1)} %copy-done.62), channel_id=1, source_target_pairs={{0,4},{2,6},{4,0},{6,2},{1,5},{3,7},{5,1},{7,3},{8,12},{10,14},{12... | collective-permute-start | bytes 1634312 | tf_op jit(solution)/shard_map/ppermute | solution.py:25
  552.6 40.9 %collective-permute-start.58 = (bf16[1024,896]{1,0:T(8,128)(2,1)S(1)}, bf16[1024,896]{1,0:T(8,128)(2,1)S(1)}, u32[]{:S(2)}, u32[]{:S(2)}) collective-permute-start(bf16[1024,896]{1,0:T(8,128)(2,1)S(1)} %convolution_convert_fusion.3), channel_id=1, source_target_pairs={{0,1},{1,0},{2,3},{3,2},{4,5},{5,4},{6,7},{7,6},{8,9},{9,8},{10,11... | collective-permute-start | bytes 5505032 | tf_op jit(solution)/shard_map/ppermute | solution.py:25
  552.6 18.7 %collective-permute-start.69 = (bf16[112,448]{1,0:T(8,128)(2,1)S(1)}, bf16[112,448]{1,0:T(8,128)(2,1)S(1)}, u32[]{:S(2)}, u32[]{:S(2)}) collective-permute-start(bf16[112,448]{1,0:T(8,128)(2,1)S(1)} %broadcast_select_fusion.10), channel_id=1, source_target_pairs={{0,4},{2,6},{4,0},{6,2},{1,5},{3,7},{5,1},{7,3},{8,12},{10,14},{12... | collective-permute-start | bytes 301064 | tf_op jit(solution)/shard_map/ppermute | solution.py:25
  560.2 24.6 %collective-permute-start.92 = (bf16[56,2432]{1,0:T(8,128)(2,1)S(1)}, bf16[56,2432]{1,0:T(8,128)(2,1)S(1)}, u32[]{:S(2)}, u32[]{:S(2)}) collective-permute-start(bf16[56,2432]{1,0:T(8,128)(2,1)S(1)} %dynamic-slice_bitcast_fusion.14), channel_id=1, source_target_pairs={{0,2},{2,0},{4,6},{6,4},{1,3},{3,1},{5,7},{7,5},{8,10},{10,8},{12,... | collective-permute-start | bytes 817160 | tf_op jit(solution)/shard_map/ppermute | solution.py:25
  570.1 15.6 %collective-permute-start.86 = (bf16[56,2432]{1,0:T(8,128)(2,1)S(1)}, bf16[56,2432]{1,0:T(8,128)(2,1)S(1)}, u32[]{:S(2)}, u32[]{:S(2)}) collective-permute-start(bf16[56,2432]{1,0:T(8,128)(2,1)S(1)} %dynamic-slice_bitcast_fusion.15), channel_id=1, source_target_pairs={{0,2},{2,0},{4,6},{6,4},{1,3},{3,1},{5,7},{7,5},{8,10},{10,8},{12,... | collective-permute-start | bytes 817160 | tf_op jit(solution)/shard_map/ppermute | solution.py:25
  (129 other events, 2101.8 us)

commit v2 on v1

v2 whole, which is shorter than its diff:
```python
import functools

import jax
import jax.numpy as jnp
from jax import lax
from jax.experimental import pallas as pl
from jax.experimental.pallas import tpu as pltpu
from jax.sharding import PartitionSpec as P

HEAD = 64

eps = 1e-06
theta = 1000000.0
masked = -1e30
f32 = jnp.float32
bf16 = jnp.bfloat16
VMEM_LIMIT = 56 * 1024 * 1024


def contract(left, right, dims):
    return lax.dot_general(left, right, ((dims[:1], dims[1:]), ((), ())), preferred_element_type=f32)


def swap(value, axis, size, bit):
    return lax.ppermute(value, axis, [(i, i ^ bit) for i in range(size)])


def tensor_sum(partial, size):
    sent = partial.astype(bf16)
    if size == 2:
        return sent.astype(f32) + swap(sent, "tensor", 2, 1).astype(f32)
    return lax.psum(sent, "tensor").astype(f32)


def pair_of(dp, ctx):
    return dp * 2 + ctx // 2


def hold(value, held, names):
    names = [name for name in names if name in held]
    value, *got = lax.optimization_barrier((value,) + tuple(held[name] for name in names))
    held.update(zip(names, got))
    return value


def gather_whole(shard):
    return lax.all_gather(shard, ("dp", "ctx"), axis=0, tiled=True)


def scatter_whole(total):
    return lax.psum_scatter(total, ("dp", "ctx"), scatter_dimension=0, tiled=True).astype(f32)


def gather_begin(shard):
    held = {"z%d" % k: swap(shard, "ctx", 4, k) for k in (1, 2, 3)}
    held["own"] = shard
    return held


BLOCKS = ("near", "near1", "near2", "near3", "far", "far1", "far2", "far3")


def gather_next(held, *names):
    def in_order(one, two):
        even = lax.axis_index("ctx") % 2 == 0
        return jnp.concatenate([jnp.where(even, one, two), jnp.where(even, two, one)], axis=0)

    for name in names:
        if name in held:
            continue
        if name == "near":
            held[name] = in_order(held["own"], held["z1"])
        elif name == "far":
            held[name] = in_order(held["z2"], held["z3"])
        else:
            source, bit = {
                "near1": ("near", 1),
                "near2": ("near", 2),
                "near3": ("near1", 2),
                "far1": ("far", 1),
                "far2": ("far", 2),
                "far3": ("far2", 1),
            }[name]
            held[name] = swap(held[source], "dp", 4, bit)


def gather_end(held):
    gather_next(held, *BLOCKS)
    return [held[name] for name in BLOCKS]


def gathered_spots():
    me = pair_of(lax.axis_index("dp"), lax.axis_index("ctx"))
    return jnp.stack([me ^ (k * 2 + h) for h in (0, 1) for k in (0, 1, 2, 3)]).astype(jnp.int32)


def kept_spots():
    me = pair_of(lax.axis_index("dp"), lax.axis_index("ctx"))
    order = (0, 2, 4, 6, 1, 5, 3, 7)
    return jnp.stack([me ^ r for r in order]).astype(jnp.int32)


def place_kernel(where_ref, *refs):
    count = len(refs) - 2
    pieces, out_ref, sems = refs[:count], refs[count], refs[count + 1]
    copies = [
        pltpu.make_async_copy(pieces[i], out_ref.at[where_ref[i]], sems.at[i]) for i in range(count)
    ]
    for copy in copies:
        copy.start()
    for copy in copies:
        copy.wait()


def place(pieces, where):
    count = len(pieces)
    whole = pl.pallas_call(
        place_kernel,
        out_shape=jax.ShapeDtypeStruct((count,) + pieces[0].shape, pieces[0].dtype),
        in_specs=[pl.BlockSpec(memory_space=pltpu.SMEM)] + [pl.BlockSpec(memory_space=pl.ANY)] * count,
        out_specs=pl.BlockSpec(memory_space=pltpu.VMEM),
        scratch_shapes=[pltpu.SemaphoreType.DMA((count,))],
        compiler_params=pltpu.CompilerParams(vmem_limit_bytes=VMEM_LIMIT),
    )(where, *pieces)
    return whole.reshape(count * pieces[0].shape[0], pieces[0].shape[1])


def add16(left, right):
    return (left.astype(f32) + right.astype(f32)).astype(bf16)


def scatter_begin(parts):
    keep_a, send_a, keep_b, send_b = parts
    return {"keep": (keep_a, keep_b), "a1": swap(send_a, "dp", 4, 2), "b1": swap(send_b, "dp", 4, 1)}


def scatter_second(held):
    keep_a, keep_b = held["keep"]
    a, b = held["a1"], held["b1"]
    held["a2"] = swap(add16(keep_a[1], a[1]), "dp", 4, 1)
    held["b2"] = swap(add16(keep_b[1], b[1]), "dp", 4, 2)
    held["left"] = add16(keep_a[0], a[0]), add16(keep_b[0], b[0])


def scatter_third(held):
    left_a, left_b = held["left"]
    near, far = add16(left_a, held["a2"]), add16(left_b, held["b2"])
    odd = lax.axis_index("ctx") % 2

    def half_of(value, at):
        rows = value.shape[0] // 2
        return lax.dynamic_slice_in_dim(value, at * rows, rows, 0)

    held["mine"] = half_of(near, odd)
    held["c1"] = swap(half_of(near, 1 - odd), "ctx", 4, 1)
    held["c2"] = swap(half_of(far, odd), "ctx", 4, 2)
    held["c3"] = swap(half_of(far, 1 - odd), "ctx", 4, 3)


def scatter_end(held):
    if "a2" not in held:
        scatter_second(held)
    if "c1" not in held:
        scatter_third(held)
    total = held["mine"].astype(f32)
    for name in ("c1", "c2", "c3"):
        total = total + held[name].astype(f32)
    return total


def in_parts(total):
    cut, spots = total.astype(bf16).reshape(8, -1, total.shape[1]), kept_spots()
    block = [lax.dynamic_index_in_dim(cut, spots[i], 0) for i in range(8)]
    return [jnp.concatenate(block[2 * i : 2 * i + 2]) for i in range(4)]


def sum_small(value, fast):
    if not fast:
        return lax.psum(value, ("dp", "ctx"))
    for axis, bit in (("ctx", 1), ("ctx", 2), ("dp", 1), ("dp", 2)):
        value = value + swap(value, axis, 4, bit)
    return value


def earlier(value, ctx_size):
    return [value] + [
        lax.ppermute(value, "ctx", [(i, i + back) for i in range(ctx_size - back)])
        for back in range(1, ctx_size)
    ]


def give_back(blocks, ctx_size):
    total = blocks[0].astype(f32)
    for back in range(1, ctx_size):
        total = total + lax.ppermute(
            blocks[back], "ctx", [(i + back, i) for i in range(ctx_size - back)]
        ).astype(f32)
    return total


def units_kernel(counts, parts, has_base, outs, where, spots, x_ref, dy_ref, xt_ref, dyt_ref, *refs):
    pieces, refs = refs[: sum(parts)], refs[sum(parts) :]
    if has_base:
        base, refs = refs[:2], refs[2:]
    out_ref, dn_ref, *refs = refs
    grads, refs = refs[:outs], refs[outs:]
    if has_base:
        (acc_out, acc_dn), refs = refs[:2], refs[2:]
    else:
        acc_out, acc_dn = out_ref, dn_ref
    weights, xt, dyt, sems = refs
    count = sum(counts)
    moves = []
    for i in range(8):
        moves.append((xt_ref.at[spots[i]], xt.at[i]))
        moves.append((dyt_ref.at[spots[i]], dyt.at[i]))
    taken, begin = 0, 0
    for part, units in zip(parts, counts):
        for m in range(3):
            there, here = pl.ds(m * units, units), pl.ds(m * count + begin, units)
            for i in range(part):
                if part == 1:
                    moves.append((pieces[taken].at[:, :, there], weights.at[:, :, here]))
                else:
                    moves.append((pieces[taken + i].at[:, there], weights.at[where[i], :, here]))
        taken, begin = taken + part, begin + units
    copies = [pltpu.make_async_copy(a, b, sems.at[i]) for i, (a, b) in enumerate(moves)]
    for copy in copies:
        copy.start()
    if has_base:
        acc_out[...] = base[0][...]
        acc_dn[...] = base[1][...]
    else:
        acc_out[...] = jnp.zeros_like(acc_out)
        acc_dn[...] = jnp.zeros_like(acc_dn)
    for copy in copies:
        copy.wait()
    depth = x_ref.shape[1]

    def weight(m, start, size):
        return weights[:, :, pl.ds(m * count + start, size)].reshape(depth, size)

    def some_units(start, size):
        w_gate, w_up, w_down = (weight(m, start, size) for m in range(3))
        gate = jnp.dot(x_ref[...], w_gate, preferred_element_type=f32)
        up = jnp.dot(x_ref[...], w_up, preferred_element_type=f32)
        d_hidden = jnp.dot(dy_ref[...], w_down, preferred_element_type=f32)
        sigma = jax.nn.sigmoid(gate)
        silu = gate * sigma
        hidden = (silu * up).astype(bf16)
        d_gate = (d_hidden * up * (sigma * (1.0 + gate * (1.0 - sigma)))).astype(bf16)
        d_up = (d_hidden * silu).astype(bf16)
        acc_out[...] += contract(hidden, w_down, (1, 1))
        acc_dn[...] += contract(d_gate, w_gate, (1, 1)) + contract(d_up, w_up, (1, 1))
        for m, (left, right) in enumerate(((xt, d_gate), (xt, d_up), (dyt, hidden))):
            grad = jnp.dot(
                left[...].reshape(depth, left.shape[2]), right, preferred_element_type=f32
            ).astype(bf16).reshape(8, depth // 8, size)
            for i, grad_ref in enumerate(grads):
                each = 8 // outs
                grad_ref[:, :, pl.ds(m * count + start, size)] = grad[each * i : each * i + each]

    wide = UNIT_TILE
    full = count // wide

    @pl.loop(0, full)
    def _(step):
        some_units(pl.multiple_of(step * wide, 128), wide)

    if count % wide:
        some_units(full * wide, count % wide)
    if has_base:
        out_ref[...] = acc_out[...].astype(out_ref.dtype)
        dn_ref[...] = acc_dn[...].astype(dn_ref.dtype)


UNIT_TILE = 256
SHARES = (8,)


def some_units(packs, where, spots, x, dy, xt, dyt, base, outs):
    tokens, depth = x.shape
    rows = depth // 8
    counts = [pack[0].shape[-1] // 3 for pack in packs]
    parts = [len(pack) for pack in packs]
    pieces = [piece for pack in packs for piece in pack]
    wide = 3 * sum(counts)
    whole = pl.BlockSpec(memory_space=pltpu.VMEM)
    smem = pl.BlockSpec(memory_space=pltpu.SMEM)
    anywhere = pl.BlockSpec(memory_space=pl.ANY)
    has_base = base is not None
    sums = jax.ShapeDtypeStruct((tokens, depth), bf16 if has_base else f32)
    grad = jax.ShapeDtypeStruct((8 // outs, rows, wide), bf16)
    scratch = [pltpu.VMEM((tokens, depth), f32)] * 2 if has_base else []
    return pl.pallas_call(
        functools.partial(units_kernel, counts, parts, has_base, outs),
        out_shape=[sums, sums] + [grad] * outs,
        in_specs=[smem, smem, whole, whole] + [anywhere] * (2 + len(pieces)) + ([whole] * 2 if has_base else []),
        out_specs=[whole] * (2 + outs),
        scratch_shapes=scratch
        + [
            pltpu.VMEM((8, rows, wide), bf16),
            pltpu.VMEM((8, rows, tokens), bf16),
            pltpu.VMEM((8, rows, tokens), bf16),
            pltpu.SemaphoreType.DMA((16 + 3 * len(pieces),)),
        ],
        compiler_params=pltpu.CompilerParams(vmem_limit_bytes=VMEM_LIMIT),
    )(where, spots, x, dy, xt, dyt, *pieces, *(base or ()))


def set_up(keys, queries, bias):
    info = keys[0].T
    allowed = (info[:, 0:1] == queries[0, 0:1]) & (info[:, 1:2] <= queries[0, 1:2])
    bias[...] = jnp.where(allowed, 0.0, masked)


def turned(value):
    return value.astype(f32).T.astype(bf16)


def forward_kernel(count, q_ref, keys, queries, *refs):
    kv_refs, (out_ref, log_ref, bias, key, pair) = refs[:count], refs[count:]

    @pl.when(pl.program_id(1) == 0)
    def _():
        set_up(keys, queries, bias)
        wide = kv_refs[0].shape[1]
        for i, kv_ref in enumerate(kv_refs):
            pair[:, i * wide : (i + 1) * wide] = kv_ref[...]
            key[i * wide : (i + 1) * wide, :] = turned(kv_ref[:HEAD, :])

    scores = jnp.dot(key[...], q_ref[...], preferred_element_type=f32) + bias[...]
    top = jnp.max(scores, axis=0, keepdims=True)
    weights = jnp.exp(scores - top)
    total = jnp.sum(weights, axis=0, keepdims=True)
    summed = jnp.dot(pair[HEAD:, :], weights.astype(bf16), preferred_element_type=f32)
    out_ref[...] = (summed / total).astype(bf16)
    log_ref[0, 0] = top + jnp.log(total)


def backward_kernel(count, q_ref, do_ref, out_ref, log_ref, keys, queries, *refs):
    kv_refs, dq_ref, dkv_refs = refs[:count], refs[count], refs[count + 1 : 2 * count + 1]
    bias, key, val, pair, acc = refs[2 * count + 1 :]
    head = pl.program_id(1)
    wide = kv_refs[0].shape[1]

    @pl.when(head == 0)
    def _():
        set_up(keys, queries, bias)
        for i, kv_ref in enumerate(kv_refs):
            pair[:, i * wide : (i + 1) * wide] = kv_ref[...]
            key[i * wide : (i + 1) * wide, :] = turned(kv_ref[:HEAD, :])
            val[i * wide : (i + 1) * wide, :] = turned(kv_ref[HEAD:, :])
        acc[...] = jnp.zeros_like(acc)

    query, grad = q_ref[...], do_ref[...]
    scores = jnp.dot(key[...], query, preferred_element_type=f32) + bias[...]
    prob = jnp.exp(scores - log_ref[0, 0])
    delta = jnp.sum(grad.astype(f32) * out_ref[...].astype(f32), axis=0, keepdims=True)
    grad_prob = jnp.dot(val[...], grad, preferred_element_type=f32)
    grad_score = (prob * (grad_prob - delta)).astype(bf16)
    dq_ref[...] = jnp.dot(pair[:HEAD, :], grad_score, preferred_element_type=f32)
    acc[:HEAD, :] += contract(query, grad_score, (1, 1))
    acc[HEAD:, :] += contract(grad, prob.astype(bf16), (1, 1))

    @pl.when(head == pl.num_programs(1) - 1)
    def _():
        for i, dkv_ref in enumerate(dkv_refs):
            dkv_ref[...] = acc[:, i * wide : (i + 1) * wide].astype(bf16)


def attention_specs(stretch, wide, length):
    head_block = pl.BlockSpec((HEAD, stretch), lambda s, h: (h, s))
    log_block = pl.BlockSpec((1, 1, 1, stretch), lambda s, h: (s, h, 0, 0))
    kv_block = pl.BlockSpec((2 * HEAD, wide), lambda s, h: (0, s))
    key_block = pl.BlockSpec((1, 8, length), lambda s, h: (s, 0, 0))
    query_block = pl.BlockSpec((1, 8, stretch), lambda s, h: (s, 0, 0))
    return head_block, log_block, kv_block, [key_block, query_block]


def attention_forward(query, blocks, ids, seqs):
    stretch, group = query.shape[1] // seqs, query.shape[0] // HEAD
    wide, length = blocks[0].shape[1] // seqs, ids[0].shape[2]
    head_block, log_block, kv_block, id_blocks = attention_specs(stretch, wide, length)
    return pl.pallas_call(
        functools.partial(forward_kernel, len(blocks)),
        grid=(seqs, group),
        in_specs=[head_block] + id_blocks + [kv_block] * len(blocks),
        out_specs=[head_block, log_block],
        out_shape=[
            jax.ShapeDtypeStruct(query.shape, bf16),
            jax.ShapeDtypeStruct((seqs, group, 1, stretch), f32),
        ],
        scratch_shapes=[
            pltpu.VMEM((length, stretch), f32),
            pltpu.VMEM((length, HEAD), bf16),
            pltpu.VMEM((2 * HEAD, length), bf16),
        ],
        compiler_params=pltpu.CompilerParams(vmem_limit_bytes=VMEM_LIMIT),
    )(query, *ids, *blocks)


def attention_backward(query, grad, attended, logsum, blocks, ids, seqs):
    stretch, group = query.shape[1] // seqs, query.shape[0] // HEAD
    wide, length = blocks[0].shape[1] // seqs, ids[0].shape[2]
    head_block, log_block, kv_block, id_blocks = attention_specs(stretch, wide, length)
    dq, *dkv = pl.pallas_call(
        functools.partial(backward_kernel, len(blocks)),
        grid=(seqs, group),
        in_specs=[head_block, head_block, head_block, log_block] + id_blocks + [kv_block] * len(blocks),
        out_specs=[head_block] + [kv_block] * len(blocks),
        out_shape=[jax.ShapeDtypeStruct(query.shape, f32)]
        + [jax.ShapeDtypeStruct(block.shape, bf16) for block in blocks],
        scratch_shapes=[
            pltpu.VMEM((length, stretch), f32),
            pltpu.VMEM((length, HEAD), bf16),
            pltpu.VMEM((length, HEAD), bf16),
            pltpu.VMEM((2 * HEAD, length), bf16),
            pltpu.VMEM((2 * HEAD, length), f32),
        ],
        compiler_params=pltpu.CompilerParams(vmem_limit_bytes=VMEM_LIMIT),
    )(query, grad, attended, logsum, *ids, *blocks)
    return dq, dkv


def turn(values, cosine, sine, sign):
    feats, tokens = values.shape
    parts = values.reshape(feats // HEAD, 2, HEAD // 2, tokens)
    a, b = parts[:, 0], parts[:, 1]
    s = sine * sign
    return jnp.stack([a * cosine - b * s, b * cosine + a * s], axis=1).reshape(feats, tokens)


def norm_grad(grad, gain, unit, inverse):
    scaled = grad * gain
    return inverse * (scaled - unit * jnp.mean(scaled * unit, axis=-1, keepdims=True))


def local(
    sizes,
    activations,
    segments,
    cotangent,
    query_weight,
    key_weight,
    value_weight,
    out_weight,
    query_bias,
    key_bias_vector,
    value_bias,
    attention_gain,
    gate_weight,
    up_weight,
    down_weight,
    mlp_gain,
):
    dp_size, ctx_size, tensor_size = sizes
    fast = dp_size == 4 and ctx_size == 4
    near_keys = ctx_size <= 4
    micros, per_micro, stretch, width = activations.shape
    seqs = micros * per_micro
    tokens = seqs * stretch
    length = ctx_size * stretch
    qw = query_weight.shape[1]
    units = gate_weight.shape[1]
    scale = HEAD ** (-0.5)
    ctx = lax.axis_index("ctx")

    plain = jnp.arange(8, dtype=jnp.int32)
    where, spots = (gathered_spots(), kept_spots()) if fast else (plain, plain)
    down_rows = down_weight.T
    ends = [0] + [units * share // (19 * 128) * 128 for share in SHARES] + [units]
    cuts = list(zip(ends[:-1], ends[1:]))
    packs = [
        jnp.concatenate([w[:, lo:hi] for w in (gate_weight, up_weight, down_rows)], axis=1) for lo, hi in cuts
    ]
    first = gather_whole(packs[0])
    if fast:
        second = gather_whole(packs[1])
    qkv_shard = jnp.concatenate([query_weight, key_weight, value_weight], axis=1)
    if fast:
        get_qkv = gather_begin(qkv_shard)
        get_out = gather_begin(out_weight.T)
        qkv_blocks = gather_end(get_qkv)
        w_qkv = place(qkv_blocks, where)
    else:
        w_out = gather_whole(out_weight.T)
        w_qkv = gather_whole(qkv_shard)

    own_ids = segments.reshape(seqs, stretch)
    steps = jnp.arange(stretch, dtype=jnp.int32)
    query_pos = ctx * stretch + steps
    if near_keys:
        key_pos = jnp.concatenate([(ctx - r) * stretch + steps for r in range(ctx_size)])
        key_ids = jnp.where(key_pos >= 0, jnp.concatenate(earlier(own_ids, ctx_size), axis=1), -1)
    else:
        key_pos = jnp.arange(length, dtype=jnp.int32)
        key_ids = lax.all_gather(own_ids, "ctx", axis=1, tiled=True)
    before = (key_ids[:, :, None] == own_ids[:, None, :]) & (
        key_pos[None, :, None] < query_pos[None, None, :]
    )
    position = jnp.sum(before.astype(f32), axis=1).reshape(1, tokens)
    freq = theta ** (-(2.0 / HEAD) * jnp.arange(HEAD // 2, dtype=f32))
    angle = freq[:, None] * position
    cosine, sine = jnp.cos(angle), jnp.sin(angle)
    ids = tuple(
        jnp.concatenate(
            [number[:, None], jnp.broadcast_to(place_of, number.shape)[:, None]] + [number[:, None]] * 6, axis=1
        ).astype(f32)
        for number, place_of in ((key_ids, key_pos), (own_ids, query_pos))
    )

    source = activations.reshape(tokens, width).astype(f32)
    inverse1 = lax.rsqrt(jnp.mean(source * source, axis=-1, keepdims=True) + eps)
    unit1 = source * inverse1
    normed1 = (unit1 * attention_gain).astype(bf16)
    bias = jnp.concatenate([query_bias, key_bias_vector, value_bias])
    qkv = contract(w_qkv, normed1, (0, 1)) + bias[:, None]
    query = (turn(qkv[:qw], cosine, sine, 1.0).astype(bf16) * scale).astype(bf16)
    key = turn(qkv[qw : qw + HEAD], cosine, sine, 1.0).astype(bf16)
    pair = jnp.concatenate([key, qkv[qw + HEAD :].astype(bf16)], axis=0)

    def group_of(value, m):
        wide = value.shape[1] // micros
        return value[:, m * wide : (m + 1) * wide]

    def ids_of(m):
        return tuple(v[m * per_micro : (m + 1) * per_micro] for v in ids)

    pairs, attended, logsums = [], [], []
    for m in range(micros):
        mine = group_of(pair, m)
        if near_keys:
            pairs.append(earlier(mine, ctx_size))
        else:
            wide = [
                lax.all_gather(mine[:, i * stretch : (i + 1) * stretch], "ctx", axis=1, tiled=True)
                for i in range(per_micro)
            ]
            pairs.append([jnp.concatenate(wide, axis=1)])
    plan = ()
    if fast:
        plan = (
            ((get_out, ("near", "far", "near1", "near2", "far1", "far2")),),
            ((get_out, ("near3", "far3")),),
        )
    for m in range(micros):
        query_now = group_of(query, m)
        if fast:
            for held, names in plan[min(m, 1)]:
                gather_next(held, *names)
                query_now = hold(query_now, held, names)
        out, logsum = attention_forward(query_now, pairs[m], ids_of(m), per_micro)
        attended.append(out)
        logsums.append(logsum)
    if fast:
        out_blocks = gather_end(get_out)
        w_out = place(out_blocks, where)
    partial = jnp.concatenate([contract(out, w_out, (0, 1)) for out in attended], axis=0)
    mixed = source + tensor_sum(partial, tensor_size)

    inverse2 = lax.rsqrt(jnp.mean(mixed * mixed, axis=-1, keepdims=True) + eps)
    unit2 = mixed * inverse2
    normed2 = (unit2 * mlp_gain).astype(bf16)
    grad_branch = cotangent.reshape(tokens, width)
    grad_result = grad_branch.astype(f32)
    normed2_t, branch_t = (v.T.reshape(8, width // 8, tokens) for v in (normed2, grad_branch))
    shape = (8, width // 8, -1)
    *sums, grads_a = some_units(
        [[first.reshape(shape)]], plain, plain, normed2, grad_branch, normed2_t, branch_t, None, 1
    )
    grads_a = scatter_whole(grads_a.reshape(width, -1))
    if not fast:
        grads_a, pack = lax.optimization_barrier((grads_a, packs[1]))
        second = gather_whole(pack)
    out, dn, *grads_b = some_units(
        [[second.reshape(shape)]], plain, spots, normed2, grad_branch, normed2_t, branch_t, sums, 4 if fast else 1
    )
    sums = [out, dn]
    if fast:
        grads_b = scatter_begin(grads_b)
    result = mixed + tensor_sum(sums[0], tensor_size)
    output = result.astype(bf16).reshape(activations.shape)
    grad_normed2 = tensor_sum(sums[1], tensor_size)
    grad_gain2 = jnp.sum(grad_normed2 * unit2, axis=0)
    grad_mixed = grad_result + norm_grad(grad_normed2, mlp_gain, unit2, inverse2)

    grad_attn = grad_mixed.astype(bf16)
    grad_attended = contract(w_out, grad_attn, (0, 1)).astype(bf16)
    grad_out_w = contract(grad_attn, jnp.concatenate(attended, axis=1), (0, 1))
    grads_c = scatter_begin(in_parts(grad_out_w)) if fast else None
    grad_queries, grad_pairs = [], []
    for m in range(micros):
        grad_now = group_of(grad_attended, m)
        if fast and m == 1:
            grad_now = hold(grad_now, grads_b, ["a1", "b1"])
            scatter_second(grads_b)
        grad_query, grad_blocks = attention_backward(
            group_of(query, m), grad_now, attended[m], logsums[m], pairs[m], ids_of(m), per_micro
        )
        if near_keys:
            own = give_back(grad_blocks, ctx_size)
        else:
            wide = [grad_blocks[0][:, i * length : (i + 1) * length] for i in range(per_micro)]
            own = [lax.psum_scatter(w, "ctx", scatter_dimension=1, tiled=True) for w in wide]
            own = jnp.concatenate(own, axis=1).astype(f32)
        if fast and m == 1:
            grad_query = hold(grad_query, grads_c, ["a1", "b1"])
            scatter_second(grads_c)
        grad_queries.append(grad_query)
        grad_pairs.append(own.reshape(2 * HEAD, per_micro * stretch))
    grad_query = jnp.concatenate(grad_queries, axis=1) * scale
    grad_pair = jnp.concatenate(grad_pairs, axis=1)
    grad_qkv = jnp.concatenate(
        [
            turn(grad_query, cosine, sine, -1.0),
            turn(grad_pair[:HEAD], cosine, sine, -1.0),
            grad_pair[HEAD:],
        ],
        axis=0,
    ).astype(bf16)
    grad_bias = jnp.sum(grad_qkv.astype(f32), axis=1)
    grad_qkv_w = contract(normed1, grad_qkv, (0, 1))
    if fast:
        parts = in_parts(grad_qkv_w)
        grad_qkv, *parts = lax.optimization_barrier((grad_qkv, *parts))
        grads_d = scatter_begin(parts)
        for held in (grads_b, grads_c):
            grad_qkv = hold(grad_qkv, held, ["a2", "b2"])
            scatter_third(held)
    grad_normed1 = tensor_sum(contract(grad_qkv, w_qkv, (0, 1)), tensor_size)
    grad_gain1 = jnp.sum(grad_normed1 * unit1, axis=0)
    grad_source = grad_mixed + norm_grad(grad_normed1, attention_gain, unit1, inverse1)

    if fast:
        for held in (grads_b, grads_c):
            grad_source = hold(grad_source, held, ["c1", "c2", "c3"])
        grad_units = [grads_a, scatter_end(grads_b)]
        grad_out_w, grad_qkv_w = scatter_end(grads_c), scatter_end(grads_d)
    else:
        grad_units = [grads_a, scatter_whole(grads_b[0].reshape(width, -1))]
        grad_out_w, grad_qkv_w = (scatter_whole(g.astype(bf16)) for g in (grad_out_w, grad_qkv_w))
    grad_gate_w, grad_up_w, grad_down = (
        jnp.concatenate(
            [g[:, m * (hi - lo) : (m + 1) * (hi - lo)] for g, (lo, hi) in zip(grad_units, cuts)], axis=1
        )
        for m in range(3)
    )

    smalls = sum_small(jnp.concatenate([grad_bias, grad_gain1, grad_gain2]), fast)
    ends = [qw, qw + HEAD, qw + 2 * HEAD, qw + 2 * HEAD + width]
    small = jnp.split(smalls, ends)
    return (
        output,
        grad_source.reshape(activations.shape),
        grad_qkv_w[:, :qw],
        grad_qkv_w[:, qw : qw + HEAD],
        grad_qkv_w[:, qw + HEAD :],
        grad_out_w.T,
        small[0],
        small[1],
        small[2],
        small[3],
        grad_gate_w,
        grad_up_w,
        grad_down.T,
        small[4],
    )


def solution(mesh):
    sizes = (mesh.shape["dp"], mesh.shape["ctx"], mesh.shape["tensor"])
    return jax.shard_map(
        functools.partial(local, sizes),
        mesh=mesh,
        in_specs=(
            P(None, "dp", "ctx", None),
            P(None, "dp", "ctx"),
            P(None, "dp", "ctx", None),
            P(("dp", "ctx"), "tensor"),
            P(("dp", "ctx"), "tensor"),
            P(("dp", "ctx"), "tensor"),
            P("tensor", ("dp", "ctx")),
            P("tensor"),
            P("tensor"),
            P("tensor"),
            P(),
            P(("dp", "ctx"), "tensor"),
            P(("dp", "ctx"), "tensor"),
            P("tensor", ("dp", "ctx")),
            P(),
        ),
        out_specs=(
            P(None, "dp", "ctx", None),
            P(None, "dp", "ctx", None),
            P(("dp", "ctx"), "tensor"),
            P(("dp", "ctx"), "tensor"),
            P(("dp", "ctx"), "tensor"),
            P("tensor", ("dp", "ctx")),
            P("tensor"),
            P("tensor"),
            P("tensor"),
            P(),
            P(("dp", "ctx"), "tensor"),
            P(("dp", "ctx"), "tensor"),
            P("tensor", ("dp", "ctx")),
            P(),
        ),
        check_vma=False,
    )
```

time: 647 us -> 502 us (0.78)
  matrix products: 110 us -> 14.2 us
  Pallas kernels: 79.2 us -> 135 us
  starting transfers between devices: 139 us -> 88.8 us
  waiting for transfers between devices: 198 us -> 148 us
  local copies, waits for them, and re-layouts: 50 us -> 37.1 us
  between operations: 3.09 us -> 15.9 us
    ppermute x78 -> x47, waiting for transfers between devices: 180 us -> 78.2 us  [swap(): return lax.ppermute(value, axis, [(i, i ^ bit) for i in range(size)])]
    dot_general x18 -> x7, matrix products: 110 us -> 14.2 us  [contract(): lax.dot_general(left, right, ((dims[:1], dims[1:]), ((), ())), preferred_...]
    pallas_call x4 -> x6, Pallas kernels: 58.3 us -> 129 us  [the longest x2 70.2 us: some_units(): pl.pallas_call(functools.partial(units_kernel, counts, parts, has_base, o...]
    all_gather x0 -> x2, waiting for transfers between devices: none -> 59.5 us  [gather_whole(): return lax.all_gather(shard, ('dp', 'ctx'), axis=0, tiled=True)]
    ppermute x9, starting transfers between devices: 48.6 us -> 17.5 us  [earlier(): lax.ppermute(value, 'ctx', [(i, i + back) for i in range(ctx_size - back)])]
    ppermute x78 -> x47, starting transfers between devices: 82.1 us -> 63.3 us  [swap(): return lax.ppermute(value, axis, [(i, i ^ bit) for i in range(size)])]
    pallas_call x5 -> x2, Pallas kernels: 20.9 us -> 6.03 us  [place(): pl.pallas_call(place_kernel, out_shape=jax.ShapeDtypeStruct((count,) + pi...]
    ppermute x6, waiting for transfers between devices: 17.9 us -> 9.24 us  [give_back(): lax.ppermute(blocks[back], 'ctx', [(i + back, i) for i in range(ctx_size...]
  transfers between devices with their start and end apart: 93 -> 65, of which waited for: 36 -> 18; matrix products, arithmetic and copies ran while one was open for 24% -> 18% of each run, Pallas kernels for 12% -> 19%
where the time goes in v2:
time: 502 us; the launch traced here: 493 us
  waiting for transfers between devices  148 us (29%)
  Pallas kernels  135 us (27%)
  starting transfers between devices  88.8 us (18%)
  other arithmetic  54.4 us (11%)
  local copies, waits for them, and re-layouts  37.1 us (7%)
  between operations  15.9 us (3%)
  matrix products  14.2 us (3%)
    ppermute x47, waiting for transfers between devices, swap(): return lax.ppermute(value, axis, [(i, i ^ bit) for i in range(size)])  78.2 us
    pallas_call x2, Pallas kernels, some_units(): pl.pallas_call(functools.partial(units_kernel, counts, parts, has_base, o...  70.2 us
    ppermute x47, starting transfers between devices, swap(): return lax.ppermute(value, axis, [(i, i ^ bit) for i in range(size)])  63.3 us
    all_gather x2, waiting for transfers between devices, gather_whole(): return lax.all_gather(shard, ('dp', 'ctx'), axis=0, tiled=True)  59.5 us
    pallas_call x2, Pallas kernels, attention_backward(): pl.pallas_call(functools.partial(backward_kernel, len(blocks)), grid=(seq...  30.9 us
    pallas_call x2, Pallas kernels, attention_forward(): pl.pallas_call(functools.partial(forward_kernel, len(blocks)), grid=(seqs...  28.3 us
    ppermute x9, starting transfers between devices, earlier(): lax.ppermute(value, 'ctx', [(i, i + back) for i in range(ctx_size - back)])  17.5 us
    dot_general x7, matrix products, contract(): lax.dot_general(left, right, ((dims[:1], dims[1:]), ((), ())), preferred_...  14.2 us
  transfers between devices with their start and end apart: 65, of which 18 were waited for; matrix products, arithmetic and copies ran while one was open for 18% of the time, Pallas kernels for 19%

profile of v2, /device:TPU:0, one launch (start us, length us, event | category | flops | bytes accessed | tf_op | source)
XLA Modules:
  0.0 493.3 jit_solution(14568490554359539702)
XLA Ops:
  13.0 4.1 collective-permute-start.4
  18.4 3.6 collective-permute-start.10
  22.0 2.1 collective-permute-start.11
  24.1 1.8 collective-permute-start.9
  27.6 1.7 fusion.12
  30.0 4.3 collective-permute-start.14
  36.7 1.6 collective-permute-start.7
  38.5 1.6 collective-permute-start.1
  40.1 1.5 collective-permute-start.17
  45.7 9.7 %collective-permute-done.6.refs_5_ = bf16[112,576]{1,0:T(8,128)(2,1)S(1)} collective-permute-done((bf16[112,576]{1,0:T(8,128)(2,1)S(1)}, bf16[112,576]{1,0:T(8,128)(2,1)S(1)}, u32[]{:S(2)}, u32[]{:S(2)}) %collective-permute-start.6) | collective-permute-done | bytes 129056 | tf_op jit(solution)/shard_map/ppermute | solution.py:25
  55.5 2.6 collective-permute-start.15
  58.0 2.0 collective-permute-done.8.refs_7_
  61.4 3.1 shard_map.254
  64.5 2.8 convolution_add_fusion
  68.3 3.5 collective-permute-start.19
  73.3 1.5 collective-permute-start.22
  74.8 2.4 collective-permute-start.23
  84.8 2.9 shard_map.256
  88.9 14.4 %shard_map.255 = (bf16[448,512]{1,0:T(8,128)(2,1)}, f32[2,7,1,256]{3,2,1,0:T(1,128)}) custom-call(bf16[448,512]{1,0:T(8,128)(2,1)} %get-tuple-element.72.q_ref, f32[2,8,1024]{2,1,0:T(8,128)} %get-tuple-element.229.keys, f32[2,8,256]{2,1,0:T(8,128)} %get-tuple-element.237.queries, bf16[128,512]{1,0:T(8,128)(2,1)} %copy-done.26, bf16[128,512]{1,0:T(8,128)(2,1)} %copy-done.33, ...), custom_call_target="tpu_custom_call" | custom-call | tf_op jit(solution)/shard_map/pallas_call | solution.py:385
  104.0 13.9 %shard_map.257 = (bf16[448,512]{1,0:T(8,128)(2,1)}, f32[2,7,1,256]{3,2,1,0:T(1,128)}) custom-call(bf16[448,512]{1,0:T(8,128)(2,1)} %get-tuple-element.82.q_ref, f32[2,8,1024]{2,1,0:T(8,128)} %get-tuple-element.230.keys, f32[2,8,256]{2,1,0:T(8,128)} %get-tuple-element.238.queries, bf16[128,512]{1,0:T(8,128)(2,1)} %copy-done.25, bf16[128,512]{1,0:T(8,128)(2,1)} %copy-done.34, ...), custom_call_target="tpu_custom_call" | custom-call | tf_op jit(solution)/shard_map/pallas_call | solution.py:385
  117.9 1.8 convolution_convert_fusion.4
  123.5 3.8 copy.117
  127.3 4.5 multiply_reduce_fusion.2
  131.8 1.8 copy-done
  133.7 1.6 fusion.80
  135.3 3.9 copy.116
  139.1 3.7 multiply_convert_fusion.x_ref
  143.3 28.7 %shard_map.258 = (f32[1024,896]{1,0:T(8,128)}, f32[1024,896]{1,0:T(8,128)}, bf16[8,112,3072]{2,1,0:T(8,128)(2,1)}) custom-call(s32[8]{0:T(128)} %iota.31.where.spots, s32[8]{0:T(128)} %iota.31.where.spots, bf16[1024,896]{1,0:T(8,128)(2,1)} %multiply_convert_fusion.x_ref, bf16[1024,896]{1,0:T(8,128)(2,1)} %bitcast.128, bf16[8,112,1024]{2,1,0:T(8,128)(2,1)} %bitcast.132, ...), custom_call_target="tpu_custom_call" | custom-call | tf_op jit(solution)/shard_map/pallas_call | solution.py:295
  172.0 59.5 %all-gather.3.cloned.1.call-done = bf16[896,4224]{1,0:T(8,128)(2,1)} async-done(((bf16[56,4224]{1,0:T(8,128)(2,1)}), bf16[896,4224]{1,0:T(8,128)(2,1)}) %all-gather.3.cloned.1.call-update) | async-done | bytes 7569424 | tf_op jit(solution)/shard_map/all_gather | solution.py:47
  232.0 41.5 %shard_map.259 = (bf16[1024,896]{1,0:T(8,128)(2,1)}, bf16[1024,896]{1,0:T(8,128)(2,1)}, bf16[2,112,4224]{2,1,0:T(8,128)(2,1)}, bf16[2,112,4224]{2,1,0:T(8,128)(2...) custom-call(s32[8]{0:T(128)} %iota.30.where, s32[8]{0:T(128)} %stack.73.spots, ...), custom_call_target="tpu_custom_call" | custom-call | tf_op jit(solution)/shard_map/pallas_call | solution.py:295
  274.1 1.5 collective-permute-start.30
  276.2 1.5 collective-permute-done.29
  277.7 5.3 %multiply_reduce_fusion = (f32[896]{0:T(1024)}, f32[1024]{0:T(1024)S(1)}) fusion(bf16[1024,896]{1,0:T(8,128)(2,1)} %collective-permute-done.29, bf16[1024,896]{1,0:T(8,128)(2,1)} %get-tuple-element.87, f32[1024,896]{1,0:T(8,128)} %copy-done, f32[1024]{0:T(1024)S(1)} %add_rsqrt_fusion, f32[896]{0:T(1024)S(1)} %copy-done.63), kind=kLoop, calls=%fused_computation.18 | loop fusion | flops 8255616 | bytes 7355392 | tf_op jit(solution)/shard_map/reduce_sum | solution.py:585
  283.1 5.2 %multiply_add_fusion = (f32[1024,896]{1,0:T(8,128)S(1)}, bf16[1024,896]{1,0:T(8,128)(2,1)}) fusion(bf16[1024,896]{1,0:T(8,128)(2,1)} %collective-permute-done.29, bf16[1024,896]{1,0:T(8,128)(2,1)S(1)} %copy-done.5, f32[1024,896]{1,0:T(8,128)S(1)} %copy-done.1, f32[1024]{0:T(1024)S(1)} %broadcast_multiply_fusion.2, f32[896]{0:T(1024)S(1)} %copy-done.63, ...), kind=kLoop, calls=%fused_computation.20 | loop fusion | flops 13762560 | bytes 18361856 | tf_op jit(solution)/shard_map/add | solution.py:586
  288.3 1.8 copy-done.2
  294.1 3.4 convolution_convert_fusion.2
  298.5 15.5 %shard_map.260 = (f32[448,512]{1,0:T(8,128)}, bf16[128,512]{1,0:T(8,128)(2,1)}, bf16[128,512]{1,0:T(8,128)(2,1)}, bf16[128,512]{1,0:T(8,128)(2,1)}, bf16[128,512]{1,0:T(8,128)(2,1)}) custom-call(bf16[448,512]{1,0:T(8,128)(2,1)} %get-tuple-element.72.q_ref, bf16[448,512]{1,0:T(8,128)(2,1)} %get-tuple-element.208.do_ref, ...), custom_call_target="tpu_custom_call" | custom-call | tf_op jit(solution)/shard_map/pallas_call | solution.py:407
  315.3 13.2 %collective-permute-done.30 = bf16[2,112,4224]{2,1,0:T(8,128)(2,1)} collective-permute-done((bf16[2,112,4224]{2,1,0:T(8,128)(2,1)}, bf16[2,112,4224]{2,1,0:T(8,128)(2,1)}, u32[]{:S(2)}, u32[]{:S(2)}) %collective-permute-start.30) | collective-permute-done | bytes 1892384 | tf_op jit(solution)/shard_map/ppermute | solution.py:25
  331.6 2.5 fusion.18
  334.1 15.4 %shard_map.261 = (f32[448,512]{1,0:T(8,128)}, bf16[128,512]{1,0:T(8,128)(2,1)}, bf16[128,512]{1,0:T(8,128)(2,1)}, bf16[128,512]{1,0:T(8,128)(2,1)}, bf16[128,512]{1,0:T(8,128)(2,1)}) custom-call(bf16[448,512]{1,0:T(8,128)(2,1)} %get-tuple-element.82.q_ref, bf16[448,512]{1,0:T(8,128)(2,1)} %get-tuple-element.92.do_ref, ...), custom_call_target="tpu_custom_call" | custom-call | tf_op jit(solution)/shard_map/pallas_call | solution.py:407
  353.7 3.7 collective-permute-done.37
  358.8 5.6 %collective-permute-done.38 = bf16[128,512]{1,0:T(8,128)(2,1)S(1)} collective-permute-done((bf16[128,512]{1,0:T(8,128)(2,1)}, bf16[128,512]{1,0:T(8,128)(2,1)S(1)}, u32[]{:S(2)}, u32[]{:S(2)}) %collective-permute-start.38) | collective-permute-done | bytes 131104 | tf_op jit(solution)/shard_map/ppermute | solution.py:195
  369.4 2.4 convolution_convert_fusion.1
  371.9 2.3 copy.135
  374.5 1.5 collective-permute-start.51
  376.6 1.5 fusion.17
  378.1 1.7 collective-permute-start.40
  379.9 17.1 %collective-permute-done.51 = bf16[2,112,576]{2,1,0:T(8,128)(2,1)S(1)} collective-permute-done((bf16[2,112,576]{2,1,0:T(8,128)(2,1)S(1)}, bf16[2,112,576]{2,1,0:T(8,128)(2,1)S(1)}, u32[]{:S(2)}, u32[]{:S(2)}) %collective-permute-start.51) | collective-permute-done | bytes 258080 | tf_op jit(solution)/shard_map/ppermute | solution.py:25
  399.1 10.0 %collective-permute-done.52 = bf16[112,576]{1,0:T(8,128)(2,1)S(1)} collective-permute-done((bf16[112,576]{1,0:T(8,128)(2,1)S(1)}, bf16[112,576]{1,0:T(8,128)(2,1)S(1)}, u32[]{:S(2)}, u32[]{:S(2)}) %collective-permute-start.52) | collective-permute-done | bytes 129056 | tf_op jit(solution)/shard_map/ppermute | solution.py:25
  410.0 3.9 collective-permute-start.57
  416.0 3.0 collective-permute-done.57
  420.4 1.9 fusion.15
  424.7 1.8 collective-permute-start.47
  426.5 1.8 convolution_convert_fusion
  428.4 2.3 fusion.16
  432.1 2.3 collective-permute-start.49
  434.5 2.0 fusion.9
  438.5 5.0 %fusion.8 = f32[1024,896]{1,0:T(8,128)} fusion(f32[1024,896]{1,0:T(8,128)} %copy-done.2, bf16[2,2,256,896]{3,2,1,0:T(8,128)(2,1)S(1)} %copy-done.3, bf16[1024,896]{1,0:T(8,128)(2,1)} %copy-done.7, bf16[1024,896]{1,0:T(8,128)(2,1)} %copy-done.6, f32[1024]{0:T(1024)S(1)} %broadcast_multiply_fusion.1, f32[896]{0:T(1024)S(1)} %copy-done.60, f32[1024]{0:T(1024)S(1)} %bitcast.162), kind=kLoop, calls=%fused_computation.13 | loop fusion | flops 9175040 | bytes 12856832 | tf_op jit(solution)/shard_map/add | solution.py:633
  443.6 13.2 %collective-permute-done.46 = bf16[56,4224]{1,0:T(8,128)(2,1)S(1)} collective-permute-done((bf16[56,4224]{1,0:T(8,128)(2,1)}, bf16[56,4224]{1,0:T(8,128)(2,1)S(1)}, u32[]{:S(2)}, u32[]{:S(2)}) %collective-permute-start.46) | collective-permute-done | bytes 473120 | tf_op jit(solution)/shard_map/ppermute | solution.py:25
  456.8 1.6 collective-permute-start.50
  458.4 10.4 %collective-permute-start.48 = (bf16[56,448]{1,0:T(8,128)(2,1)S(1)}, bf16[56,448]{1,0:T(8,128)(2,1)S(1)}, u32[]{:S(2)}, u32[]{:S(2)}) collective-permute-start(bf16[56,448]{1,0:T(8,128)(2,1)S(1)} %constant_dynamic-slice_fusion.5), channel_id=1, source_target_pairs={{0,2},{2,0},{4,6},{6,4},{1,3},{3,1},{5,7},{7,5},{8,10},{10,8},{12,... | collective-permute-start | bytes 150536 | tf_op jit(solution)/shard_map/ppermute | solution.py:25
  470.4 3.1 collective-permute-done.59
  474.3 2.8 collective-permute-done.60
  478.2 1.5 add_bitcast_fusion
  (367 shorter events, 77.6 us)
Async XLA Ops:
  7.2 135.6 %all-gather.5.cloned.1.call-start = ((), (), s32[]{:S(2)}) async-start(), calls=%async_computation.2 | async-start | bytes 5849088 | tf_op jit(solution)/shard_map/all_gather | solution.py:47
  11.0 220.5 %all-gather.3.cloned.1.call-start = ((), (), s32[]{:S(2)}) async-start(), calls=%async_computation.1 | async-start | bytes 8042496 | tf_op jit(solution)/shard_map/all_gather | solution.py:47
  12.8 469.9 %reduce-scatter.2.cloned.1.call-start = ((), (), s32[]{:S(2)}) async-start(), calls=%async_computation.3 | async-start | bytes 5849088 | tf_op jit(solution)/shard_map/reduce_scatter | solution.py:51
  13.0 23.6 %collective-permute-start.4 = (bf16[56,576]{1,0:T(8,128)(2,1)S(1)}, bf16[56,576]{1,0:T(8,128)(2,1)S(1)}, u32[]{:S(2)}, u32[]{:S(2)}) collective-permute-start(bf16[56,576]{1,0:T(8,128)(2,1)S(1)} %pad_maximum_fusion.21), channel_id=1, source_target_pairs={{0,4},{2,6},{4,0},{6,2},{1,5},{3,7},{5,1},{7,3},{8,12},{10,14},{12... | collective-permute-start | bytes 193544 | tf_op jit(solution)/shard_map/ppermute | solution.py:25
  17.1 19.6 %collective-permute-start.5 = (bf16[56,576]{1,0:T(8,128)(2,1)S(1)}, bf16[56,576]{1,0:T(8,128)(2,1)S(1)}, u32[]{:S(2)}, u32[]{:S(2)}) collective-permute-start(bf16[56,576]{1,0:T(8,128)(2,1)S(1)} %pad_maximum_fusion.21), channel_id=1, source_target_pairs={{0,6},{2,4},{4,2},{6,0},{1,7},{3,5},{5,3},{7,1},{8,14},{10,12},{12... | collective-permute-start | bytes 193544 | tf_op jit(solution)/shard_map/ppermute | solution.py:25
  18.4 11.5 %collective-permute-start.10 = (s32[4,256]{1,0:T(4,128)S(1)}, s32[4,256]{1,0:T(4,128)S(1)}, u32[]{:S(2)}, u32[]{:S(2)}) collective-permute-start(s32[4,256]{1,0:T(4,128)S(1)} %concatenate.119), channel_id=1, source_target_pairs={{0,4},{2,6},{1,5},{3,7},{8,12},{10,14},{9,13},{11,15},{16,20},{18,... | collective-permute-start | bytes 12296 | tf_op jit(solution)/shard_map/ppermute | solution.py:187
  22.0 7.9 %collective-permute-start.11 = (s32[4,256]{1,0:T(4,128)S(1)}, s32[4,256]{1,0:T(4,128)S(1)}, u32[]{:S(2)}, u32[]{:S(2)}) collective-permute-start(s32[4,256]{1,0:T(4,128)S(1)} %concatenate.119), channel_id=1, source_target_pairs={{0,6},{1,7},{8,14},{9,15},{16,22},{17,23},{24,30},{25,31}} | collective-permute-start | bytes 12296 | tf_op jit(solution)/shard_map/ppermute | solution.py:187
  24.1 5.9 %collective-permute-start.9 = (s32[4,256]{1,0:T(4,128)S(1)}, s32[4,256]{1,0:T(4,128)S(1)}, u32[]{:S(2)}, u32[]{:S(2)}) collective-permute-start(s32[4,256]{1,0:T(4,128)S(1)} %concatenate.119), channel_id=1, source_target_pairs={{0,2},{2,4},{4,6},{1,3},{3,5},{5,7},{8,10},{10,12},{12,14},{9,11},... | collective-permute-start | bytes 12296 | tf_op jit(solution)/shard_map/ppermute | solution.py:187
  29.9 8.4 %collective-permute-start = (bf16[56,576]{1,0:T(8,128)(2,1)S(1)}, bf16[56,576]{1,0:T(8,128)(2,1)S(1)}, u32[]{:S(2)}, u32[]{:S(2)}) collective-permute-start(bf16[56,576]{1,0:T(8,128)(2,1)S(1)} %pad_maximum_fusion.21), channel_id=1, source_target_pairs={{0,2},{2,0},{4,6},{6,4},{1,3},{3,1},{5,7},{7,5},{8,10},{10,8},{12,... | collective-permute-start | bytes 193544 | tf_op jit(solution)/shard_map/ppermute | solution.py:25
  30.0 10.1 %collective-permute-start.13 = (bf16[56,448]{1,0:T(8,128)(2,1)S(1)}, bf16[56,448]{1,0:T(8,128)(2,1)S(1)}, u32[]{:S(2)}, u32[]{:S(2)}) collective-permute-start(bf16[56,448]{1,0:T(8,128)(2,1)S(1)} %bitcast.166), channel_id=1, source_target_pairs={{0,4},{2,6},{4,0},{6,2},{1,5},{3,7},{5,1},{7,3},{8,12},{10,14},{12... | collective-permute-start | bytes 150536 | tf_op jit(solution)/shard_map/ppermute | solution.py:25
  30.0 10.0 %collective-permute-start.14 = (bf16[56,448]{1,0:T(8,128)(2,1)S(1)}, bf16[56,448]{1,0:T(8,128)(2,1)S(1)}, u32[]{:S(2)}, u32[]{:S(2)}) collective-permute-start(bf16[56,448]{1,0:T(8,128)(2,1)S(1)} %bitcast.167), channel_id=1, source_target_pairs={{0,6},{2,4},{4,2},{6,0},{1,7},{3,5},{5,3},{7,1},{8,14},{10,12},{12... | collective-permute-start | bytes 150536 | tf_op jit(solution)/shard_map/ppermute | solution.py:25
  36.6 5.6 %collective-permute-start.12 = (bf16[56,448]{1,0:T(8,128)(2,1)S(1)}, bf16[56,448]{1,0:T(8,128)(2,1)S(1)}, u32[]{:S(2)}, u32[]{:S(2)}) collective-permute-start(bf16[56,448]{1,0:T(8,128)(2,1)S(1)} %bitcast.168), channel_id=1, source_target_pairs={{0,2},{2,0},{4,6},{6,4},{1,3},{3,1},{5,7},{7,5},{8,10},{10,8},{12,... | collective-permute-start | bytes 150536 | tf_op jit(solution)/shard_map/ppermute | solution.py:25
  36.7 6.9 %collective-permute-start.7 = (bf16[112,576]{1,0:T(8,128)(2,1)S(1)}, bf16[112,576]{1,0:T(8,128)(2,1)S(1)}, u32[]{:S(2)}, u32[]{:S(2)}) collective-permute-start(bf16[112,576]{1,0:T(8,128)(2,1)S(1)} %pad_maximum_fusion.15.refs_4_), channel_id=1, source_target_pairs={{0,16},{8,24},{16,0},{24,8},{1,17},{9,25},{17,1},{25,9},{2,18},{10... | collective-permute-start | bytes 387080 | tf_op jit(solution)/shard_map/ppermute | solution.py:25
  38.5 6.7 %collective-permute-start.1 = (bf16[112,576]{1,0:T(8,128)(2,1)S(1)}, bf16[112,576]{1,0:T(8,128)(2,1)S(1)}, u32[]{:S(2)}, u32[]{:S(2)}) collective-permute-start(bf16[112,576]{1,0:T(8,128)(2,1)S(1)} %pad_maximum_fusion.14.refs_0_), channel_id=1, source_target_pairs={{0,8},{8,0},{16,24},{24,16},{1,9},{9,1},{17,25},{25,17},{2,10},{10... | collective-permute-start | bytes 387080 | tf_op jit(solution)/shard_map/ppermute | solution.py:25
  40.1 33.1 %collective-permute-start.17 = (bf16[112,448]{1,0:T(8,128)(2,1)S(1)}, bf16[112,448]{1,0:T(8,128)(2,1)S(1)}, u32[]{:S(2)}, u32[]{:S(2)}) collective-permute-start(bf16[112,448]{1,0:T(8,128)(2,1)S(1)} %pad_maximum_fusion.20.refs_4_), channel_id=1, source_target_pairs={{0,8},{8,0},{16,24},{24,16},{1,9},{9,1},{17,25},{25,17},{2,10},{10... | collective-permute-start | bytes 301064 | tf_op jit(solution)/shard_map/ppermute | solution.py:25
  41.6 13.9 %collective-permute-start.6 = (bf16[112,576]{1,0:T(8,128)(2,1)S(1)}, bf16[112,576]{1,0:T(8,128)(2,1)S(1)}, u32[]{:S(2)}, u32[]{:S(2)}) collective-permute-start(bf16[112,576]{1,0:T(8,128)(2,1)S(1)} %pad_maximum_fusion.15.refs_4_), channel_id=1, source_target_pairs={{0,8},{8,0},{16,24},{24,16},{1,9},{9,1},{17,25},{25,17},{2,10},{10... | collective-permute-start | bytes 387080 | tf_op jit(solution)/shard_map/ppermute | solution.py:25
  42.2 13.3 %collective-permute-start.2 = (bf16[112,576]{1,0:T(8,128)(2,1)S(1)}, bf16[112,576]{1,0:T(8,128)(2,1)S(1)}, u32[]{:S(2)}, u32[]{:S(2)}) collective-permute-start(bf16[112,576]{1,0:T(8,128)(2,1)S(1)} %pad_maximum_fusion.14.refs_0_), channel_id=1, source_target_pairs={{0,16},{8,24},{16,0},{24,8},{1,17},{9,25},{17,1},{25,9},{2,18},{10... | collective-permute-start | bytes 387080 | tf_op jit(solution)/shard_map/ppermute | solution.py:25
  43.6 16.4 %collective-permute-start.8 = (bf16[112,576]{1,0:T(8,128)(2,1)S(1)}, bf16[112,576]{1,0:T(8,128)(2,1)S(1)}, u32[]{:S(2)}, u32[]{:S(2)}) collective-permute-start(bf16[112,576]{1,0:T(8,128)(2,1)S(1)} %collective-permute-done.7.refs_6_), channel_id=1, source_target_pairs={{0,8},{8,0},{16,24},{24,16},{1,9},{9,1},{17,25},{25,17},{2,10},{10... | collective-permute-start | bytes 387080 | tf_op jit(solution)/shard_map/ppermute | solution.py:25
  45.2 15.6 %collective-permute-start.3 = (bf16[112,576]{1,0:T(8,128)(2,1)S(1)}, bf16[112,576]{1,0:T(8,128)(2,1)S(1)}, u32[]{:S(2)}, u32[]{:S(2)}) collective-permute-start(bf16[112,576]{1,0:T(8,128)(2,1)S(1)} %collective-permute-done.1.refs_1_), channel_id=1, source_target_pairs={{0,16},{8,24},{16,0},{24,8},{1,17},{9,25},{17,1},{25,9},{2,18},{10... | collective-permute-start | bytes 387080 | tf_op jit(solution)/shard_map/ppermute | solution.py:25
  55.5 17.8 %collective-permute-start.18 = (bf16[112,448]{1,0:T(8,128)(2,1)S(1)}, bf16[112,448]{1,0:T(8,128)(2,1)S(1)}, u32[]{:S(2)}, u32[]{:S(2)}) collective-permute-start(bf16[112,448]{1,0:T(8,128)(2,1)S(1)} %pad_maximum_fusion.20.refs_4_), channel_id=1, source_target_pairs={{0,16},{8,24},{16,0},{24,8},{1,17},{9,25},{17,1},{25,9},{2,18},{10... | collective-permute-start | bytes 301064 | tf_op jit(solution)/shard_map/ppermute | solution.py:25
  55.5 17.8 %collective-permute-start.15 = (bf16[112,448]{1,0:T(8,128)(2,1)S(1)}, bf16[112,448]{1,0:T(8,128)(2,1)S(1)}, u32[]{:S(2)}, u32[]{:S(2)}) collective-permute-start(bf16[112,448]{1,0:T(8,128)(2,1)S(1)} %pad_maximum_fusion.19.refs_0_), channel_id=1, source_target_pairs={{0,8},{8,0},{16,24},{24,16},{1,9},{9,1},{17,25},{25,17},{2,10},{10... | collective-permute-start | bytes 301064 | tf_op jit(solution)/shard_map/ppermute | solution.py:25
  60.1 13.2 %collective-permute-start.16 = (bf16[112,448]{1,0:T(8,128)(2,1)S(1)}, bf16[112,448]{1,0:T(8,128)(2,1)S(1)}, u32[]{:S(2)}, u32[]{:S(2)}) collective-permute-start(bf16[112,448]{1,0:T(8,128)(2,1)S(1)} %pad_maximum_fusion.19.refs_0_), channel_id=1, source_target_pairs={{0,16},{8,24},{16,0},{24,8},{1,17},{9,25},{17,1},{25,9},{2,18},{10... | collective-permute-start | bytes 301064 | tf_op jit(solution)/shard_map/ppermute | solution.py:25
  68.3 14.5 %collective-permute-start.19 = (bf16[128,512]{1,0:T(8,128)(2,1)S(1)}, bf16[128,512]{1,0:T(8,128)(2,1)S(1)}, u32[]{:S(2)}, u32[]{:S(2)}) collective-permute-start(bf16[128,512]{1,0:T(8,128)(2,1)S(1)} %get-tuple-element.219.refs_0_), channel_id=1, source_target_pairs={{0,2},{2,4},{4,6},{1,3},{3,5},{5,7},{8,10},{10,12},{12,14},{9,11},... | collective-permute-start | bytes 393224 | tf_op jit(solution)/shard_map/ppermute | solution.py:187
  73.3 6.8 %collective-permute-start.22 = (bf16[112,448]{1,0:T(8,128)(2,1)S(1)}, bf16[112,448]{1,0:T(8,128)(2,1)S(1)}, u32[]{:S(2)}, u32[]{:S(2)}) collective-permute-start(bf16[112,448]{1,0:T(8,128)(2,1)S(1)} %collective-permute-done.15.refs_1_), channel_id=1, source_target_pairs={{0,16},{8,24},{16,0},{24,8},{1,17},{9,25},{17,1},{25,9},{2,18},{10... | collective-permute-start | bytes 301064 | tf_op jit(solution)/shard_map/ppermute | solution.py:25
  74.8 6.7 %collective-permute-start.23 = (bf16[112,448]{1,0:T(8,128)(2,1)S(1)}, bf16[112,448]{1,0:T(8,128)(2,1)S(1)}, u32[]{:S(2)}, u32[]{:S(2)}) collective-permute-start(bf16[112,448]{1,0:T(8,128)(2,1)S(1)} %collective-permute-done.18.refs_6_), channel_id=1, source_target_pairs={{0,8},{8,0},{16,24},{24,16},{1,9},{9,1},{17,25},{25,17},{2,10},{10... | collective-permute-start | bytes 301064 | tf_op jit(solution)/shard_map/ppermute | solution.py:25
  77.5 10.3 %collective-permute-start.20 = (bf16[128,512]{1,0:T(8,128)(2,1)S(1)}, bf16[128,512]{1,0:T(8,128)(2,1)S(1)}, u32[]{:S(2)}, u32[]{:S(2)}) collective-permute-start(bf16[128,512]{1,0:T(8,128)(2,1)S(1)} %get-tuple-element.219.refs_0_), channel_id=1, source_target_pairs={{0,4},{2,6},{1,5},{3,7},{8,12},{10,14},{9,13},{11,15},{16,20},{18,... | collective-permute-start | bytes 393224 | tf_op jit(solution)/shard_map/ppermute | solution.py:187
  78.8 9.4 %collective-permute-start.21 = (bf16[128,512]{1,0:T(8,128)(2,1)S(1)}, bf16[128,512]{1,0:T(8,128)(2,1)S(1)}, u32[]{:S(2)}, u32[]{:S(2)}) collective-permute-start(bf16[128,512]{1,0:T(8,128)(2,1)S(1)} %get-tuple-element.219.refs_0_), channel_id=1, source_target_pairs={{0,6},{1,7},{8,14},{9,15},{16,22},{17,23},{24,30},{25,31}} | collective-permute-start | bytes 393224 | tf_op jit(solution)/shard_map/ppermute | solution.py:187
  80.1 23.1 %collective-permute-start.24 = (bf16[128,512]{1,0:T(8,128)(2,1)S(1)}, bf16[128,512]{1,0:T(8,128)(2,1)S(1)}, u32[]{:S(2)}, u32[]{:S(2)}) collective-permute-start(bf16[128,512]{1,0:T(8,128)(2,1)S(1)} %get-tuple-element.220.refs_0_), channel_id=1, source_target_pairs={{0,2},{2,4},{4,6},{1,3},{3,5},{5,7},{8,10},{10,12},{12,14},{9,11},... | collective-permute-start | bytes 393224 | tf_op jit(solution)/shard_map/ppermute | solution.py:187
  81.5 21.8 %collective-permute-start.25 = (bf16[128,512]{1,0:T(8,128)(2,1)S(1)}, bf16[128,512]{1,0:T(8,128)(2,1)S(1)}, u32[]{:S(2)}, u32[]{:S(2)}) collective-permute-start(bf16[128,512]{1,0:T(8,128)(2,1)S(1)} %get-tuple-element.220.refs_0_), channel_id=1, source_target_pairs={{0,4},{2,6},{1,5},{3,7},{8,12},{10,14},{9,13},{11,15},{16,20},{18,... | collective-permute-start | bytes 393224 | tf_op jit(solution)/shard_map/ppermute | solution.py:187
  82.8 20.5 %collective-permute-start.26 = (bf16[128,512]{1,0:T(8,128)(2,1)S(1)}, bf16[128,512]{1,0:T(8,128)(2,1)S(1)}, u32[]{:S(2)}, u32[]{:S(2)}) collective-permute-start(bf16[128,512]{1,0:T(8,128)(2,1)S(1)} %get-tuple-element.220.refs_0_), channel_id=1, source_target_pairs={{0,6},{1,7},{8,14},{9,15},{16,22},{17,23},{24,30},{25,31}} | collective-permute-start | bytes 393224 | tf_op jit(solution)/shard_map/ppermute | solution.py:187
  122.8 4.4 collective-permute-start.27
  273.5 4.2 collective-permute-start.29
  273.6 9.4 %collective-permute-start.28 = (bf16[1024,896]{1,0:T(8,128)(2,1)}, bf16[1024,896]{1,0:T(8,128)(2,1)}, u32[]{:S(2)}, u32[]{:S(2)}) collective-permute-start(bf16[1024,896]{1,0:T(8,128)(2,1)} %get-tuple-element.86), channel_id=1, source_target_pairs={{0,1},{1,0},{2,3},{3,2},{4,5},{5,4},{6,7},{7,6},{8,9},{9,8},{10,11... | collective-permute-start | bytes 5505032 | tf_op jit(solution)/shard_map/ppermute | solution.py:25
  274.1 54.3 %collective-permute-start.30 = (bf16[2,112,4224]{2,1,0:T(8,128)(2,1)}, bf16[2,112,4224]{2,1,0:T(8,128)(2,1)}, u32[]{:S(2)}, u32[]{:S(2)}) collective-permute-start(bf16[2,112,4224]{2,1,0:T(8,128)(2,1)} %get-tuple-element.90), channel_id=1, source_target_pairs={{0,16},{8,24},{16,0},{24,8},{1,17},{9,25},{17,1},{25,9},{2,18},{10... | collective-permute-start | bytes 5677064 | tf_op jit(solution)/shard_map/ppermute | solution.py:25
  275.7 54.6 %collective-permute-start.31 = (bf16[2,112,4224]{2,1,0:T(8,128)(2,1)}, bf16[2,112,4224]{2,1,0:T(8,128)(2,1)}, u32[]{:S(2)}, u32[]{:S(2)}) collective-permute-start(bf16[2,112,4224]{2,1,0:T(8,128)(2,1)} %get-tuple-element.91), channel_id=1, source_target_pairs={{0,8},{8,0},{16,24},{24,16},{1,9},{9,1},{17,25},{25,17},{2,10},{10... | collective-permute-start | bytes 5677064 | tf_op jit(solution)/shard_map/ppermute | solution.py:25
  292.1 73.9 %collective-permute-start.33 = (bf16[2,112,448]{2,1,0:T(8,128)(2,1)S(1)}, bf16[2,112,448]{2,1,0:T(8,128)(2,1)S(1)}, u32[]{:S(2)}, u32[]{:S(2)}) collective-permute-start(bf16[2,112,448]{2,1,0:T(8,128)(2,1)S(1)} %pad_maximum_fusion.13), channel_id=1, source_target_pairs={{0,8},{8,0},{16,24},{24,16},{1,9},{9,1},{17,25},{25,17},{2,10},{10... | collective-permute-start | bytes 602120 | tf_op jit(solution)/shard_map/ppermute | solution.py:25
  293.4 72.6 %collective-permute-start.32 = (bf16[2,112,448]{2,1,0:T(8,128)(2,1)S(1)}, bf16[2,112,448]{2,1,0:T(8,128)(2,1)S(1)}, u32[]{:S(2)}, u32[]{:S(2)}) collective-permute-start(bf16[2,112,448]{2,1,0:T(8,128)(2,1)S(1)} %pad_maximum_fusion.12), channel_id=1, source_target_pairs={{0,16},{8,24},{16,0},{24,8},{1,17},{9,25},{17,1},{25,9},{2,18},{10... | collective-permute-start | bytes 602120 | tf_op jit(solution)/shard_map/ppermute | solution.py:25
  314.0 35.6 %collective-permute-start.34 = (bf16[128,512]{1,0:T(8,128)(2,1)}, bf16[128,512]{1,0:T(8,128)(2,1)S(1)}, u32[]{:S(2)}, u32[]{:S(2)}) collective-permute-start(bf16[128,512]{1,0:T(8,128)(2,1)} %get-tuple-element.97), channel_id=1, source_target_pairs={{2,0},{4,2},{6,4},{3,1},{5,3},{7,5},{10,8},{12,10},{14,12},{11,9},... | collective-permute-start | bytes 393224 | tf_op jit(solution)/shard_map/ppermute | solution.py:195
  328.5 22.6 %collective-permute-start.35 = (bf16[128,512]{1,0:T(8,128)(2,1)}, bf16[128,512]{1,0:T(8,128)(2,1)S(1)}, u32[]{:S(2)}, u32[]{:S(2)}) collective-permute-start(bf16[128,512]{1,0:T(8,128)(2,1)} %get-tuple-element.98), channel_id=1, source_target_pairs={{4,0},{6,2},{5,1},{7,3},{12,8},{14,10},{13,9},{15,11},{20,16},{22,... | collective-permute-start | bytes 393224 | tf_op jit(solution)/shard_map/ppermute | solution.py:195
  330.3 22.0 %collective-permute-start.36 = (bf16[128,512]{1,0:T(8,128)(2,1)}, bf16[128,512]{1,0:T(8,128)(2,1)S(1)}, u32[]{:S(2)}, u32[]{:S(2)}) collective-permute-start(bf16[128,512]{1,0:T(8,128)(2,1)} %get-tuple-element.99), channel_id=1, source_target_pairs={{6,0},{7,1},{14,8},{15,9},{22,16},{23,17},{30,24},{31,25}} | collective-permute-start | bytes 393224 | tf_op jit(solution)/shard_map/ppermute | solution.py:195
  349.6 7.8 %collective-permute-start.37 = (bf16[128,512]{1,0:T(8,128)(2,1)}, bf16[128,512]{1,0:T(8,128)(2,1)S(1)}, u32[]{:S(2)}, u32[]{:S(2)}) collective-permute-start(bf16[128,512]{1,0:T(8,128)(2,1)} %get-tuple-element.101), channel_id=1, source_target_pairs={{2,0},{4,2},{6,4},{3,1},{5,3},{7,5},{10,8},{12,10},{14,12},{11,9},... | collective-permute-start | bytes 393224 | tf_op jit(solution)/shard_map/ppermute | solution.py:195
  351.0 13.4 %collective-permute-start.38 = (bf16[128,512]{1,0:T(8,128)(2,1)}, bf16[128,512]{1,0:T(8,128)(2,1)S(1)}, u32[]{:S(2)}, u32[]{:S(2)}) collective-permute-start(bf16[128,512]{1,0:T(8,128)(2,1)} %get-tuple-element.102), channel_id=1, source_target_pairs={{4,0},{6,2},{5,1},{7,3},{12,8},{14,10},{13,9},{15,11},{20,16},{22,... | collective-permute-start | bytes 393224 | tf_op jit(solution)/shard_map/ppermute | solution.py:195
  352.3 12.1 %collective-permute-start.39 = (bf16[128,512]{1,0:T(8,128)(2,1)}, bf16[128,512]{1,0:T(8,128)(2,1)S(1)}, u32[]{:S(2)}, u32[]{:S(2)}) collective-permute-start(bf16[128,512]{1,0:T(8,128)(2,1)} %get-tuple-element.103), channel_id=1, source_target_pairs={{6,0},{7,1},{14,8},{15,9},{22,16},{23,17},{30,24},{31,25}} | collective-permute-start | bytes 393224 | tf_op jit(solution)/shard_map/ppermute | solution.py:195
  357.4 63.0 %collective-permute-start.41 = (bf16[112,4224]{1,0:T(8,128)(2,1)}, bf16[112,4224]{1,0:T(8,128)(2,1)}, u32[]{:S(2)}, u32[]{:S(2)}) collective-permute-start(bf16[112,4224]{1,0:T(8,128)(2,1)} %fusion.18), channel_id=1, source_target_pairs={{0,16},{8,24},{16,0},{24,8},{1,17},{9,25},{17,1},{25,9},{2,18},{10... | collective-permute-start | bytes 2838536 | tf_op jit(solution)/shard_map/ppermute | solution.py:25
  374.5 22.5 %collective-permute-start.51 = (bf16[2,112,576]{2,1,0:T(8,128)(2,1)S(1)}, bf16[2,112,576]{2,1,0:T(8,128)(2,1)S(1)}, u32[]{:S(2)}, u32[]{:S(2)}) collective-permute-start(bf16[2,112,576]{2,1,0:T(8,128)(2,1)S(1)} %pad_maximum_fusion.8), channel_id=1, source_target_pairs={{0,16},{8,24},{16,0},{24,8},{1,17},{9,25},{17,1},{25,9},{2,18},{10... | collective-permute-start | bytes 774152 | tf_op jit(solution)/shard_map/ppermute | solution.py:25
  376.0 22.5 %collective-permute-start.54 = (bf16[2,112,576]{2,1,0:T(8,128)(2,1)S(1)}, bf16[2,112,576]{2,1,0:T(8,128)(2,1)S(1)}, u32[]{:S(2)}, u32[]{:S(2)}) collective-permute-start(bf16[2,112,576]{2,1,0:T(8,128)(2,1)S(1)} %pad_maximum_fusion.10), channel_id=1, source_target_pairs={{0,8},{8,0},{16,24},{24,16},{1,9},{9,1},{17,25},{25,17},{2,10},{10... | collective-permute-start | bytes 774152 | tf_op jit(solution)/shard_map/ppermute | solution.py:25
  378.1 42.2 %collective-permute-start.40 = (bf16[112,4224]{1,0:T(8,128)(2,1)S(1)}, bf16[112,4224]{1,0:T(8,128)(2,1)S(1)}, u32[]{:S(2)}, u32[]{:S(2)}) collective-permute-start(bf16[112,4224]{1,0:T(8,128)(2,1)S(1)} %fusion.17), channel_id=1, source_target_pairs={{0,8},{8,0},{16,24},{24,16},{1,9},{9,1},{17,25},{25,17},{2,10},{10... | collective-permute-start | bytes 2838536 | tf_op jit(solution)/shard_map/ppermute | solution.py:25
  397.0 12.1 %collective-permute-start.52 = (bf16[112,576]{1,0:T(8,128)(2,1)S(1)}, bf16[112,576]{1,0:T(8,128)(2,1)S(1)}, u32[]{:S(2)}, u32[]{:S(2)}) collective-permute-start(bf16[112,576]{1,0:T(8,128)(2,1)S(1)} %fusion.42), channel_id=1, source_target_pairs={{0,8},{8,0},{16,24},{24,16},{1,9},{9,1},{17,25},{25,17},{2,10},{10... | collective-permute-start | bytes 387080 | tf_op jit(solution)/shard_map/ppermute | solution.py:25
  398.5 10.8 %collective-permute-start.55 = (bf16[112,576]{1,0:T(8,128)(2,1)S(1)}, bf16[112,576]{1,0:T(8,128)(2,1)S(1)}, u32[]{:S(2)}, u32[]{:S(2)}) collective-permute-start(bf16[112,576]{1,0:T(8,128)(2,1)S(1)} %fusion.44), channel_id=1, source_target_pairs={{0,16},{8,24},{16,0},{24,8},{1,17},{9,25},{17,1},{25,9},{2,18},{10... | collective-permute-start | bytes 387080 | tf_op jit(solution)/shard_map/ppermute | solution.py:25
  409.2 4.7 collective-permute-start.53
  409.4 5.4 %collective-permute-start.56 = (bf16[56,576]{1,0:T(8,128)(2,1)S(1)}, bf16[56,576]{1,0:T(8,128)(2,1)S(1)}, u32[]{:S(2)}, u32[]{:S(2)}) collective-permute-start(bf16[56,576]{1,0:T(8,128)(2,1)S(1)} %get-tuple-element.223), channel_id=1, source_target_pairs={{0,4},{2,6},{4,0},{6,2},{1,5},{3,7},{5,1},{7,3},{8,12},{10,14},{12... | collective-permute-start | bytes 193544 | tf_op jit(solution)/shard_map/ppermute | solution.py:25
  410.0 9.0 %collective-permute-start.57 = (bf16[56,576]{1,0:T(8,128)(2,1)S(1)}, bf16[56,576]{1,0:T(8,128)(2,1)S(1)}, u32[]{:S(2)}, u32[]{:S(2)}) collective-permute-start(bf16[56,576]{1,0:T(8,128)(2,1)S(1)} %get-tuple-element.224), channel_id=1, source_target_pairs={{0,6},{2,4},{4,2},{6,0},{1,7},{3,5},{5,3},{7,1},{8,14},{10,12},{12... | collective-permute-start | bytes 193544 | tf_op jit(solution)/shard_map/ppermute | solution.py:25
  413.9 12.5 %collective-permute-start.42 = (bf16[112,448]{1,0:T(8,128)(2,1)S(1)}, bf16[112,448]{1,0:T(8,128)(2,1)S(1)}, u32[]{:S(2)}, u32[]{:S(2)}) collective-permute-start(bf16[112,448]{1,0:T(8,128)(2,1)S(1)} %get-tuple-element.203), channel_id=1, source_target_pairs={{0,8},{8,0},{16,24},{24,16},{1,9},{9,1},{17,25},{25,17},{2,10},{10... | collective-permute-start | bytes 301064 | tf_op jit(solution)/shard_map/ppermute | solution.py:25
  414.8 11.7 %collective-permute-start.43 = (bf16[112,448]{1,0:T(8,128)(2,1)S(1)}, bf16[112,448]{1,0:T(8,128)(2,1)S(1)}, u32[]{:S(2)}, u32[]{:S(2)}) collective-permute-start(bf16[112,448]{1,0:T(8,128)(2,1)S(1)} %get-tuple-element.202), channel_id=1, source_target_pairs={{0,16},{8,24},{16,0},{24,8},{1,17},{9,25},{17,1},{25,9},{2,18},{10... | collective-permute-start | bytes 301064 | tf_op jit(solution)/shard_map/ppermute | solution.py:25
  423.3 33.5 %collective-permute-start.46 = (bf16[56,4224]{1,0:T(8,128)(2,1)}, bf16[56,4224]{1,0:T(8,128)(2,1)S(1)}, u32[]{:S(2)}, u32[]{:S(2)}) collective-permute-start(bf16[56,4224]{1,0:T(8,128)(2,1)} %get-tuple-element.199), channel_id=1, source_target_pairs={{0,4},{2,6},{4,0},{6,2},{1,5},{3,7},{5,1},{7,3},{8,12},{10,14},{12... | collective-permute-start | bytes 1419272 | tf_op jit(solution)/shard_map/ppermute | solution.py:25
  424.7 33.7 %collective-permute-start.47 = (bf16[56,4224]{1,0:T(8,128)(2,1)}, bf16[56,4224]{1,0:T(8,128)(2,1)}, u32[]{:S(2)}, u32[]{:S(2)}) collective-permute-start(bf16[56,4224]{1,0:T(8,128)(2,1)} %get-tuple-element.198), channel_id=1, source_target_pairs={{0,6},{2,4},{4,2},{6,0},{1,7},{3,5},{5,3},{7,1},{8,14},{10,12},{12... | collective-permute-start | bytes 1419272 | tf_op jit(solution)/shard_map/ppermute | solution.py:25
  428.3 6.1 %collective-permute-start.44 = (bf16[1024,896]{1,0:T(8,128)(2,1)S(1)}, bf16[1024,896]{1,0:T(8,128)(2,1)S(1)}, u32[]{:S(2)}, u32[]{:S(2)}) collective-permute-start(bf16[1024,896]{1,0:T(8,128)(2,1)S(1)} %convolution_convert_fusion), channel_id=1, source_target_pairs={{0,1},{1,0},{2,3},{3,2},{4,5},{5,4},{6,7},{7,6},{8,9},{9,8},{10,11... | collective-permute-start | bytes 5505032 | tf_op jit(solution)/shard_map/ppermute | solution.py:25
  431.6 37.2 %collective-permute-start.45 = (bf16[56,4224]{1,0:T(8,128)(2,1)}, bf16[56,4224]{1,0:T(8,128)(2,1)}, u32[]{:S(2)}, u32[]{:S(2)}) collective-permute-start(bf16[56,4224]{1,0:T(8,128)(2,1)} %constant_dynamic-slice_fusion.8), channel_id=1, source_target_pairs={{0,2},{2,0},{4,6},{6,4},{1,3},{3,1},{5,7},{7,5},{8,10},{10,8},{12,... | collective-permute-start | bytes 1419272 | tf_op jit(solution)/shard_map/ppermute | solution.py:25
  432.1 42.2 %collective-permute-start.49 = (bf16[56,448]{1,0:T(8,128)(2,1)S(1)}, bf16[56,448]{1,0:T(8,128)(2,1)}, u32[]{:S(2)}, u32[]{:S(2)}) collective-permute-start(bf16[56,448]{1,0:T(8,128)(2,1)S(1)} %get-tuple-element.232), channel_id=1, source_target_pairs={{0,4},{2,6},{4,0},{6,2},{1,5},{3,7},{5,1},{7,3},{8,12},{10,14},{12... | collective-permute-start | bytes 150536 | tf_op jit(solution)/shard_map/ppermute | solution.py:25
  437.9 31.0 %collective-permute-start.58 = (f32[2368]{0:T(1024)}, f32[2368]{0:T(1024)S(1)}, u32[]{:S(2)}, u32[]{:S(2)}) collective-permute-start(f32[2368]{0:T(1024)} %concatenate.146), channel_id=1, source_target_pairs={{0,2},{2,0},{4,6},{6,4},{1,3},{3,1},{5,7},{7,5},{8,10},{10,8},{12,... | collective-permute-start | bytes 28424 | tf_op jit(solution)/shard_map/ppermute | solution.py:25
  456.8 17.6 %collective-permute-start.50 = (bf16[56,448]{1,0:T(8,128)(2,1)S(1)}, bf16[56,448]{1,0:T(8,128)(2,1)S(1)}, u32[]{:S(2)}, u32[]{:S(2)}) collective-permute-start(bf16[56,448]{1,0:T(8,128)(2,1)S(1)} %get-tuple-element.231), channel_id=1, source_target_pairs={{0,6},{2,4},{4,2},{6,0},{1,7},{3,5},{5,3},{7,1},{8,14},{10,12},{12... | collective-permute-start | bytes 150536 | tf_op jit(solution)/shard_map/ppermute | solution.py:25
  458.4 16.0 %collective-permute-start.48 = (bf16[56,448]{1,0:T(8,128)(2,1)S(1)}, bf16[56,448]{1,0:T(8,128)(2,1)S(1)}, u32[]{:S(2)}, u32[]{:S(2)}) collective-permute-start(bf16[56,448]{1,0:T(8,128)(2,1)S(1)} %constant_dynamic-slice_fusion.5), channel_id=1, source_target_pairs={{0,2},{2,0},{4,6},{6,4},{1,3},{3,1},{5,7},{7,5},{8,10},{10,8},{12,... | collective-permute-start | bytes 150536 | tf_op jit(solution)/shard_map/ppermute | solution.py:25
  468.8 4.7 collective-permute-start.59
  473.5 3.7 collective-permute-start.60
  (80 other events, 973.4 us)
Sparse Core Ops, SparseCore 0:
  11.1 105.7 all-gather.4
  120.1 111.3 all-gather.2
  274.3 170.3 reduce-scatter.1

commit v3 on v2

--- a/solution.py
+++ b/solution.py
@@ -611,6 +611,9 @@
         grad_pairs.append(own.reshape(2 * HEAD, per_micro * stretch))
     grad_query = jnp.concatenate(grad_queries, axis=1) * scale
     grad_pair = jnp.concatenate(grad_pairs, axis=1)
+    if fast:
+        grad_pair = hold(grad_pair, grads_b, ["a2", "b2"])
+        scatter_third(grads_b)
     grad_qkv = jnp.concatenate(
         [
             turn(grad_query, cosine, sine, -1.0),
@@ -625,16 +628,18 @@
         parts = in_parts(grad_qkv_w)
         grad_qkv, *parts = lax.optimization_barrier((grad_qkv, *parts))
         grads_d = scatter_begin(parts)
-        for held in (grads_b, grads_c):
-            grad_qkv = hold(grad_qkv, held, ["a2", "b2"])
-            scatter_third(held)
+        grad_qkv = hold(grad_qkv, grads_c, ["a2", "b2"])
+        scatter_third(grads_c)
     grad_normed1 = tensor_sum(contract(grad_qkv, w_qkv, (0, 1)), tensor_size)
     grad_gain1 = jnp.sum(grad_normed1 * unit1, axis=0)
     grad_source = grad_mixed + norm_grad(grad_normed1, attention_gain, unit1, inverse1)
 
+    smalls = sum_small(jnp.concatenate([grad_bias, grad_gain1, grad_gain2]), fast)
     if fast:
+        scatter_second(grads_d)
         for held in (grads_b, grads_c):
-            grad_source = hold(grad_source, held, ["c1", "c2", "c3"])
+            grads_d["a2"] = hold(grads_d["a2"], held, ["c1", "c2", "c3"])
+        grads_d["a2"], grad_source, smalls = lax.optimization_barrier((grads_d["a2"], grad_source, smalls))
         grad_units = [grads_a, scatter_end(grads_b)]
         grad_out_w, grad_qkv_w = scatter_end(grads_c), scatter_end(grads_d)
     else:
@@ -647,7 +652,6 @@
         for m in range(3)
     )
 
-    smalls = sum_small(jnp.concatenate([grad_bias, grad_gain1, grad_gain2]), fast)
     ends = [qw, qw + HEAD, qw + 2 * HEAD, qw + 2 * HEAD + width]
     small = jnp.split(smalls, ends)
     return (

time: 502 us -> 501 us (level)
  transfers between devices with their start and end apart: 65 -> 65, of which waited for: 18 -> 20; matrix products, arithmetic and copies ran while one was open for 18% -> 18% of each run, Pallas kernels for 19% -> 19%
where the time goes in v3:
time: 501 us; the launch traced here: 491 us
  waiting for transfers between devices  143 us (29%)
  Pallas kernels  135 us (27%)
  starting transfers between devices  93.1 us (19%)
  other arithmetic  55.7 us (11%)
  local copies, waits for them, and re-layouts  36.7 us (7%)
  between operations  16 us (3%)
  matrix products  11.9 us (2%)
    ppermute x47, waiting for transfers between devices, swap(): return lax.ppermute(value, axis, [(i, i ^ bit) for i in range(size)])  75.3 us
    pallas_call x2, Pallas kernels, some_units(): pl.pallas_call(functools.partial(units_kernel, counts, parts, has_base, o...  70.2 us
    ppermute x47, starting transfers between devices, swap(): return lax.ppermute(value, axis, [(i, i ^ bit) for i in range(size)])  67.1 us
    all_gather x2, waiting for transfers between devices, gather_whole(): return lax.all_gather(shard, ('dp', 'ctx'), axis=0, tiled=True)  58.6 us
    pallas_call x2, Pallas kernels, attention_backward(): pl.pallas_call(functools.partial(backward_kernel, len(blocks)), grid=(seq...  30.9 us
    pallas_call x2, Pallas kernels, attention_forward(): pl.pallas_call(functools.partial(forward_kernel, len(blocks)), grid=(seqs...  27.8 us
    ppermute x9, starting transfers between devices, earlier(): lax.ppermute(value, 'ctx', [(i, i + back) for i in range(ctx_size - back)])  18 us
    dot_general x7, matrix products, contract(): lax.dot_general(left, right, ((dims[:1], dims[1:]), ((), ())), preferred_...  11.9 us
  transfers between devices with their start and end apart: 65, of which 20 were waited for; matrix products, arithmetic and copies ran while one was open for 18% of the time, Pallas kernels for 19%

profile of v3, /device:TPU:0, one launch (start us, length us, event | category | flops | bytes accessed | tf_op | source)
XLA Modules:
  0.0 491.5 jit_solution(18089186036201621678)
XLA Ops:
  12.9 4.1 collective-permute-start.4
  18.4 3.6 collective-permute-start.10
  22.0 2.1 collective-permute-start.11
  24.1 1.8 collective-permute-start.9
  27.5 1.7 fusion.12
  30.0 4.3 collective-permute-start.14
  36.7 1.6 collective-permute-start.7
  38.5 1.6 collective-permute-start.1
  40.1 1.5 collective-permute-start.17
  42.2 1.5 collective-permute-start.2
  45.7 9.9 %collective-permute-done.6.refs_5_ = bf16[112,576]{1,0:T(8,128)(2,1)S(1)} collective-permute-done((bf16[112,576]{1,0:T(8,128)(2,1)S(1)}, bf16[112,576]{1,0:T(8,128)(2,1)S(1)}, u32[]{:S(2)}, u32[]{:S(2)}) %collective-permute-start.6) | collective-permute-done | bytes 129056 | tf_op jit(solution)/shard_map/ppermute | solution.py:25
  55.6 2.6 collective-permute-start.15
  58.2 2.0 collective-permute-done.8.refs_7_
  61.6 3.1 shard_map.254
  64.6 2.8 convolution_add_fusion
  68.4 3.6 collective-permute-start.19
  73.4 1.5 collective-permute-start.22
  74.9 2.4 collective-permute-start.23
  83.5 1.8 collective-permute-start.26
  86.0 2.9 shard_map.256
  90.2 13.9 %shard_map.255 = (bf16[448,512]{1,0:T(8,128)(2,1)}, f32[2,7,1,256]{3,2,1,0:T(1,128)}) custom-call(bf16[448,512]{1,0:T(8,128)(2,1)} %get-tuple-element.75.q_ref, f32[2,8,1024]{2,1,0:T(8,128)} %get-tuple-element.235.keys, f32[2,8,256]{2,1,0:T(8,128)} %get-tuple-element.243.queries, bf16[128,512]{1,0:T(8,128)(2,1)} %copy-done.29, bf16[128,512]{1,0:T(8,128)(2,1)} %copy-done.39, ...), custom_call_target="tpu_custom_call" | custom-call | tf_op jit(solution)/shard_map/pallas_call | solution.py:385
  104.8 13.9 %shard_map.257 = (bf16[448,512]{1,0:T(8,128)(2,1)}, f32[2,7,1,256]{3,2,1,0:T(1,128)}) custom-call(bf16[448,512]{1,0:T(8,128)(2,1)} %get-tuple-element.85.q_ref, f32[2,8,1024]{2,1,0:T(8,128)} %get-tuple-element.236.keys, f32[2,8,256]{2,1,0:T(8,128)} %get-tuple-element.244.queries, bf16[128,512]{1,0:T(8,128)(2,1)} %copy-done.28, bf16[128,512]{1,0:T(8,128)(2,1)} %copy-done.38, ...), custom_call_target="tpu_custom_call" | custom-call | tf_op jit(solution)/shard_map/pallas_call | solution.py:385
  118.8 1.8 convolution_convert_fusion.4
  124.3 3.8 copy.117
  128.1 4.5 multiply_reduce_fusion.2
  132.6 1.8 copy-done
  134.4 1.6 fusion.78
  136.0 3.8 copy.116
  139.9 3.7 multiply_convert_fusion.x_ref
  144.1 28.7 %shard_map.258 = (f32[1024,896]{1,0:T(8,128)}, f32[1024,896]{1,0:T(8,128)}, bf16[8,112,3072]{2,1,0:T(8,128)(2,1)}) custom-call(s32[8]{0:T(128)} %iota.31.where.spots, s32[8]{0:T(128)} %iota.31.where.spots, bf16[1024,896]{1,0:T(8,128)(2,1)} %multiply_convert_fusion.x_ref, bf16[1024,896]{1,0:T(8,128)(2,1)} %bitcast.128, bf16[8,112,1024]{2,1,0:T(8,128)(2,1)} %bitcast.132, ...), custom_call_target="tpu_custom_call" | custom-call | tf_op jit(solution)/shard_map/pallas_call | solution.py:295
  172.7 58.6 %all-gather.3.cloned.1.call-done = bf16[896,4224]{1,0:T(8,128)(2,1)} async-done(((bf16[56,4224]{1,0:T(8,128)(2,1)}), bf16[896,4224]{1,0:T(8,128)(2,1)}) %all-gather.3.cloned.1.call-update) | async-done | bytes 7569424 | tf_op jit(solution)/shard_map/all_gather | solution.py:47
  231.8 41.5 %shard_map.259 = (bf16[1024,896]{1,0:T(8,128)(2,1)}, bf16[1024,896]{1,0:T(8,128)(2,1)}, bf16[2,112,4224]{2,1,0:T(8,128)(2,1)}, bf16[2,112,4224]{2,1,0:T(8,128)(2...) custom-call(s32[8]{0:T(128)} %iota.30.where, s32[8]{0:T(128)} %stack.73.spots, ...), custom_call_target="tpu_custom_call" | custom-call | tf_op jit(solution)/shard_map/pallas_call | solution.py:295
  274.0 1.5 collective-permute-start.30
  276.1 1.5 collective-permute-done.29
  277.6 5.3 %multiply_reduce_fusion = (f32[896]{0:T(1024)}, f32[1024]{0:T(1024)S(1)}) fusion(bf16[1024,896]{1,0:T(8,128)(2,1)} %collective-permute-done.29, bf16[1024,896]{1,0:T(8,128)(2,1)} %get-tuple-element.90, f32[1024,896]{1,0:T(8,128)} %copy-done, f32[1024]{0:T(1024)S(1)} %add_rsqrt_fusion, f32[896]{0:T(1024)S(1)} %copy-done.73), kind=kLoop, calls=%fused_computation.18 | loop fusion | flops 8255616 | bytes 7355392 | tf_op jit(solution)/shard_map/reduce_sum | solution.py:585
  282.9 5.1 %multiply_add_fusion = (f32[1024,896]{1,0:T(8,128)S(1)}, bf16[1024,896]{1,0:T(8,128)(2,1)}) fusion(bf16[1024,896]{1,0:T(8,128)(2,1)} %collective-permute-done.29, bf16[1024,896]{1,0:T(8,128)(2,1)S(1)} %copy-done.5, f32[1024,896]{1,0:T(8,128)S(1)} %copy-done.1, f32[1024]{0:T(1024)S(1)} %broadcast_multiply_fusion.2, f32[896]{0:T(1024)S(1)} %copy-done.73, ...), kind=kLoop, calls=%fused_computation.20 | loop fusion | flops 13762560 | bytes 18361856 | tf_op jit(solution)/shard_map/add | solution.py:586
  290.3 15.5 %shard_map.260 = (f32[448,512]{1,0:T(8,128)}, bf16[128,512]{1,0:T(8,128)(2,1)}, bf16[128,512]{1,0:T(8,128)(2,1)}, bf16[128,512]{1,0:T(8,128)(2,1)}, bf16[128,512]{1,0:T(8,128)(2,1)}) custom-call(bf16[448,512]{1,0:T(8,128)(2,1)} %get-tuple-element.75.q_ref, bf16[448,512]{1,0:T(8,128)(2,1)} %get-tuple-element.214.do_ref, ...), custom_call_target="tpu_custom_call" | custom-call | tf_op jit(solution)/shard_map/pallas_call | solution.py:407
  311.7 15.1 %collective-permute-done.30 = bf16[2,112,4224]{2,1,0:T(8,128)(2,1)} collective-permute-done((bf16[2,112,4224]{2,1,0:T(8,128)(2,1)}, bf16[2,112,4224]{2,1,0:T(8,128)(2,1)}, u32[]{:S(2)}, u32[]{:S(2)}) %collective-permute-start.30) | collective-permute-done | bytes 1892384 | tf_op jit(solution)/shard_map/ppermute | solution.py:25
  328.8 2.7 fusion.18
  333.0 15.5 %shard_map.261 = (f32[448,512]{1,0:T(8,128)}, bf16[128,512]{1,0:T(8,128)(2,1)}, bf16[128,512]{1,0:T(8,128)(2,1)}, bf16[128,512]{1,0:T(8,128)(2,1)}, bf16[128,512]{1,0:T(8,128)(2,1)}) custom-call(bf16[448,512]{1,0:T(8,128)(2,1)} %get-tuple-element.85.q_ref, bf16[448,512]{1,0:T(8,128)(2,1)} %get-tuple-element.95.do_ref, ...), custom_call_target="tpu_custom_call" | custom-call | tf_op jit(solution)/shard_map/pallas_call | solution.py:407
  353.6 3.0 collective-permute-done.37
  356.6 1.4 collective-permute-start.41
  358.1 5.6 %collective-permute-done.38 = bf16[128,512]{1,0:T(8,128)(2,1)S(1)} collective-permute-done((bf16[128,512]{1,0:T(8,128)(2,1)}, bf16[128,512]{1,0:T(8,128)(2,1)S(1)}, u32[]{:S(2)}, u32[]{:S(2)}) %collective-permute-start.38) | collective-permute-done | bytes 131104 | tf_op jit(solution)/shard_map/ppermute | solution.py:195
  363.6 1.5 collective-permute-start.40
  369.8 12.4 %collective-permute-done.41 = bf16[112,4224]{1,0:T(8,128)(2,1)S(1)} collective-permute-done((bf16[112,4224]{1,0:T(8,128)(2,1)}, bf16[112,4224]{1,0:T(8,128)(2,1)S(1)}, u32[]{:S(2)}, u32[]{:S(2)}) %collective-permute-start.41) | collective-permute-done | bytes 946208 | tf_op jit(solution)/shard_map/ppermute | solution.py:25
  382.1 1.5 collective-permute-done.40
  383.7 1.8 fusion.15
  386.9 4.2 collective-permute-start.46
  391.2 1.5 fusion.16
  396.4 2.4 convolution_convert_fusion.1
  398.7 2.3 copy.135
  401.4 1.6 collective-permute-start.42
  403.5 1.8 convolution_convert_fusion
  405.4 1.8 fusion.28
  410.4 5.6 %collective-permute-done.59 = bf16[112,576]{1,0:T(8,128)(2,1)S(1)} collective-permute-done((bf16[112,576]{1,0:T(8,128)(2,1)S(1)}, bf16[112,576]{1,0:T(8,128)(2,1)S(1)}, u32[]{:S(2)}, u32[]{:S(2)}) %collective-permute-start.59) | collective-permute-done | bytes 129056 | tf_op jit(solution)/shard_map/ppermute | solution.py:25
  417.2 4.2 collective-permute-done.43
  422.1 12.6 %collective-permute-done.45 = bf16[56,4224]{1,0:T(8,128)(2,1)S(1)} collective-permute-done((bf16[56,4224]{1,0:T(8,128)(2,1)}, bf16[56,4224]{1,0:T(8,128)(2,1)S(1)}, u32[]{:S(2)}, u32[]{:S(2)}) %collective-permute-start.45) | collective-permute-done | bytes 473120 | tf_op jit(solution)/shard_map/ppermute | solution.py:25
  434.7 18.1 %collective-permute-start.49 = (bf16[56,448]{1,0:T(8,128)(2,1)}, bf16[56,448]{1,0:T(8,128)(2,1)}, u32[]{:S(2)}, u32[]{:S(2)}) collective-permute-start(bf16[56,448]{1,0:T(8,128)(2,1)} %constant_dynamic-slice_fusion.5), channel_id=1, source_target_pairs={{0,2},{2,0},{4,6},{6,4},{1,3},{3,1},{5,7},{7,5},{8,10},{10,8},{12,... | collective-permute-start | bytes 150536 | tf_op jit(solution)/shard_map/ppermute | solution.py:25
  456.9 4.2 collective-permute-start.61
  462.5 1.5 add_bitcast_fusion
  464.1 1.7 collective-permute-done.54
  465.7 3.7 collective-permute-done.55
  469.5 4.6 fusion.8
  476.2 2.5 collective-permute-done.57
  (387 shorter events, 77.9 us)
Async XLA Ops:
  7.2 136.4 %all-gather.5.cloned.1.call-start = ((), (), s32[]{:S(2)}) async-start(), calls=%async_computation.2 | async-start | bytes 5849088 | tf_op jit(solution)/shard_map/all_gather | solution.py:47
  10.9 220.4 %all-gather.3.cloned.1.call-start = ((), (), s32[]{:S(2)}) async-start(), calls=%async_computation.1 | async-start | bytes 8042496 | tf_op jit(solution)/shard_map/all_gather | solution.py:47
  12.8 468.1 %reduce-scatter.2.cloned.1.call-start = ((), (), s32[]{:S(2)}) async-start(), calls=%async_computation.3 | async-start | bytes 5849088 | tf_op jit(solution)/shard_map/reduce_scatter | solution.py:51
  12.9 23.6 %collective-permute-start.4 = (bf16[56,576]{1,0:T(8,128)(2,1)S(1)}, bf16[56,576]{1,0:T(8,128)(2,1)S(1)}, u32[]{:S(2)}, u32[]{:S(2)}) collective-permute-start(bf16[56,576]{1,0:T(8,128)(2,1)S(1)} %pad_maximum_fusion.21), channel_id=1, source_target_pairs={{0,4},{2,6},{4,0},{6,2},{1,5},{3,7},{5,1},{7,3},{8,12},{10,14},{12... | collective-permute-start | bytes 193544 | tf_op jit(solution)/shard_map/ppermute | solution.py:25
  17.0 19.6 %collective-permute-start.5 = (bf16[56,576]{1,0:T(8,128)(2,1)S(1)}, bf16[56,576]{1,0:T(8,128)(2,1)S(1)}, u32[]{:S(2)}, u32[]{:S(2)}) collective-permute-start(bf16[56,576]{1,0:T(8,128)(2,1)S(1)} %pad_maximum_fusion.21), channel_id=1, source_target_pairs={{0,6},{2,4},{4,2},{6,0},{1,7},{3,5},{5,3},{7,1},{8,14},{10,12},{12... | collective-permute-start | bytes 193544 | tf_op jit(solution)/shard_map/ppermute | solution.py:25
  18.4 11.5 %collective-permute-start.10 = (s32[4,256]{1,0:T(4,128)S(1)}, s32[4,256]{1,0:T(4,128)S(1)}, u32[]{:S(2)}, u32[]{:S(2)}) collective-permute-start(s32[4,256]{1,0:T(4,128)S(1)} %concatenate.119), channel_id=1, source_target_pairs={{0,4},{2,6},{1,5},{3,7},{8,12},{10,14},{9,13},{11,15},{16,20},{18,... | collective-permute-start | bytes 12296 | tf_op jit(solution)/shard_map/ppermute | solution.py:187
  22.0 7.9 %collective-permute-start.11 = (s32[4,256]{1,0:T(4,128)S(1)}, s32[4,256]{1,0:T(4,128)S(1)}, u32[]{:S(2)}, u32[]{:S(2)}) collective-permute-start(s32[4,256]{1,0:T(4,128)S(1)} %concatenate.119), channel_id=1, source_target_pairs={{0,6},{1,7},{8,14},{9,15},{16,22},{17,23},{24,30},{25,31}} | collective-permute-start | bytes 12296 | tf_op jit(solution)/shard_map/ppermute | solution.py:187
  24.1 5.9 %collective-permute-start.9 = (s32[4,256]{1,0:T(4,128)S(1)}, s32[4,256]{1,0:T(4,128)S(1)}, u32[]{:S(2)}, u32[]{:S(2)}) collective-permute-start(s32[4,256]{1,0:T(4,128)S(1)} %concatenate.119), channel_id=1, source_target_pairs={{0,2},{2,4},{4,6},{1,3},{3,5},{5,7},{8,10},{10,12},{12,14},{9,11},... | collective-permute-start | bytes 12296 | tf_op jit(solution)/shard_map/ppermute | solution.py:187
  29.9 8.4 %collective-permute-start = (bf16[56,576]{1,0:T(8,128)(2,1)S(1)}, bf16[56,576]{1,0:T(8,128)(2,1)S(1)}, u32[]{:S(2)}, u32[]{:S(2)}) collective-permute-start(bf16[56,576]{1,0:T(8,128)(2,1)S(1)} %pad_maximum_fusion.21), channel_id=1, source_target_pairs={{0,2},{2,0},{4,6},{6,4},{1,3},{3,1},{5,7},{7,5},{8,10},{10,8},{12,... | collective-permute-start | bytes 193544 | tf_op jit(solution)/shard_map/ppermute | solution.py:25
  29.9 10.1 %collective-permute-start.13 = (bf16[56,448]{1,0:T(8,128)(2,1)S(1)}, bf16[56,448]{1,0:T(8,128)(2,1)S(1)}, u32[]{:S(2)}, u32[]{:S(2)}) collective-permute-start(bf16[56,448]{1,0:T(8,128)(2,1)S(1)} %bitcast.166), channel_id=1, source_target_pairs={{0,4},{2,6},{4,0},{6,2},{1,5},{3,7},{5,1},{7,3},{8,12},{10,14},{12... | collective-permute-start | bytes 150536 | tf_op jit(solution)/shard_map/ppermute | solution.py:25
  30.0 10.0 %collective-permute-start.14 = (bf16[56,448]{1,0:T(8,128)(2,1)S(1)}, bf16[56,448]{1,0:T(8,128)(2,1)S(1)}, u32[]{:S(2)}, u32[]{:S(2)}) collective-permute-start(bf16[56,448]{1,0:T(8,128)(2,1)S(1)} %bitcast.167), channel_id=1, source_target_pairs={{0,6},{2,4},{4,2},{6,0},{1,7},{3,5},{5,3},{7,1},{8,14},{10,12},{12... | collective-permute-start | bytes 150536 | tf_op jit(solution)/shard_map/ppermute | solution.py:25
  36.6 5.6 %collective-permute-start.12 = (bf16[56,448]{1,0:T(8,128)(2,1)S(1)}, bf16[56,448]{1,0:T(8,128)(2,1)S(1)}, u32[]{:S(2)}, u32[]{:S(2)}) collective-permute-start(bf16[56,448]{1,0:T(8,128)(2,1)S(1)} %bitcast.168), channel_id=1, source_target_pairs={{0,2},{2,0},{4,6},{6,4},{1,3},{3,1},{5,7},{7,5},{8,10},{10,8},{12,... | collective-permute-start | bytes 150536 | tf_op jit(solution)/shard_map/ppermute | solution.py:25
  36.7 6.9 %collective-permute-start.7 = (bf16[112,576]{1,0:T(8,128)(2,1)S(1)}, bf16[112,576]{1,0:T(8,128)(2,1)S(1)}, u32[]{:S(2)}, u32[]{:S(2)}) collective-permute-start(bf16[112,576]{1,0:T(8,128)(2,1)S(1)} %pad_maximum_fusion.15.refs_4_), channel_id=1, source_target_pairs={{0,16},{8,24},{16,0},{24,8},{1,17},{9,25},{17,1},{25,9},{2,18},{10... | collective-permute-start | bytes 387080 | tf_op jit(solution)/shard_map/ppermute | solution.py:25
  38.5 6.7 %collective-permute-start.1 = (bf16[112,576]{1,0:T(8,128)(2,1)S(1)}, bf16[112,576]{1,0:T(8,128)(2,1)S(1)}, u32[]{:S(2)}, u32[]{:S(2)}) collective-permute-start(bf16[112,576]{1,0:T(8,128)(2,1)S(1)} %pad_maximum_fusion.14.refs_0_), channel_id=1, source_target_pairs={{0,8},{8,0},{16,24},{24,16},{1,9},{9,1},{17,25},{25,17},{2,10},{10... | collective-permute-start | bytes 387080 | tf_op jit(solution)/shard_map/ppermute | solution.py:25
  40.1 33.3 %collective-permute-start.17 = (bf16[112,448]{1,0:T(8,128)(2,1)S(1)}, bf16[112,448]{1,0:T(8,128)(2,1)S(1)}, u32[]{:S(2)}, u32[]{:S(2)}) collective-permute-start(bf16[112,448]{1,0:T(8,128)(2,1)S(1)} %pad_maximum_fusion.20.refs_4_), channel_id=1, source_target_pairs={{0,8},{8,0},{16,24},{24,16},{1,9},{9,1},{17,25},{25,17},{2,10},{10... | collective-permute-start | bytes 301064 | tf_op jit(solution)/shard_map/ppermute | solution.py:25
  41.6 14.0 %collective-permute-start.6 = (bf16[112,576]{1,0:T(8,128)(2,1)S(1)}, bf16[112,576]{1,0:T(8,128)(2,1)S(1)}, u32[]{:S(2)}, u32[]{:S(2)}) collective-permute-start(bf16[112,576]{1,0:T(8,128)(2,1)S(1)} %pad_maximum_fusion.15.refs_4_), channel_id=1, source_target_pairs={{0,8},{8,0},{16,24},{24,16},{1,9},{9,1},{17,25},{25,17},{2,10},{10... | collective-permute-start | bytes 387080 | tf_op jit(solution)/shard_map/ppermute | solution.py:25
  42.2 13.5 %collective-permute-start.2 = (bf16[112,576]{1,0:T(8,128)(2,1)S(1)}, bf16[112,576]{1,0:T(8,128)(2,1)S(1)}, u32[]{:S(2)}, u32[]{:S(2)}) collective-permute-start(bf16[112,576]{1,0:T(8,128)(2,1)S(1)} %pad_maximum_fusion.14.refs_0_), channel_id=1, source_target_pairs={{0,16},{8,24},{16,0},{24,8},{1,17},{9,25},{17,1},{25,9},{2,18},{10... | collective-permute-start | bytes 387080 | tf_op jit(solution)/shard_map/ppermute | solution.py:25
  43.6 16.6 %collective-permute-start.8 = (bf16[112,576]{1,0:T(8,128)(2,1)S(1)}, bf16[112,576]{1,0:T(8,128)(2,1)S(1)}, u32[]{:S(2)}, u32[]{:S(2)}) collective-permute-start(bf16[112,576]{1,0:T(8,128)(2,1)S(1)} %collective-permute-done.7.refs_6_), channel_id=1, source_target_pairs={{0,8},{8,0},{16,24},{24,16},{1,9},{9,1},{17,25},{25,17},{2,10},{10... | collective-permute-start | bytes 387080 | tf_op jit(solution)/shard_map/ppermute | solution.py:25
  45.2 15.7 %collective-permute-start.3 = (bf16[112,576]{1,0:T(8,128)(2,1)S(1)}, bf16[112,576]{1,0:T(8,128)(2,1)S(1)}, u32[]{:S(2)}, u32[]{:S(2)}) collective-permute-start(bf16[112,576]{1,0:T(8,128)(2,1)S(1)} %collective-permute-done.1.refs_1_), channel_id=1, source_target_pairs={{0,16},{8,24},{16,0},{24,8},{1,17},{9,25},{17,1},{25,9},{2,18},{10... | collective-permute-start | bytes 387080 | tf_op jit(solution)/shard_map/ppermute | solution.py:25
  55.6 17.7 %collective-permute-start.18 = (bf16[112,448]{1,0:T(8,128)(2,1)S(1)}, bf16[112,448]{1,0:T(8,128)(2,1)S(1)}, u32[]{:S(2)}, u32[]{:S(2)}) collective-permute-start(bf16[112,448]{1,0:T(8,128)(2,1)S(1)} %pad_maximum_fusion.20.refs_4_), channel_id=1, source_target_pairs={{0,16},{8,24},{16,0},{24,8},{1,17},{9,25},{17,1},{25,9},{2,18},{10... | collective-permute-start | bytes 301064 | tf_op jit(solution)/shard_map/ppermute | solution.py:25
  55.6 17.7 %collective-permute-start.15 = (bf16[112,448]{1,0:T(8,128)(2,1)S(1)}, bf16[112,448]{1,0:T(8,128)(2,1)}, u32[]{:S(2)}, u32[]{:S(2)}) collective-permute-start(bf16[112,448]{1,0:T(8,128)(2,1)S(1)} %pad_maximum_fusion.19.refs_0_), channel_id=1, source_target_pairs={{0,8},{8,0},{16,24},{24,16},{1,9},{9,1},{17,25},{25,17},{2,10},{10... | collective-permute-start | bytes 301064 | tf_op jit(solution)/shard_map/ppermute | solution.py:25
  60.2 13.2 %collective-permute-start.16 = (bf16[112,448]{1,0:T(8,128)(2,1)S(1)}, bf16[112,448]{1,0:T(8,128)(2,1)S(1)}, u32[]{:S(2)}, u32[]{:S(2)}) collective-permute-start(bf16[112,448]{1,0:T(8,128)(2,1)S(1)} %pad_maximum_fusion.19.refs_0_), channel_id=1, source_target_pairs={{0,16},{8,24},{16,0},{24,8},{1,17},{9,25},{17,1},{25,9},{2,18},{10... | collective-permute-start | bytes 301064 | tf_op jit(solution)/shard_map/ppermute | solution.py:25
  68.4 15.1 %collective-permute-start.19 = (bf16[128,512]{1,0:T(8,128)(2,1)S(1)}, bf16[128,512]{1,0:T(8,128)(2,1)S(1)}, u32[]{:S(2)}, u32[]{:S(2)}) collective-permute-start(bf16[128,512]{1,0:T(8,128)(2,1)S(1)} %get-tuple-element.225.refs_0_), channel_id=1, source_target_pairs={{0,2},{2,4},{4,6},{1,3},{3,5},{5,7},{8,10},{10,12},{12,14},{9,11},... | collective-permute-start | bytes 393224 | tf_op jit(solution)/shard_map/ppermute | solution.py:187
  73.4 6.8 %collective-permute-start.22 = (bf16[112,448]{1,0:T(8,128)(2,1)}, bf16[112,448]{1,0:T(8,128)(2,1)S(1)}, u32[]{:S(2)}, u32[]{:S(2)}) collective-permute-start(bf16[112,448]{1,0:T(8,128)(2,1)} %collective-permute-done.15.refs_1_), channel_id=1, source_target_pairs={{0,16},{8,24},{16,0},{24,8},{1,17},{9,25},{17,1},{25,9},{2,18},{10... | collective-permute-start | bytes 301064 | tf_op jit(solution)/shard_map/ppermute | solution.py:25
  74.9 7.3 %collective-permute-start.23 = (bf16[112,448]{1,0:T(8,128)(2,1)S(1)}, bf16[112,448]{1,0:T(8,128)(2,1)S(1)}, u32[]{:S(2)}, u32[]{:S(2)}) collective-permute-start(bf16[112,448]{1,0:T(8,128)(2,1)S(1)} %collective-permute-done.18.refs_6_), channel_id=1, source_target_pairs={{0,8},{8,0},{16,24},{24,16},{1,9},{9,1},{17,25},{25,17},{2,10},{10... | collective-permute-start | bytes 301064 | tf_op jit(solution)/shard_map/ppermute | solution.py:25
  77.6 11.3 %collective-permute-start.20 = (bf16[128,512]{1,0:T(8,128)(2,1)S(1)}, bf16[128,512]{1,0:T(8,128)(2,1)S(1)}, u32[]{:S(2)}, u32[]{:S(2)}) collective-permute-start(bf16[128,512]{1,0:T(8,128)(2,1)S(1)} %get-tuple-element.225.refs_0_), channel_id=1, source_target_pairs={{0,4},{2,6},{1,5},{3,7},{8,12},{10,14},{9,13},{11,15},{16,20},{18,... | collective-permute-start | bytes 393224 | tf_op jit(solution)/shard_map/ppermute | solution.py:187
  78.9 10.6 %collective-permute-start.21 = (bf16[128,512]{1,0:T(8,128)(2,1)S(1)}, bf16[128,512]{1,0:T(8,128)(2,1)S(1)}, u32[]{:S(2)}, u32[]{:S(2)}) collective-permute-start(bf16[128,512]{1,0:T(8,128)(2,1)S(1)} %get-tuple-element.225.refs_0_), channel_id=1, source_target_pairs={{0,6},{1,7},{8,14},{9,15},{16,22},{17,23},{24,30},{25,31}} | collective-permute-start | bytes 393224 | tf_op jit(solution)/shard_map/ppermute | solution.py:187
  80.3 23.8 %collective-permute-start.24 = (bf16[128,512]{1,0:T(8,128)(2,1)S(1)}, bf16[128,512]{1,0:T(8,128)(2,1)S(1)}, u32[]{:S(2)}, u32[]{:S(2)}) collective-permute-start(bf16[128,512]{1,0:T(8,128)(2,1)S(1)} %get-tuple-element.226.refs_0_), channel_id=1, source_target_pairs={{0,2},{2,4},{4,6},{1,3},{3,5},{5,7},{8,10},{10,12},{12,14},{9,11},... | collective-permute-start | bytes 393224 | tf_op jit(solution)/shard_map/ppermute | solution.py:187
  82.2 21.9 %collective-permute-start.25 = (bf16[128,512]{1,0:T(8,128)(2,1)S(1)}, bf16[128,512]{1,0:T(8,128)(2,1)S(1)}, u32[]{:S(2)}, u32[]{:S(2)}) collective-permute-start(bf16[128,512]{1,0:T(8,128)(2,1)S(1)} %get-tuple-element.226.refs_0_), channel_id=1, source_target_pairs={{0,4},{2,6},{1,5},{3,7},{8,12},{10,14},{9,13},{11,15},{16,20},{18,... | collective-permute-start | bytes 393224 | tf_op jit(solution)/shard_map/ppermute | solution.py:187
  83.5 20.6 %collective-permute-start.26 = (bf16[128,512]{1,0:T(8,128)(2,1)S(1)}, bf16[128,512]{1,0:T(8,128)(2,1)S(1)}, u32[]{:S(2)}, u32[]{:S(2)}) collective-permute-start(bf16[128,512]{1,0:T(8,128)(2,1)S(1)} %get-tuple-element.226.refs_0_), channel_id=1, source_target_pairs={{0,6},{1,7},{8,14},{9,15},{16,22},{17,23},{24,30},{25,31}} | collective-permute-start | bytes 393224 | tf_op jit(solution)/shard_map/ppermute | solution.py:187
  123.7 4.4 collective-permute-start.27
  273.4 4.2 collective-permute-start.29
  273.4 9.4 %collective-permute-start.28 = (bf16[1024,896]{1,0:T(8,128)(2,1)}, bf16[1024,896]{1,0:T(8,128)(2,1)}, u32[]{:S(2)}, u32[]{:S(2)}) collective-permute-start(bf16[1024,896]{1,0:T(8,128)(2,1)} %get-tuple-element.89), channel_id=1, source_target_pairs={{0,1},{1,0},{2,3},{3,2},{4,5},{5,4},{6,7},{7,6},{8,9},{9,8},{10,11... | collective-permute-start | bytes 5505032 | tf_op jit(solution)/shard_map/ppermute | solution.py:25
  274.0 52.8 %collective-permute-start.30 = (bf16[2,112,4224]{2,1,0:T(8,128)(2,1)}, bf16[2,112,4224]{2,1,0:T(8,128)(2,1)}, u32[]{:S(2)}, u32[]{:S(2)}) collective-permute-start(bf16[2,112,4224]{2,1,0:T(8,128)(2,1)} %get-tuple-element.93), channel_id=1, source_target_pairs={{0,16},{8,24},{16,0},{24,8},{1,17},{9,25},{17,1},{25,9},{2,18},{10... | collective-permute-start | bytes 5677064 | tf_op jit(solution)/shard_map/ppermute | solution.py:25
  275.5 52.5 %collective-permute-start.31 = (bf16[2,112,4224]{2,1,0:T(8,128)(2,1)}, bf16[2,112,4224]{2,1,0:T(8,128)(2,1)}, u32[]{:S(2)}, u32[]{:S(2)}) collective-permute-start(bf16[2,112,4224]{2,1,0:T(8,128)(2,1)} %get-tuple-element.94), channel_id=1, source_target_pairs={{0,8},{8,0},{16,24},{24,16},{1,9},{9,1},{17,25},{25,17},{2,10},{10... | collective-permute-start | bytes 5677064 | tf_op jit(solution)/shard_map/ppermute | solution.py:25
  305.8 42.7 %collective-permute-start.34 = (bf16[128,512]{1,0:T(8,128)(2,1)}, bf16[128,512]{1,0:T(8,128)(2,1)}, u32[]{:S(2)}, u32[]{:S(2)}) collective-permute-start(bf16[128,512]{1,0:T(8,128)(2,1)} %get-tuple-element.100), channel_id=1, source_target_pairs={{2,0},{4,2},{6,4},{3,1},{5,3},{7,5},{10,8},{12,10},{14,12},{11,9},... | collective-permute-start | bytes 393224 | tf_op jit(solution)/shard_map/ppermute | solution.py:195
  307.1 42.8 %collective-permute-start.35 = (bf16[128,512]{1,0:T(8,128)(2,1)}, bf16[128,512]{1,0:T(8,128)(2,1)}, u32[]{:S(2)}, u32[]{:S(2)}) collective-permute-start(bf16[128,512]{1,0:T(8,128)(2,1)} %get-tuple-element.101), channel_id=1, source_target_pairs={{4,0},{6,2},{5,1},{7,3},{12,8},{14,10},{13,9},{15,11},{20,16},{22,... | collective-permute-start | bytes 393224 | tf_op jit(solution)/shard_map/ppermute | solution.py:195
  308.4 42.8 %collective-permute-start.36 = (bf16[128,512]{1,0:T(8,128)(2,1)}, bf16[128,512]{1,0:T(8,128)(2,1)}, u32[]{:S(2)}, u32[]{:S(2)}) collective-permute-start(bf16[128,512]{1,0:T(8,128)(2,1)} %get-tuple-element.102), channel_id=1, source_target_pairs={{6,0},{7,1},{14,8},{15,9},{22,16},{23,17},{30,24},{31,25}} | collective-permute-start | bytes 393224 | tf_op jit(solution)/shard_map/ppermute | solution.py:195
  326.8 39.4 %collective-permute-start.33 = (bf16[2,112,448]{2,1,0:T(8,128)(2,1)S(1)}, bf16[2,112,448]{2,1,0:T(8,128)(2,1)S(1)}, u32[]{:S(2)}, u32[]{:S(2)}) collective-permute-start(bf16[2,112,448]{2,1,0:T(8,128)(2,1)S(1)} %pad_maximum_fusion.13), channel_id=1, source_target_pairs={{0,8},{8,0},{16,24},{24,16},{1,9},{9,1},{17,25},{25,17},{2,10},{10... | collective-permute-start | bytes 602120 | tf_op jit(solution)/shard_map/ppermute | solution.py:25
  328.0 38.2 %collective-permute-start.32 = (bf16[2,112,448]{2,1,0:T(8,128)(2,1)S(1)}, bf16[2,112,448]{2,1,0:T(8,128)(2,1)S(1)}, u32[]{:S(2)}, u32[]{:S(2)}) collective-permute-start(bf16[2,112,448]{2,1,0:T(8,128)(2,1)S(1)} %pad_maximum_fusion.12), channel_id=1, source_target_pairs={{0,16},{8,24},{16,0},{24,8},{1,17},{9,25},{17,1},{25,9},{2,18},{10... | collective-permute-start | bytes 602120 | tf_op jit(solution)/shard_map/ppermute | solution.py:25
  348.5 8.2 %collective-permute-start.37 = (bf16[128,512]{1,0:T(8,128)(2,1)}, bf16[128,512]{1,0:T(8,128)(2,1)S(1)}, u32[]{:S(2)}, u32[]{:S(2)}) collective-permute-start(bf16[128,512]{1,0:T(8,128)(2,1)} %get-tuple-element.104), channel_id=1, source_target_pairs={{2,0},{4,2},{6,4},{3,1},{5,3},{7,5},{10,8},{12,10},{14,12},{11,9},... | collective-permute-start | bytes 393224 | tf_op jit(solution)/shard_map/ppermute | solution.py:195
  349.9 13.7 %collective-permute-start.38 = (bf16[128,512]{1,0:T(8,128)(2,1)}, bf16[128,512]{1,0:T(8,128)(2,1)S(1)}, u32[]{:S(2)}, u32[]{:S(2)}) collective-permute-start(bf16[128,512]{1,0:T(8,128)(2,1)} %get-tuple-element.105), channel_id=1, source_target_pairs={{4,0},{6,2},{5,1},{7,3},{12,8},{14,10},{13,9},{15,11},{20,16},{22,... | collective-permute-start | bytes 393224 | tf_op jit(solution)/shard_map/ppermute | solution.py:195
  351.2 13.9 %collective-permute-start.39 = (bf16[128,512]{1,0:T(8,128)(2,1)}, bf16[128,512]{1,0:T(8,128)(2,1)S(1)}, u32[]{:S(2)}, u32[]{:S(2)}) collective-permute-start(bf16[128,512]{1,0:T(8,128)(2,1)} %get-tuple-element.106), channel_id=1, source_target_pairs={{6,0},{7,1},{14,8},{15,9},{22,16},{23,17},{30,24},{31,25}} | collective-permute-start | bytes 393224 | tf_op jit(solution)/shard_map/ppermute | solution.py:195
  356.6 25.5 %collective-permute-start.41 = (bf16[112,4224]{1,0:T(8,128)(2,1)}, bf16[112,4224]{1,0:T(8,128)(2,1)S(1)}, u32[]{:S(2)}, u32[]{:S(2)}) collective-permute-start(bf16[112,4224]{1,0:T(8,128)(2,1)} %fusion.18), channel_id=1, source_target_pairs={{0,16},{8,24},{16,0},{24,8},{1,17},{9,25},{17,1},{25,9},{2,18},{10... | collective-permute-start | bytes 2838536 | tf_op jit(solution)/shard_map/ppermute | solution.py:25
  363.6 20.0 %collective-permute-start.40 = (bf16[112,4224]{1,0:T(8,128)(2,1)S(1)}, bf16[112,4224]{1,0:T(8,128)(2,1)S(1)}, u32[]{:S(2)}, u32[]{:S(2)}) collective-permute-start(bf16[112,4224]{1,0:T(8,128)(2,1)S(1)} %fusion.17), channel_id=1, source_target_pairs={{0,8},{8,0},{16,24},{24,16},{1,9},{9,1},{17,25},{25,17},{2,10},{10... | collective-permute-start | bytes 2838536 | tf_op jit(solution)/shard_map/ppermute | solution.py:25
  367.1 34.3 %collective-permute-start.47 = (bf16[112,448]{1,0:T(8,128)(2,1)}, bf16[112,448]{1,0:T(8,128)(2,1)}, u32[]{:S(2)}, u32[]{:S(2)}) collective-permute-start(bf16[112,448]{1,0:T(8,128)(2,1)} %get-tuple-element.209), channel_id=1, source_target_pairs={{0,8},{8,0},{16,24},{24,16},{1,9},{9,1},{17,25},{25,17},{2,10},{10... | collective-permute-start | bytes 301064 | tf_op jit(solution)/shard_map/ppermute | solution.py:25
  367.7 35.4 %collective-permute-start.48 = (bf16[112,448]{1,0:T(8,128)(2,1)}, bf16[112,448]{1,0:T(8,128)(2,1)}, u32[]{:S(2)}, u32[]{:S(2)}) collective-permute-start(bf16[112,448]{1,0:T(8,128)(2,1)} %get-tuple-element.208), channel_id=1, source_target_pairs={{0,16},{8,24},{16,0},{24,8},{1,17},{9,25},{17,1},{25,9},{2,18},{10... | collective-permute-start | bytes 301064 | tf_op jit(solution)/shard_map/ppermute | solution.py:25
  386.6 48.2 %collective-permute-start.45 = (bf16[56,4224]{1,0:T(8,128)(2,1)}, bf16[56,4224]{1,0:T(8,128)(2,1)S(1)}, u32[]{:S(2)}, u32[]{:S(2)}) collective-permute-start(bf16[56,4224]{1,0:T(8,128)(2,1)} %get-tuple-element.205), channel_id=1, source_target_pairs={{0,4},{2,6},{4,0},{6,2},{1,5},{3,7},{5,1},{7,3},{8,12},{10,14},{12... | collective-permute-start | bytes 1419272 | tf_op jit(solution)/shard_map/ppermute | solution.py:25
  386.9 47.8 %collective-permute-start.46 = (bf16[56,4224]{1,0:T(8,128)(2,1)}, bf16[56,4224]{1,0:T(8,128)(2,1)}, u32[]{:S(2)}, u32[]{:S(2)}) collective-permute-start(bf16[56,4224]{1,0:T(8,128)(2,1)} %get-tuple-element.204), channel_id=1, source_target_pairs={{0,6},{2,4},{4,2},{6,0},{1,7},{3,5},{5,3},{7,1},{8,14},{10,12},{12... | collective-permute-start | bytes 1419272 | tf_op jit(solution)/shard_map/ppermute | solution.py:25
  394.5 58.4 %collective-permute-start.44 = (bf16[56,4224]{1,0:T(8,128)(2,1)}, bf16[56,4224]{1,0:T(8,128)(2,1)}, u32[]{:S(2)}, u32[]{:S(2)}) collective-permute-start(bf16[56,4224]{1,0:T(8,128)(2,1)} %constant_dynamic-slice_fusion.8), channel_id=1, source_target_pairs={{0,2},{2,0},{4,6},{6,4},{1,3},{3,1},{5,7},{7,5},{8,10},{10,8},{12,... | collective-permute-start | bytes 1419272 | tf_op jit(solution)/shard_map/ppermute | solution.py:25
  401.4 8.3 %collective-permute-start.42 = (bf16[2,112,576]{2,1,0:T(8,128)(2,1)S(1)}, bf16[2,112,576]{2,1,0:T(8,128)(2,1)S(1)}, u32[]{:S(2)}, u32[]{:S(2)}) collective-permute-start(bf16[2,112,576]{2,1,0:T(8,128)(2,1)S(1)} %pad_maximum_fusion.9), channel_id=1, source_target_pairs={{0,16},{8,24},{16,0},{24,8},{1,17},{9,25},{17,1},{25,9},{2,18},{10... | collective-permute-start | bytes 774152 | tf_op jit(solution)/shard_map/ppermute | solution.py:25
  403.0 6.6 %collective-permute-start.58 = (bf16[2,112,576]{2,1,0:T(8,128)(2,1)S(1)}, bf16[2,112,576]{2,1,0:T(8,128)(2,1)S(1)}, u32[]{:S(2)}, u32[]{:S(2)}) collective-permute-start(bf16[2,112,576]{2,1,0:T(8,128)(2,1)S(1)} %pad_maximum_fusion.11), channel_id=1, source_target_pairs={{0,8},{8,0},{16,24},{24,16},{1,9},{9,1},{17,25},{25,17},{2,10},{10... | collective-permute-start | bytes 774152 | tf_op jit(solution)/shard_map/ppermute | solution.py:25
  409.7 44.6 %collective-permute-start.52 = (bf16[1024,896]{1,0:T(8,128)(2,1)S(1)}, bf16[1024,896]{1,0:T(8,128)(2,1)S(1)}, u32[]{:S(2)}, u32[]{:S(2)}) collective-permute-start(bf16[1024,896]{1,0:T(8,128)(2,1)S(1)} %convolution_convert_fusion), channel_id=1, source_target_pairs={{0,1},{1,0},{2,3},{3,2},{4,5},{5,4},{6,7},{7,6},{8,9},{9,8},{10,11... | collective-permute-start | bytes 5505032 | tf_op jit(solution)/shard_map/ppermute | solution.py:25
  409.7 6.2 %collective-permute-start.59 = (bf16[112,576]{1,0:T(8,128)(2,1)S(1)}, bf16[112,576]{1,0:T(8,128)(2,1)S(1)}, u32[]{:S(2)}, u32[]{:S(2)}) collective-permute-start(bf16[112,576]{1,0:T(8,128)(2,1)S(1)} %fusion.42), channel_id=1, source_target_pairs={{0,16},{8,24},{16,0},{24,8},{1,17},{9,25},{17,1},{25,9},{2,18},{10... | collective-permute-start | bytes 387080 | tf_op jit(solution)/shard_map/ppermute | solution.py:25
  416.0 5.5 %collective-permute-start.43 = (bf16[112,576]{1,0:T(8,128)(2,1)S(1)}, bf16[112,576]{1,0:T(8,128)(2,1)S(1)}, u32[]{:S(2)}, u32[]{:S(2)}) collective-permute-start(bf16[112,576]{1,0:T(8,128)(2,1)S(1)} %fusion.39), channel_id=1, source_target_pairs={{0,8},{8,0},{16,24},{24,16},{1,9},{9,1},{17,25},{25,17},{2,10},{10... | collective-permute-start | bytes 387080 | tf_op jit(solution)/shard_map/ppermute | solution.py:25
  421.5 35.4 %collective-permute-start.50 = (bf16[56,448]{1,0:T(8,128)(2,1)}, bf16[56,448]{1,0:T(8,128)(2,1)}, u32[]{:S(2)}, u32[]{:S(2)}) collective-permute-start(bf16[56,448]{1,0:T(8,128)(2,1)} %get-tuple-element.238), channel_id=1, source_target_pairs={{0,4},{2,6},{4,0},{6,2},{1,5},{3,7},{5,1},{7,3},{8,12},{10,14},{12... | collective-permute-start | bytes 150536 | tf_op jit(solution)/shard_map/ppermute | solution.py:25
  434.7 26.3 %collective-permute-start.51 = (bf16[56,448]{1,0:T(8,128)(2,1)}, bf16[56,448]{1,0:T(8,128)(2,1)}, u32[]{:S(2)}, u32[]{:S(2)}) collective-permute-start(bf16[56,448]{1,0:T(8,128)(2,1)} %get-tuple-element.237), channel_id=1, source_target_pairs={{0,6},{2,4},{4,2},{6,0},{1,7},{3,5},{5,3},{7,1},{8,14},{10,12},{12... | collective-permute-start | bytes 150536 | tf_op jit(solution)/shard_map/ppermute | solution.py:25
  434.7 26.3 %collective-permute-start.49 = (bf16[56,448]{1,0:T(8,128)(2,1)}, bf16[56,448]{1,0:T(8,128)(2,1)}, u32[]{:S(2)}, u32[]{:S(2)}) collective-permute-start(bf16[56,448]{1,0:T(8,128)(2,1)} %constant_dynamic-slice_fusion.5), channel_id=1, source_target_pairs={{0,2},{2,0},{4,6},{6,4},{1,3},{3,1},{5,7},{7,5},{8,10},{10,8},{12,... | collective-permute-start | bytes 150536 | tf_op jit(solution)/shard_map/ppermute | solution.py:25
  452.8 23.3 %collective-permute-start.60 = (bf16[56,576]{1,0:T(8,128)(2,1)}, bf16[56,576]{1,0:T(8,128)(2,1)}, u32[]{:S(2)}, u32[]{:S(2)}) collective-permute-start(bf16[56,576]{1,0:T(8,128)(2,1)} %get-tuple-element.229), channel_id=1, source_target_pairs={{0,4},{2,6},{4,0},{6,2},{1,5},{3,7},{5,1},{7,3},{8,12},{10,14},{12... | collective-permute-start | bytes 193544 | tf_op jit(solution)/shard_map/ppermute | solution.py:25
  455.9 5.2 %collective-permute-start.53 = (f32[2368]{0:T(1024)S(1)}, f32[2368]{0:T(1024)S(1)}, u32[]{:S(2)}, u32[]{:S(2)}) collective-permute-start(f32[2368]{0:T(1024)S(1)} %concatenate.146), channel_id=1, source_target_pairs={{0,2},{2,0},{4,6},{6,4},{1,3},{3,1},{5,7},{7,5},{8,10},{10,8},{12,... | collective-permute-start | bytes 28424 | tf_op jit(solution)/shard_map/ppermute | solution.py:25
  456.9 19.3 %collective-permute-start.61 = (bf16[56,576]{1,0:T(8,128)(2,1)}, bf16[56,576]{1,0:T(8,128)(2,1)S(1)}, u32[]{:S(2)}, u32[]{:S(2)}) collective-permute-start(bf16[56,576]{1,0:T(8,128)(2,1)} %get-tuple-element.230), channel_id=1, source_target_pairs={{0,6},{2,4},{4,2},{6,0},{1,7},{3,5},{5,3},{7,1},{8,14},{10,12},{12... | collective-permute-start | bytes 193544 | tf_op jit(solution)/shard_map/ppermute | solution.py:25
  461.1 4.7 collective-permute-start.54
  469.5 4.7 collective-permute-start.56
  474.3 4.4 collective-permute-start.57
  (90 other events, 1150.0 us)
Sparse Core Ops, SparseCore 0:
  11.1 104.9 all-gather.4
  119.4 111.9 all-gather.2
  274.1 179.2 reduce-scatter.1
